TPU v7x, 32 devices: a whole 2x2x4 slice. The times are simulated.
32 devices in a mesh: seq: 8 (over z, x), wide: 4 (over y, core).
Axes of the slice: x: 2, y: 2, z: 4, core: 2. Of those that a mesh axis runs over, the one named last changes fastest.
Arguments:
- hidden_in: bfloat16 [1024, 24, 768], P('wide', 'seq'), may hold values from -9 to 9
- cotangent: bfloat16 [1024, 24, 768], P('wide', 'seq'), may hold values from -6 to 6
- seq_offsets: int32 [24, 8], P('seq'), may hold values from 0 to 896, as said below
- owner_blocks: int32 [8], replicated, may hold values from 1 to 6, 24 in all
- master: float32 [1536, 12288], P('seq', 'wide'), may hold values from -0.72168784 to 0.72168784
- first_moment: float32 [1536, 12288], P('seq', 'wide'), may hold values from -0.00048828125 to 0.00048828125
- second_moment: float32 [1536, 12288], P('seq', 'wide'), may hold values from 1.0592933e-10 to 4.237173e-10
- ln_params: float32 [4, 768], replicated, may hold values from -1 to 2.4
- ln_first: float32 [4, 768], replicated, may hold values from -0.00048828125 to 0.00048828125
- ln_second: float32 [4, 768], replicated, may hold values from 1.0592933e-10 to 4.237173e-10
Outputs:
- mixed: bfloat16 [1024, 24, 768], P('wide', 'seq')
- input_grad: float32 [1024, 24, 768], P('wide', 'seq')
- new_master: float32 [1536, 12288], P('seq', 'wide')
- new_first: float32 [1536, 12288], P('seq', 'wide')
- new_second: float32 [1536, 12288], P('seq', 'wide')
- new_norms: float32 [4, 768], replicated
- norms_first: float32 [4, 768], replicated
- norms_second: float32 [4, 768], replicated
- grad_norm: float32 [], replicated
Inputs may be any that keep to these rules, and one draw needn't show every extreme that they name: `seq_offsets`: each pack is cut into whole sequences of 1, 2 or 4 runs of 128 positions, each starting where the previous one ends; every pack holds one sequence of 4 runs; some pack's last run is a sequence of its own. `owner_blocks`: the counts sum to three times the number of indices of seq; some index owns exactly 6 blocks.
All inputs are finite; a program needn't handle non-finite values.
Results may differ from a plain program's by a relative error of at most 0.024.
Values may be sent and summed in bfloat16 or wider, within the bound.
A program may use at most 256 MiB of HBM per device.

v0:
```python
import jax
import jax.numpy as jnp
from jax import lax
from jax.sharding import PartitionSpec as P

H = 12
HD = 64
FF = 3072
UNIT = 128
CAP = 6
STEP = 10


RATE = 0.02
NORM_RATE = 0.6
BETA_ONE = 0.9
BETA_TWO = 0.999
EPSILON = 1e-08
DECAY = 0.01
NORM_EPS = 1e-05
ROOT_HALF = 0.7071067811865476
DENSITY_SCALE = 0.3989422804014327


def owner_maps(owner_blocks, rows, cap, block):
    ends = jnp.cumsum(owner_blocks)
    starts = ends - owner_blocks
    slot = jnp.arange(cap * block, dtype=jnp.int32)
    which = slot // block
    source = (starts[:, None] + which[None, :]) * block + (slot % block)[None, :]
    valid = which[None, :] < owner_blocks[:, None]
    source = jnp.where(valid, source, 0).reshape(-1)
    valid = valid.reshape(-1)
    param = jnp.arange(rows, dtype=jnp.int32)
    blocks = param // block
    owner = jnp.sum((ends[None, :] <= blocks[:, None]).astype(jnp.int32), axis=1)
    onehot = owner[:, None] == jnp.arange(owner_blocks.shape[0], dtype=jnp.int32)[None, :]
    first = jnp.sum(jnp.where(onehot, starts[None, :], 0), axis=1)
    target = owner * (cap * block) + (blocks - first) * block + param % block
    return (source, valid, target)


def norm_forward(values, gain, shift):
    center = values - jnp.mean(values, axis=-1, keepdims=True)
    variance = jnp.mean(center * center, axis=-1, keepdims=True)
    inverse = lax.rsqrt(variance + NORM_EPS)
    normal = center * inverse
    return (normal * gain + shift, normal, inverse)


def norm_backward(grad, normal, inverse, gain):
    scaled = grad * gain
    result = inverse * (
        scaled
        - jnp.mean(scaled, axis=-1, keepdims=True)
        - normal * jnp.mean(scaled * normal, axis=-1, keepdims=True)
    )
    return (result, jnp.sum(grad * normal, axis=(0, 1)), jnp.sum(grad, axis=(0, 1)))


def adamw(param, grad, first, second, decay, rate):
    first_new = BETA_ONE * first + (1.0 - BETA_ONE) * grad
    second_new = BETA_TWO * second + (1.0 - BETA_TWO) * grad * grad
    first_hat = first_new / (1.0 - BETA_ONE**STEP)
    second_hat = second_new / (1.0 - BETA_TWO**STEP)
    param_new = param - rate * (first_hat / (jnp.sqrt(second_hat) + EPSILON) + decay * param)
    return (param_new, first_new, second_new)


def scores_of(queries, keys_all, same, slope, distance, scale):
    raw = jnp.einsum("qhd,khd->hqk", queries, keys_all, preferred_element_type=jnp.float32)
    scores = raw * scale - slope[:, None, None] * distance[None]
    return jnp.where(same[None], scores, -1e30)


def per_device(
    hidden_in,
    cotangent,
    seq_offsets,
    owner_blocks,
    master,
    first_moment,
    second_moment,
    ln_params,
    ln_first,
    ln_second,
):
    wide_count = lax.axis_size("wide")
    share = hidden_in.shape[0]
    packs = hidden_in.shape[1]
    width = hidden_in.shape[2]
    pack_len = share * wide_count
    slab_rows = master.shape[0]
    block = slab_rows // CAP
    width_e = width // wide_count
    width_f = FF // wide_count
    heads_local = width_e // HD
    scale = HD ** (-0.5)
    source, valid, target = owner_maps(owner_blocks, width, CAP, block)
    gathered = lax.all_gather(master.astype(jnp.bfloat16), "seq", axis=0, tiled=True)
    weights = jnp.take(gathered, target, axis=0)
    w_qkv = weights[:, : 3 * width_e]
    w_out = weights[:, 3 * width_e : 4 * width_e]
    base = 4 * width_e
    w_gate = weights[:, base : base + width_f]
    w_up = weights[:, base + width_f : base + 2 * width_f]
    w_down = weights[:, base + 2 * width_f : base + 3 * width_f]
    head_ids = lax.axis_index("wide") * heads_local + jnp.arange(heads_local, dtype=jnp.int32)
    slope = jnp.exp2(-8.0 * (head_ids.astype(jnp.float32) + 1.0) / H)
    places = jnp.arange(pack_len, dtype=jnp.float32)
    distance = jnp.abs(places[:, None] - places[None, :])
    piece = lax.all_gather(hidden_in, "wide", axis=0, tiled=True)
    tokens_all = piece
    qkv = jnp.einsum("rpd,dc->rpc", piece, w_qkv, preferred_element_type=jnp.float32).astype(
        jnp.bfloat16
    )
    masks = []
    contexts = []
    totals = []
    for index in range(packs):
        starts = jnp.repeat(seq_offsets[index], UNIT)
        same = starts[:, None] == starts[None, :]
        masks.append(same)
        queries = qkv[:, index, :width_e].reshape(pack_len, heads_local, HD)
        keys_all = qkv[:, index, width_e : 2 * width_e].reshape(pack_len, heads_local, HD)
        values_all = qkv[:, index, 2 * width_e :].reshape(pack_len, heads_local, HD)
        scores = scores_of(queries, keys_all, same, slope, distance, scale)
        highest = jnp.max(scores, axis=-1, keepdims=True)
        total = highest + jnp.log(jnp.sum(jnp.exp(scores - highest), axis=-1, keepdims=True))
        probs = jnp.exp(scores - total)
        context = jnp.einsum(
            "hqk,khd->qhd",
            probs.astype(jnp.bfloat16),
            values_all,
            preferred_element_type=jnp.float32,
        )
        contexts.append(context.reshape(pack_len, width_e).astype(jnp.bfloat16))
        totals.append(total)
    context_all = jnp.stack(contexts, axis=1)
    piece = context_all
    attn = lax.psum_scatter(
        jnp.einsum("rpe,de->rpd", piece, w_out, preferred_element_type=jnp.float32).astype(
            jnp.bfloat16
        ),
        "wide",
        scatter_dimension=0,
        tiled=True,
    ).astype(jnp.float32)
    tokens = hidden_in.astype(jnp.float32)
    normed, normal_one, inverse_one = norm_forward(tokens + attn, ln_params[0], ln_params[1])
    normed_low = normed.astype(jnp.bfloat16)
    piece = lax.all_gather(normed_low, "wide", axis=0, tiled=True)
    gate = jnp.einsum("rpd,df->rpf", piece, w_gate, preferred_element_type=jnp.float32)
    up_vals = jnp.einsum("rpd,df->rpf", piece, w_up, preferred_element_type=jnp.float32)
    ffn_in, gate, up_vals = (piece, gate, up_vals)
    cumulative = 0.5 * (1.0 + lax.erf(gate * ROOT_HALF))
    hidden = (gate * cumulative * up_vals).astype(jnp.bfloat16)
    piece = hidden
    ffn = lax.psum_scatter(
        jnp.einsum("rpf,df->rpd", piece, w_down, preferred_element_type=jnp.float32).astype(
            jnp.bfloat16
        ),
        "wide",
        scatter_dimension=0,
        tiled=True,
    ).astype(jnp.float32)
    out, normal_two, inverse_two = norm_forward(normed + ffn, ln_params[2], ln_params[3])
    mixed = out.astype(jnp.bfloat16)
    grad_two, gain_two, shift_two = norm_backward(
        cotangent.astype(jnp.float32), normal_two, inverse_two, ln_params[2]
    )
    piece = lax.all_gather(grad_two.astype(jnp.bfloat16), "wide", axis=0, tiled=True)
    dffn_all = piece
    dhidden = jnp.einsum("rpd,df->rpf", piece, w_down, preferred_element_type=jnp.float32)
    density = jnp.exp(-0.5 * gate * gate) * DENSITY_SCALE
    d_gate = (dhidden * up_vals * (cumulative + gate * density)).astype(jnp.bfloat16)
    d_up = (dhidden * gate * cumulative).astype(jnp.bfloat16)
    grad_down = jnp.einsum("rpd,rpf->df", dffn_all, hidden, preferred_element_type=jnp.float32)
    grad_gate = jnp.einsum("rpd,rpf->df", ffn_in, d_gate, preferred_element_type=jnp.float32)
    grad_up = jnp.einsum("rpd,rpf->df", ffn_in, d_up, preferred_element_type=jnp.float32)
    grad_normed = grad_two + lax.psum_scatter(
        (
            jnp.einsum("rpf,df->rpd", d_gate, w_gate, preferred_element_type=jnp.float32)
            + jnp.einsum("rpf,df->rpd", d_up, w_up, preferred_element_type=jnp.float32)
        ).astype(jnp.bfloat16),
        "wide",
        scatter_dimension=0,
        tiled=True,
    ).astype(jnp.float32)
    ffn_grads = jnp.concatenate([grad_gate, grad_up, grad_down], axis=1)

    def to_owner(grads):
        return jnp.where(valid[:, None], jnp.take(grads, source, axis=0), 0.0)

    ffn_owned = lax.psum_scatter(to_owner(ffn_grads), "seq", scatter_dimension=0, tiled=True)
    grad_one, gain_one, shift_one = norm_backward(
        grad_normed, normal_one, inverse_one, ln_params[0]
    )
    piece = lax.all_gather(grad_one.astype(jnp.bfloat16), "wide", axis=0, tiled=True)
    dattn_all = piece
    dcontext = jnp.einsum("rpd,de->rpe", piece, w_out, preferred_element_type=jnp.float32).astype(
        jnp.bfloat16
    )
    grad_out = jnp.einsum("rpd,rpe->de", dattn_all, context_all, preferred_element_type=jnp.float32)
    pieces = []
    for index in range(packs):
        queries = qkv[:, index, :width_e].reshape(pack_len, heads_local, HD)
        keys_all = qkv[:, index, width_e : 2 * width_e].reshape(pack_len, heads_local, HD)
        values_all = qkv[:, index, 2 * width_e :].reshape(pack_len, heads_local, HD)
        scores = scores_of(queries, keys_all, masks[index], slope, distance, scale)
        probs = jnp.exp(scores - totals[index])
        dctx = dcontext[:, index, :].reshape(pack_len, heads_local, HD)
        dprobs = jnp.einsum("qhd,khd->hqk", dctx, values_all, preferred_element_type=jnp.float32)
        dscaled = (
            probs * (dprobs - jnp.sum(probs * dprobs, axis=-1, keepdims=True)) * scale
        ).astype(jnp.bfloat16)
        dqueries = jnp.einsum("hqk,khd->qhd", dscaled, keys_all, preferred_element_type=jnp.float32)
        dkeys = jnp.einsum("hqk,qhd->khd", dscaled, queries, preferred_element_type=jnp.float32)
        dvalues = jnp.einsum(
            "hqk,qhd->khd", probs.astype(jnp.bfloat16), dctx, preferred_element_type=jnp.float32
        )
        pieces.append(
            jnp.concatenate(
                [
                    dqueries.reshape(pack_len, width_e),
                    dkeys.reshape(pack_len, width_e),
                    dvalues.reshape(pack_len, width_e),
                ],
                axis=1,
            ).astype(jnp.bfloat16)
        )
    d_qkv = jnp.stack(pieces, axis=1)
    grad_qkv = jnp.einsum("rpd,rpc->dc", tokens_all, d_qkv, preferred_element_type=jnp.float32)
    piece = d_qkv
    input_grad = grad_one + lax.psum_scatter(
        jnp.einsum("rpc,dc->rpd", piece, w_qkv, preferred_element_type=jnp.float32).astype(
            jnp.bfloat16
        ),
        "wide",
        scatter_dimension=0,
        tiled=True,
    ).astype(jnp.float32)
    attn_grads = jnp.concatenate([grad_qkv, grad_out], axis=1)
    attn_owned = lax.psum_scatter(to_owner(attn_grads), "seq", scatter_dimension=0, tiled=True)
    owned = jnp.concatenate([attn_owned, ffn_owned], axis=1)
    ln_grads = jnp.stack([gain_one, shift_one, gain_two, shift_two], axis=0)
    squares, ln_total = lax.psum((jnp.sum(owned * owned), ln_grads), ("seq", "wide"))
    grad_norm = jnp.sqrt(squares + jnp.sum(ln_total * ln_total))
    clip = jnp.minimum(1.0, 1.0 / (grad_norm + 1e-06))
    seq_count = owner_blocks.shape[0]
    mine = jnp.arange(seq_count, dtype=jnp.int32) == lax.axis_index("seq")
    own_count = jnp.sum(jnp.where(mine, owner_blocks, 0))
    kept = (jnp.arange(slab_rows, dtype=jnp.int32) // block < own_count)[:, None]
    param_new, first_new, second_new = adamw(
        master, owned * clip, first_moment, second_moment, DECAY, RATE
    )
    norms_new, norms_first, norms_second = adamw(
        ln_params, ln_total * clip, ln_first, ln_second, 0.0, NORM_RATE
    )
    return (
        mixed,
        input_grad,
        jnp.where(kept, param_new, 0.0),
        jnp.where(kept, first_new, 0.0),
        jnp.where(kept, second_new, 0.0),
        norms_new,
        norms_first,
        norms_second,
        grad_norm,
    )


def solution(mesh):
    return jax.shard_map(
        per_device,
        mesh=mesh,
        in_specs=(
            P("wide", "seq", None),
            P("wide", "seq", None),
            P("seq", None),
            P(),
            P("seq", "wide"),
            P("seq", "wide"),
            P("seq", "wide"),
            P(),
            P(),
            P(),
        ),
        out_specs=(
            P("wide", "seq", None),
            P("wide", "seq", None),
            P("seq", "wide"),
            P("seq", "wide"),
            P("seq", "wide"),
            P(),
            P(),
            P(),
            P(),
        ),
        check_vma=False,
    )
```

profile of v0, /device:TPU:0, one launch (start us, length us, event | category | flops | bytes accessed | tf_op | source)
XLA Modules:
  0.0 1201.9 jit_solution(972082656674842848)
XLA Ops:
  19.3 132.3 %all-gather.6.cloned.1.call-done = bf16[1536,3072]{1,0:T(8,128)(2,1)} async-done(((bf16[192,3072]{1,0:T(8,128)(2,1)}), bf16[1536,3072]{1,0:T(8,128)(2,1)}) %all-gather.6.cloned.1.call-update) | async-done | bytes 9437200 | tf_op jit(solution)/shard_map/all_gather | solution.py:100
  151.6 15.2 %gather_fusion = bf16[768,3072]{1,0:T(8,128)(2,1)} fusion(bf16[1536,3072]{1,0:T(8,128)(2,1)} %all-gather.6.cloned.1.call-done, s32[1024]{0:T(1024)S(1)} %pad_clamp_fusion.1), kind=kCustom, calls=%fused_computation | custom fusion | bytes 9440256 | tf_op jit(solution)/shard_map/jit(_take)/gather | solution.py:101
  166.7 6.7 copy.67
  173.4 5.0 broadcast_select_fusion
  178.4 10.5 all-gather.8.cloned.1.call-done
  188.8 5.6 convert_bitcast_fusion
  207.7 5.9 fusion.148
  219.1 5.3 fusion.147
  227.1 8.3 fusion.69
  235.5 6.8 fusion.75
  251.0 46.7 %reduce-scatter.7.cloned.1.call-done = bf16[256,3,768]{2,0,1:T(8,128)(2,1)} async-done(((bf16[1024,3,768]{2,0,1:T(8,128)(2,1)}), bf16[256,3,768]{2,0,1:T(8,128)(2,1)}) %reduce-scatter.7.cloned.1.call-update) | async-done | bytes 1179664 | tf_op jit(solution)/shard_map/reduce_scatter | solution.py:141
  303.1 37.6 %all-gather.10.cloned.1.call-done = bf16[1024,3,768]{2,0,1:T(8,128)(2,1)} async-done(((bf16[256,3,768]{2,0,1:T(8,128)(2,1)}), bf16[1024,3,768]{2,0,1:T(8,128)(2,1)}) %all-gather.10.cloned.1.call-update) | async-done | bytes 4718608 | tf_op jit(solution)/shard_map/all_gather | solution.py:152
  340.6 6.5 fusion.106
  347.2 7.8 multiply_convert_fusion.4
  357.0 6.8 convolution_convert_fusion.1
  363.9 47.9 %reduce-scatter.9.cloned.1.call-done = bf16[256,3,768]{2,0,1:T(8,128)(2,1)} async-done(((bf16[1024,3,768]{2,0,1:T(8,128)(2,1)}), bf16[256,3,768]{2,0,1:T(8,128)(2,1)}) %reduce-scatter.9.cloned.1.call-update) | async-done | bytes 1179664 | tf_op jit(solution)/shard_map/reduce_scatter | solution.py:159
  421.7 37.6 %all-gather.12.cloned.1.call-done = bf16[1024,3,768]{2,0,1:T(8,128)(2,1)} async-done(((bf16[256,3,768]{2,0,1:T(8,128)(2,1)}), bf16[1024,3,768]{2,0,1:T(8,128)(2,1)}) %all-gather.12.cloned.1.call-update) | async-done | bytes 4718608 | tf_op jit(solution)/shard_map/all_gather | solution.py:172
  459.3 12.7 %multiply_convert_fusion.3 = (bf16[1024,3,768]{2,0,1:T(8,128)(2,1)S(1)}, bf16[1024,3,768]{2,0,1:T(8,128)(2,1)S(1)}) fusion(f32[1024,3,768]{2,0,1:T(8,128)} %copy-done.9, f32[1024,3,768]{2,0,1:T(8,128)} %get-tuple-element.61, bf16[1024,3,768]{2,0,1:T(8,128)(2,1)} %all-gather.12.cloned.1.call-done, bf16[768,3072]{0,1:T(8,128)(2,1)} %broadcast_select_fusion), kind=kOutput, calls=%fused_computation.36 | convolution fusion | flops 3656908800 | bytes 34209792 | tf_op jit(solution)/shard_map/rpd,df->rpf/dot_general | solution.py:174
  472.0 6.2 fusion.105
  478.2 7.0 add_convert_fusion
  485.3 48.0 %reduce-scatter.11.cloned.1.call-done = bf16[256,3,768]{2,0,1:T(8,128)(2,1)} async-done(((bf16[1024,3,768]{2,0,1:T(8,128)(2,1)}), bf16[256,3,768]{2,0,1:T(8,128)(2,1)}) %reduce-scatter.11.cloned.1.call-update) | async-done | bytes 1179664 | tf_op jit(solution)/shard_map/reduce_scatter | solution.py:181
  533.2 5.5 multiply_reduce_fusion.3
  542.4 37.1 %all-gather.14.cloned.1.call-done = bf16[1024,3,768]{2,0,1:T(8,128)(2,1)} async-done(((bf16[256,3,768]{2,0,1:T(8,128)(2,1)}), bf16[1024,3,768]{2,0,1:T(8,128)(2,1)}) %all-gather.14.cloned.1.call-update) | async-done | bytes 4718608 | tf_op jit(solution)/shard_map/all_gather | solution.py:199
  583.7 6.3 fusion.150
  590.0 19.5 %fusion.99 = bf16[3,64,1024]{2,1,0:T(8,128)(2,1)} fusion(bf16[1024,3,64]{0,2,1:T(8,128)(2,1)S(1)} %bitcast.181, f32[3,1024,1024]{1,2,0:T(8,128)} %fusion.150, f32[3,1024,1024]{1,2,0:T(8,128)} %copy-done.2, f32[3,1024]{1,0:T(4,128)S(1)} %copy-done.46), kind=kOutput, calls=%fused_computation.118 | convolution fusion | flops 424873984 | bytes 25964544 | tf_op jit(solution)/shard_map/hqk,khd->qhd/dot_general | solution.py:217
  609.5 19.6 %fusion.102 = bf16[3,64,1024]{2,1,0:T(8,128)(2,1)} fusion(bf16[1024,3,64]{0,2,1:T(8,128)(2,1)S(1)} %bitcast.179, f32[3,1024,1024]{1,2,0:T(8,128)} %fusion.150, f32[3,1024,1024]{1,2,0:T(8,128)} %copy-done.2, f32[3,1024]{1,0:T(4,128)S(1)} %copy-done.46), kind=kOutput, calls=%fused_computation.119 | convolution fusion | flops 424873984 | bytes 25964544 | tf_op jit(solution)/shard_map/hqk,qhd->khd/dot_general | solution.py:218
  629.0 6.7 fusion.72
  635.7 6.4 fusion.151
  642.2 18.9 %fusion.93 = bf16[3,64,1024]{2,1,0:T(8,128)(2,1)S(1)} fusion(bf16[1024,3,64]{0,2,1:T(8,128)(2,1)S(1)} %bitcast.177, f32[3,1024,1024]{1,2,0:T(8,128)} %fusion.151, f32[3,1024,1024]{1,2,0:T(8,128)} %copy-done.1, f32[3,1024]{1,0:T(4,128)S(1)} %copy-done.44), kind=kOutput, calls=%fused_computation.116 | convolution fusion | flops 424873984 | bytes 25964544 | tf_op jit(solution)/shard_map/hqk,khd->qhd/dot_general | solution.py:217
  661.1 19.6 %fusion.96 = bf16[3,64,1024]{2,1,0:T(8,128)(2,1)} fusion(bf16[1024,3,64]{0,2,1:T(8,128)(2,1)S(1)} %bitcast.175, f32[3,1024,1024]{1,2,0:T(8,128)} %fusion.151, f32[3,1024,1024]{1,2,0:T(8,128)} %copy-done.1, f32[3,1024]{1,0:T(4,128)S(1)} %copy-done.44), kind=kOutput, calls=%fused_computation.117 | convolution fusion | flops 424873984 | bytes 25964544 | tf_op jit(solution)/shard_map/hqk,qhd->khd/dot_general | solution.py:218
  680.7 6.7 fusion.78
  687.4 6.3 fusion.152
  693.8 18.9 %fusion.87 = bf16[3,64,1024]{2,1,0:T(8,128)(2,1)S(1)} fusion(bf16[1024,3,64]{0,2,1:T(8,128)(2,1)S(1)} %bitcast.173, f32[3,1024,1024]{1,2,0:T(8,128)} %fusion.152, f32[3,1024,1024]{1,2,0:T(8,128)} %copy-done, f32[3,1024]{1,0:T(4,128)S(1)} %copy-done.42), kind=kOutput, calls=%fused_computation.114 | convolution fusion | flops 424873984 | bytes 25964544 | tf_op jit(solution)/shard_map/hqk,khd->qhd/dot_general | solution.py:217
  712.7 18.8 %fusion.90 = bf16[3,64,1024]{2,1,0:T(8,128)(2,1)S(1)} fusion(bf16[1024,3,64]{0,2,1:T(8,128)(2,1)S(1)} %bitcast.171, f32[3,1024,1024]{1,2,0:T(8,128)} %fusion.152, f32[3,1024,1024]{1,2,0:T(8,128)} %copy-done, f32[3,1024]{1,0:T(4,128)S(1)} %copy-done.42), kind=kOutput, calls=%fused_computation.115 | convolution fusion | flops 424873984 | bytes 25964544 | tf_op jit(solution)/shard_map/hqk,qhd->khd/dot_general | solution.py:218
  731.5 6.8 fusion.84
  741.9 5.2 convolution_bitcast_fusion.3
  750.8 5.6 gather_fusion.1
  760.9 7.5 convolution_bitcast_fusion
  768.4 7.3 convolution_bitcast_fusion.1
  783.3 8.1 copy.90
  791.4 17.1 %gather_fusion.2 = f32[1536,2304]{1,0:T(8,128)} fusion(f32[768,2304]{1,0:T(8,128)} %copy.90, s32[2048]{0:T(1024)S(1)} %pad_clamp_fusion), kind=kCustom, calls=%fused_computation.2 | custom fusion | bytes 28317696 | tf_op jit(solution)/shard_map/jit(_take)/gather | solution.py:193
  808.5 10.9 select_select_fusion
  821.0 6.9 convolution_convert_fusion
  829.0 27.2 %reduce-scatter.15.cloned.1.call-done = f32[192,768]{1,0:T(8,128)} async-done(((f32[1536,768]{1,0:T(8,128)}), f32[192,768]{1,0:T(8,128)}) %reduce-scatter.15.cloned.1.call-update) | async-done | bytes 589840 | tf_op jit(solution)/shard_map/reduce_scatter | solution.py:244
  858.1 231.0 %reduce-scatter.17.cloned.1.call-done = f32[192,2304]{1,0:T(8,128)} async-done(((f32[1536,2304]{1,0:T(8,128)}), f32[192,2304]{1,0:T(8,128)}) %reduce-scatter.17.cloned.1.call-update) | async-done | bytes 1769488 | tf_op jit(solution)/shard_map/reduce_scatter | solution.py:195
  1094.8 44.0 %reduce-scatter.13.cloned.1.call-done = bf16[256,3,768]{2,0,1:T(8,128)(2,1)} async-done(((bf16[1024,3,768]{2,0,1:T(8,128)(2,1)}), bf16[256,3,768]{2,0,1:T(8,128)(2,1)}) %reduce-scatter.13.cloned.1.call-update) | async-done | bytes 1179664 | tf_op jit(solution)/shard_map/reduce_scatter | solution.py:235
  1142.5 39.5 %all-reduce = (f32[]{:T(128)}, f32[4,768]{1,0:T(4,128)S(1)}) all-reduce(f32[]{:T(128)} %multiply_reduce_fusion.4, f32[4,768]{1,0:T(4,128)S(1)} %pad_maximum_fusion.5), channel_id=1, replica_groups=mesh['seq'=8,'wide'=4] {'seq','wide'}, use_global_device_ids=true, to_apply=%region_28.29 | all-reduce | flops 3073 | bytes 24584 | tf_op jit(solution)/shard_map/psum | solution.py:247
  1184.6 9.4 broadcast_select_fusion.1
  (272 shorter events, 101.4 us)
Async XLA Ops:
  7.2 8.1 copy-start.68
  7.2 144.4 %all-gather.6.cloned.1.call-start = ((), (), s32[]{:S(2)}) async-start(), calls=%async_computation.6 | async-start | bytes 10616832 | tf_op jit(solution)/shard_map/all_gather | solution.py:100
  10.1 178.7 %all-gather.8.cloned.1.call-start = ((), (), s32[]{:S(2)}) async-start(), calls=%async_computation.7 | async-start | bytes 5898240 | tf_op jit(solution)/shard_map/all_gather | solution.py:112
  10.9 286.8 %reduce-scatter.7.cloned.1.call-start = ((), (), s32[]{:S(2)}) async-start(), calls=%async_computation.8 | async-start | bytes 5898240 | tf_op jit(solution)/shard_map/reduce_scatter | solution.py:141
  195.6 23.5 %copy-start.26 = (bf16[1024,1,192]{0,2,1:T(8,128)(2,1)}, bf16[1024,1,192]{0,2,1:T(8,128)(2,1)S(1)}, u32[]{:S(2)}) copy-start(bf16[1024,1,192]{0,2,1:T(8,128)(2,1)S(1)} %get-tuple-element.36) | copy-start | bytes 1179652
  195.6 31.5 %copy-start.16 = (bf16[1024,1,192]{0,2,1:T(8,128)(2,1)}, bf16[1024,1,192]{0,2,1:T(8,128)(2,1)S(1)}, u32[]{:S(2)}) copy-start(bf16[1024,1,192]{0,2,1:T(8,128)(2,1)S(1)} %get-tuple-element.42) | copy-start | bytes 1179652
  195.6 39.9 %copy-start.14 = (bf16[1024,1,192]{0,2,1:T(8,128)(2,1)}, bf16[1024,1,192]{0,2,1:T(8,128)(2,1)S(1)}, u32[]{:S(2)}) copy-start(bf16[1024,1,192]{0,2,1:T(8,128)(2,1)S(1)} %get-tuple-element.40) | copy-start | bytes 1179652
  195.6 46.6 %copy-start.12 = (bf16[1024,1,192]{0,2,1:T(8,128)(2,1)}, bf16[1024,1,192]{0,2,1:T(8,128)(2,1)S(1)}, u32[]{:S(2)}) copy-start(bf16[1024,1,192]{0,2,1:T(8,128)(2,1)S(1)} %get-tuple-element.37) | copy-start | bytes 1179652
  219.1 16.4 %copy-start.43 = (f32[3,1024]{1,0:T(4,128)}, f32[3,1024]{1,0:T(4,128)S(1)}, u32[]{:S(2)}) copy-start(f32[3,1024]{1,0:T(4,128)S(1)} %log_add_fusion.1) | copy-start | bytes 36868
  224.5 17.8 %copy-start = (f32[3,1024,1024]{1,2,0:T(8,128)}, f32[3,1024,1024]{1,2,0:T(8,128)S(1)}, u32[]{:S(2)}) copy-start(f32[3,1024,1024]{1,2,0:T(8,128)S(1)} %get-tuple-element.55) | copy-start | bytes 37748740
  227.1 15.2 %copy-start.41 = (f32[3,1024]{1,0:T(4,128)}, f32[3,1024]{1,0:T(4,128)S(1)}, u32[]{:S(2)}) copy-start(f32[3,1024]{1,0:T(4,128)S(1)} %log_add_fusion) | copy-start | bytes 36868
  235.5 8.9 copy-start.20
  249.7 48.0 %copy-start.3 = (bf16[256,3,768]{2,0,1:T(8,128)(2,1)S(1)}, bf16[256,3,768]{2,0,1:T(8,128)(2,1)}, u32[]{:S(2)}) copy-start(bf16[256,3,768]{2,0,1:T(8,128)(2,1)} %param.10) | copy-start | bytes 3538948
  249.7 90.9 %all-gather.10.cloned.1.call-start = ((), (), s32[]{:S(2)}) async-start(), calls=%async_computation.9 | async-start | bytes 5898240 | tf_op jit(solution)/shard_map/all_gather | solution.py:152
  251.0 287.7 %copy-start.37 = (f32[768]{0:T(1024)}, f32[768]{0:T(1024)S(1)}, u32[]{:S(2)}) copy-start(f32[768]{0:T(1024)S(1)} %get-tuple-element.19) | copy-start | bytes 9220
  299.5 239.3 %copy-start.35 = (f32[256,3]{0,1:T(4,128)}, f32[256,3]{0,1:T(4,128)S(1)}, u32[]{:S(2)}) copy-start(f32[256,3]{0,1:T(4,128)S(1)} %broadcast_multiply_fusion.5) | copy-start | bytes 9220
  301.3 237.5 %copy-start.39 = (f32[256,3]{0,1:T(4,128)}, f32[256,3]{0,1:T(4,128)S(1)}, u32[]{:S(2)}) copy-start(f32[256,3]{0,1:T(4,128)S(1)} %add_rsqrt_fusion.1) | copy-start | bytes 9220
  303.0 108.8 %reduce-scatter.9.cloned.1.call-start = ((), (), s32[]{:S(2)}) async-start(), calls=%async_computation.10 | async-start | bytes 5898240 | tf_op jit(solution)/shard_map/reduce_scatter | solution.py:159
  347.2 7.8 copy-start.9
  363.8 95.4 %all-gather.12.cloned.1.call-start = ((), (), s32[]{:S(2)}) async-start(), calls=%async_computation.11 | async-start | bytes 5898240 | tf_op jit(solution)/shard_map/all_gather | solution.py:172
  421.6 111.6 %reduce-scatter.11.cloned.1.call-start = ((), (), s32[]{:S(2)}) async-start(), calls=%async_computation.12 | async-start | bytes 5898240 | tf_op jit(solution)/shard_map/reduce_scatter | solution.py:181
  485.2 94.3 %all-gather.14.cloned.1.call-start = ((), (), s32[]{:S(2)}) async-start(), calls=%async_computation.13 | async-start | bytes 5898240 | tf_op jit(solution)/shard_map/all_gather | solution.py:199
  538.7 40.8 %copy-start.52 = (f32[256,3]{0,1:T(4,128)}, f32[256,3]{0,1:T(4,128)S(1)}, u32[]{:S(2)}) copy-start(f32[256,3]{0,1:T(4,128)S(1)} %broadcast_multiply_fusion) | copy-start | bytes 9220
  538.8 40.8 %copy-start.54 = (f32[256,3]{0,1:T(4,128)}, f32[256,3]{0,1:T(4,128)S(1)}, u32[]{:S(2)}) copy-start(f32[256,3]{0,1:T(4,128)S(1)} %broadcast_multiply_fusion.1) | copy-start | bytes 9220
  541.9 41.8 %copy-start.17 = (bf16[1024,1,192]{0,2,1:T(8,128)(2,1)S(1)}, bf16[1024,1,192]{0,2,1:T(8,128)(2,1)}, u32[]{:S(2)}) copy-start(bf16[1024,1,192]{0,2,1:T(8,128)(2,1)} %copy-done.16) | copy-start | bytes 1179652
  541.9 314.3 %reduce-scatter.15.cloned.1.call-start = ((), (), s32[]{:S(2)}) async-start(), calls=%async_computation.15 | async-start | bytes 5308416 | tf_op jit(solution)/shard_map/reduce_scatter | solution.py:244
  590.0 19.5 %copy-start.32 = (bf16[1024,1,192]{0,2,1:T(8,128)(2,1)S(1)}, bf16[1024,1,192]{0,2,1:T(8,128)(2,1)}, u32[]{:S(2)}) copy-start(bf16[1024,1,192]{0,2,1:T(8,128)(2,1)} %copy-done.31) | copy-start | bytes 1179652
  642.2 18.9 %copy-start.29 = (bf16[1024,1,192]{0,2,1:T(8,128)(2,1)S(1)}, bf16[1024,1,192]{0,2,1:T(8,128)(2,1)}, u32[]{:S(2)}) copy-start(bf16[1024,1,192]{0,2,1:T(8,128)(2,1)} %get-tuple-element.39) | copy-start | bytes 1179652
  661.1 80.8 %copy-start.73 = (bf16[3,64,1024]{2,1,0:T(8,128)(2,1)}, bf16[3,64,1024]{2,1,0:T(8,128)(2,1)S(1)}, u32[]{:S(2)}) copy-start(bf16[3,64,1024]{2,1,0:T(8,128)(2,1)S(1)} %fusion.93) | copy-start | bytes 1179652
  693.7 18.9 %copy-start.27 = (bf16[1024,1,192]{0,2,1:T(8,128)(2,1)S(1)}, bf16[1024,1,192]{0,2,1:T(8,128)(2,1)}, u32[]{:S(2)}) copy-start(bf16[1024,1,192]{0,2,1:T(8,128)(2,1)} %copy-done.26) | copy-start | bytes 1179652
  712.6 29.2 %copy-start.77 = (bf16[3,64,1024]{2,1,0:T(8,128)(2,1)}, bf16[3,64,1024]{2,1,0:T(8,128)(2,1)S(1)}, u32[]{:S(2)}) copy-start(bf16[3,64,1024]{2,1,0:T(8,128)(2,1)S(1)} %fusion.87) | copy-start | bytes 1179652
  731.5 10.4 copy-start.79
  760.8 328.3 %reduce-scatter.17.cloned.1.call-start = ((), (), s32[]{:S(2)}) async-start(), calls=%async_computation.16 | async-start | bytes 15925248 | tf_op jit(solution)/shard_map/reduce_scatter | solution.py:195
  760.9 14.8 %slice-start = ((s8[4718592]{0:T(1024)(128)(4,1)}), s8[4194304]{0:T(1024)(128)(4,1)S(1)}, s32[]{:S(2)}) async-start(s8[4718592]{0:T(1024)(128)(4,1)} %bitcast.144), calls=%async_computation.17 | async-start | bytes 8388608
  760.9 14.8 %slice-start.2 = ((s8[4718592]{0:T(1024)(128)(4,1)}), s8[4194304]{0:T(1024)(128)(4,1)S(1)}, s32[]{:S(2)}) async-start(s8[4718592]{0:T(1024)(128)(4,1)} %bitcast.196), calls=%async_computation.19 | async-start | bytes 8388608
  768.4 7.3 slice-start.1
  768.4 7.3 slice-start.3
  819.5 319.3 %reduce-scatter.13.cloned.1.call-start = ((), (), s32[]{:S(2)}) async-start(), calls=%async_computation.14 | async-start | bytes 5898240 | tf_op jit(solution)/shard_map/reduce_scatter | solution.py:235
  828.0 310.8 %copy-start.4 = (bf16[256,3,768]{2,0,1:T(8,128)(2,1)S(1)}, bf16[256,3,768]{2,0,1:T(8,128)(2,1)}, u32[]{:S(2)}) copy-start(bf16[256,3,768]{2,0,1:T(8,128)(2,1)} %param.10) | copy-start | bytes 3538948
  828.0 310.8 %copy-start.7 = (bf16[256,3,768]{2,0,1:T(8,128)(2,1)S(1)}, bf16[256,3,768]{2,0,1:T(8,128)(2,1)}, u32[]{:S(2)}) copy-start(bf16[256,3,768]{2,0,1:T(8,128)(2,1)} %reduce-scatter.7.cloned.1.call-done) | copy-start | bytes 3538948
  828.0 310.8 %copy-start.36 = (f32[256,3]{0,1:T(4,128)S(1)}, f32[256,3]{0,1:T(4,128)}, u32[]{:S(2)}) copy-start(f32[256,3]{0,1:T(4,128)} %copy-done.35) | copy-start | bytes 9220
  828.0 310.8 %copy-start.38 = (f32[768]{0:T(1024)S(1)}, f32[768]{0:T(1024)}, u32[]{:S(2)}) copy-start(f32[768]{0:T(1024)} %copy-done.37) | copy-start | bytes 9220
  828.0 310.8 %copy-start.40 = (f32[256,3]{0,1:T(4,128)S(1)}, f32[256,3]{0,1:T(4,128)}, u32[]{:S(2)}) copy-start(f32[256,3]{0,1:T(4,128)} %copy-done.39) | copy-start | bytes 9220
  828.0 310.8 %copy-start.53 = (f32[256,3]{0,1:T(4,128)S(1)}, f32[256,3]{0,1:T(4,128)}, u32[]{:S(2)}) copy-start(f32[256,3]{0,1:T(4,128)} %copy-done.52) | copy-start | bytes 9220
  828.1 310.8 %copy-start.55 = (f32[256,3]{0,1:T(4,128)S(1)}, f32[256,3]{0,1:T(4,128)}, u32[]{:S(2)}) copy-start(f32[256,3]{0,1:T(4,128)} %copy-done.54) | copy-start | bytes 9220
  1094.8 89.2 %copy-start.51 = (f32[4,768]{1,0:T(4,128)S(1)}, f32[4,768]{1,0:T(4,128)}, u32[]{:S(2)}) copy-start(f32[4,768]{1,0:T(4,128)} %param.17) | copy-start | bytes 36868
  1094.8 89.2 %copy-start.62 = (f32[4,768]{1,0:T(4,128)S(1)}, f32[4,768]{1,0:T(4,128)}, u32[]{:S(2)}) copy-start(f32[4,768]{1,0:T(4,128)} %param.18) | copy-start | bytes 36868
  1094.8 89.2 %copy-start.63 = (f32[4,768]{1,0:T(4,128)S(1)}, f32[4,768]{1,0:T(4,128)}, u32[]{:S(2)}) copy-start(f32[4,768]{1,0:T(4,128)} %param.19) | copy-start | bytes 36868
  (50 other events, 180.4 us)
Sparse Core Ops, SparseCore 0:
  10.8 140.7 all-gather.5
  153.1 35.6 all-gather.7
  249.9 47.8 reduce-scatter.6
  303.1 37.4 all-gather.9
  364.0 47.7 reduce-scatter.8
  421.8 37.4 all-gather.11
  485.3 47.8 reduce-scatter.10
  542.0 37.4 all-gather.13
  760.9 95.2 reduce-scatter.14
  860.2 228.9 reduce-scatter.16
  1091.8 46.9 reduce-scatter.12
where the time goes:
time: 1210 us; the launch traced here: 1200 us
  waiting for transfers between devices  701 us (58%)
  matrix products  282 us (23%)
  other arithmetic  85.4 us (7%)
  local copies, waits for them, and re-layouts  75.9 us (6%)
  blocking collectives  39.5 us (3%)
  between operations  17.8 us (1%)
    reduce_scatter x1, waiting for transfers between devices, per_device(): lax.psum_scatter(to_owner(ffn_grads), 'seq', scatter_dimension=0, tiled=T...  231 us
    all_gather x1, waiting for transfers between devices, per_device(): lax.all_gather(master.astype(jnp.bfloat16), 'seq', axis=0, tiled=True)  132 us
    dot_general x3, matrix products, per_device(): jnp.einsum('hqk,qhd->khd', dscaled, queries, preferred_element_type=jnp.f...  58 us
    dot_general x3, matrix products, per_device(): jnp.einsum('hqk,khd->qhd', dscaled, keys_all, preferred_element_type=jnp....  57.2 us
    reduce_scatter x1, waiting for transfers between devices, per_device(): lax.psum_scatter((jnp.einsum('rpf,df->rpd', d_gate, w_gate, preferred_ele...  48 us
    reduce_scatter x1, waiting for transfers between devices, per_device(): lax.psum_scatter(jnp.einsum('rpf,df->rpd', piece, w_down, preferred_eleme...  47.9 us
    reduce_scatter x1, waiting for transfers between devices, per_device(): lax.psum_scatter(jnp.einsum('rpe,de->rpd', piece, w_out, preferred_elemen...  46.7 us
    reduce_scatter x1, waiting for transfers between devices, per_device(): lax.psum_scatter(jnp.einsum('rpc,dc->rpd', piece, w_qkv, preferred_elemen...  44 us
  transfers between devices with their start and end apart: 11, of which 11 were waited for; matrix products, arithmetic and copies ran while one was open for 9% of the time, Pallas kernels for 0%

commit v1 on v0

--- a/solution.py
+++ b/solution.py
@@ -1,7 +1,11 @@
 import jax
 import jax.numpy as jnp
 from jax import lax
+from jax.experimental import pallas as pl
+from jax.experimental.pallas import tpu as pltpu
 from jax.sharding import PartitionSpec as P
+
+MESH = pl.DeviceIdType.MESH
 
 H = 12
 HD = 64
@@ -20,6 +24,10 @@
 NORM_EPS = 1e-05
 ROOT_HALF = 0.7071067811865476
 DENSITY_SCALE = 0.3989422804014327
+EPS = 1e-05
+F32 = jnp.float32
+BF16 = jnp.bfloat16
+VMEM_LIMIT = 60 * 2**20
 
 
 def owner_maps(owner_blocks, rows, cap, block):
@@ -71,6 +79,438 @@
     raw = jnp.einsum("qhd,khd->hqk", queries, keys_all, preferred_element_type=jnp.float32)
     scores = raw * scale - slope[:, None, None] * distance[None]
     return jnp.where(same[None], scores, -1e30)
+
+
+def dot_nn(a, b):
+    return lax.dot_general(a, b, (((1,), (0,)), ((), ())), preferred_element_type=F32)
+
+
+def dot_nt(a, b):
+    return lax.dot_general(a, b, (((1,), (1,)), ((), ())), preferred_element_type=F32)
+
+
+def dot_tn(a, b):
+    return lax.dot_general(a, b, (((0,), (0,)), ((), ())), preferred_element_type=F32)
+
+
+def places():
+    wide = lax.axis_index("wide")
+    core = lax.rem(wide, 2)
+    row = wide // 2
+    return wide, core, row, wide + 1 - 2 * core, wide + 2 - 4 * row
+
+
+def greet(mate, across):
+    barrier = pltpu.get_barrier_semaphore()
+    for peer in (mate, across):
+        pl.semaphore_signal(barrier, inc=1, device_id={"wide": peer}, device_id_type=MESH)
+    pl.semaphore_wait(barrier, 2)
+
+
+def remote(source, target, send, recv, peer):
+    return pltpu.make_async_remote_copy(
+        src_ref=source,
+        dst_ref=target,
+        send_sem=send,
+        recv_sem=recv,
+        device_id={"wide": peer},
+        device_id_type=MESH,
+    )
+
+
+class Gather:
+    def __init__(self, held, send, recv, share):
+        self.held, self.send, self.recv, self.share = held, send, recv, share
+        _, self.core, self.row, self.mate, self.across = places()
+
+    def rows(self, core, row):
+        return pl.ds(pl.multiple_of((core * 2 + row) * self.share, self.share), self.share)
+
+    def copy(self, pack, leg):
+        row = 1 - self.row if leg == 2 else self.row
+        block = self.held.at[pack, self.rows(self.core, row)]
+        peer = self.mate if leg else self.across
+        return remote(block, block, self.send.at[pack, leg], self.recv.at[pack, leg], peer)
+
+    def start(self, pack):
+        self.copy(pack, 0).start()
+        self.copy(pack, 1).start()
+
+    def finish(self, pack):
+        self.copy(pack, 0).wait_recv()
+        self.copy(pack, 2).start()
+        self.copy(pack, 1).wait_recv()
+        self.copy(pack, 2).wait_recv()
+
+    def drain(self, pack):
+        for leg in range(3):
+            self.copy(pack, leg).wait_send()
+
+
+class Scatter:
+    def __init__(self, part, give, take, cross, reach, own, send, recv, share):
+        self.part, self.give, self.take = part, give, take
+        self.cross, self.reach, self.own = cross, reach, own
+        self.send, self.recv, self.share = send, recv, share
+        _, self.core, self.row, self.mate, self.across = places()
+
+    def copy(self, pack, leg):
+        source, target = (self.cross, self.reach) if leg else (self.give, self.take)
+        peer = self.across if leg else self.mate
+        return remote(
+            source.at[pack], target.at[pack], self.send.at[pack, leg], self.recv.at[pack, leg], peer
+        )
+
+    def half(self, which):
+        core = self.core if which else 1 - self.core
+        return pl.multiple_of(core * 2 * self.share, 2 * self.share)
+
+    def start(self, pack):
+        self.copy(pack, 0).start()
+
+    def middle(self, pack):
+        self.copy(pack, 0).wait_recv()
+        share = self.share
+        far = pl.ds(pl.multiple_of((1 - self.row) * share, share), share)
+        near = pl.ds(pl.multiple_of(self.row * share, share), share)
+        self.cross[pack] = (self.part[far, :] + self.take[pack, far, :].astype(F32)).astype(BF16)
+        self.copy(pack, 1).start()
+        self.own[pack] = self.part[near, :] + self.take[pack, near, :].astype(F32)
+
+    def finish(self, pack):
+        self.copy(pack, 1).wait_recv()
+
+    def drain(self, pack):
+        for leg in range(2):
+            self.copy(pack, leg).wait_send()
+
+
+def scatter_scratch(packs, share, width):
+    return [
+        pltpu.VMEM((2 * share, width), F32),
+        pltpu.VMEM((packs, 2 * share, width), BF16),
+        pltpu.VMEM((packs, 2 * share, width), BF16),
+        pltpu.VMEM((packs, share, width), BF16),
+        pltpu.VMEM((packs, share, width), BF16),
+        pltpu.VMEM((packs, share, width), F32),
+    ]
+
+
+def norm_parts(values):
+    center = values - jnp.mean(values, axis=-1, keepdims=True)
+    inverse = lax.rsqrt(jnp.mean(center * center, axis=-1, keepdims=True) + EPS)
+    return center * inverse, inverse
+
+
+def norm_pull(grad, normal, inverse, gain):
+    scaled = grad * gain
+    return inverse * (
+        scaled
+        - jnp.mean(scaled, axis=-1, keepdims=True)
+        - normal * jnp.mean(scaled * normal, axis=-1, keepdims=True)
+    )
+
+
+def loop(count, body, unroll=1):
+    def step(index, carry):
+        body(index)
+        return carry
+
+    lax.fori_loop(0, count, step, 0, unroll=unroll)
+
+
+def tile(index, size):
+    return pl.ds(pl.multiple_of(index * size, size), size)
+
+
+def ffn_kernel(
+    r1_ref,
+    cot_ref,
+    w_ref,
+    ln_ref,
+    mixed_ref,
+    dr1_ref,
+    grads_ref,
+    lngrad_ref,
+    weights,
+    held,
+    held2,
+    gates,
+    ups,
+    hid,
+    dgate,
+    dup,
+    turned,
+    turned2,
+    total,
+    g_tile,
+    u_tile,
+    send_a,
+    recv_a,
+    send_b,
+    recv_b,
+    send_c,
+    recv_c,
+    send_d,
+    recv_d,
+    load_sem,
+    store_sem,
+    *buffers,
+):
+    packs, share, width = r1_ref.shape
+    rows = 4 * share
+    fwd = buffers[:6]
+    units = weights.shape[1] // 3
+    col = 256
+    n_units, n_width = units // col, width // col
+    load = pltpu.make_async_copy(w_ref.at[:, pl.ds(w_ref.shape[1] - 3 * units, 3 * units)], weights, load_sem)
+    load.start()
+    _, core, row, mate, across = places()
+    greet(mate, across)
+    gather_one = Gather(held, send_a, recv_a, share)
+    scatter_one = Scatter(*fwd, send_b, recv_b, share)
+    gather_two = Gather(held2, send_c, recv_c, share)
+    scatter_two = Scatter(*fwd, send_d, recv_d, share)
+    gain1, shift1 = ln_ref[0:1, :], ln_ref[1:2, :]
+    gain2, shift2 = ln_ref[2:3, :], ln_ref[3:4, :]
+    lngrad_ref[...] = jnp.zeros_like(lngrad_ref)
+    chunk = 64
+
+    for pack in range(packs):
+        base = pl.multiple_of((core * 2 + row) * share, share)
+
+        def first(index, pack=pack, base=base):
+            normal, _ = norm_parts(r1_ref[pack, tile(index, chunk), :])
+            held[pack, pl.ds(pl.multiple_of(base + index * chunk, chunk), chunk), :] = (
+                normal * gain1 + shift1
+            ).astype(BF16)
+
+        loop(share // chunk, first)
+        gather_one.start(pack)
+    load.wait()
+
+    def forward(pack):
+        gather_one.finish(pack)
+        for which in range(2):
+            base = scatter_one.half(which)
+            big = pl.ds(base, 2 * share)
+
+            def ff(index):
+                cols = tile(index, col)
+                x = held[pack, big, :]
+                g_tile[...] = dot_nn(x, weights[:, cols])
+                u_tile[...] = dot_nn(x, weights[:, pl.ds(pl.multiple_of(units + index * col, col), col)])
+
+                def act(part):
+                    rws = tile(part, 32)
+                    gate, up = g_tile[rws, :], u_tile[rws, :]
+                    out = pl.ds(pl.multiple_of(base + part * 32, 32), 32)
+                    cumulative = 0.5 * (1.0 + lax.erf(gate * ROOT_HALF))
+                    hid[out, cols] = (gate * cumulative * up).astype(BF16)
+                    gates[pack, out, cols] = gate.astype(BF16)
+                    ups[pack, out, cols] = up.astype(BF16)
+
+                loop(2 * share // 32, act, unroll=2)
+
+            loop(n_units, ff)
+
+            def down(index):
+                wd = weights[tile(index, col), pl.ds(2 * units, units)]
+                value = dot_nt(hid[big, :], wd)
+                if which:
+                    scatter_one.part[:, tile(index, col)] = value
+                else:
+                    scatter_one.give[pack, :, tile(index, col)] = value.astype(BF16)
+
+            loop(n_width, down)
+            if not which:
+                scatter_one.start(pack)
+        scatter_one.middle(pack)
+
+    def turn(pack):
+        scatter_one.finish(pack)
+        gather_two_base = pl.multiple_of((core * 2 + row) * share, share)
+
+        def second(index):
+            rws = tile(index, chunk)
+            normal, _ = norm_parts(r1_ref[pack, rws, :])
+            ffn = scatter_one.own[pack, rws, :] + scatter_one.reach[pack, rws, :].astype(F32)
+            normal2, inverse2 = norm_parts(normal * gain1 + shift1 + ffn)
+            mixed_ref[pack, rws, :] = (normal2 * gain2 + shift2).astype(BF16)
+            grad = cot_ref[pack, rws, :].astype(F32)
+            value = norm_pull(grad, normal2, inverse2, gain2)
+            dr1_ref[pack, rws, :] = value
+            held2[pack, pl.ds(pl.multiple_of(gather_two_base + index * chunk, chunk), chunk), :] = value.astype(BF16)
+            lngrad_ref[2:3, :] += jnp.sum(grad * normal2, axis=0, keepdims=True)
+            lngrad_ref[3:4, :] += jnp.sum(grad, axis=0, keepdims=True)
+
+        loop(share // chunk, second)
+        scatter_one.drain(pack)
+        gather_two.start(pack)
+
+    def backward(pack):
+        gather_two.finish(pack)
+        for which in range(2):
+            base = scatter_two.half(which)
+            big = pl.ds(base, 2 * share)
+
+            def bf(index):
+                cols = tile(index, col)
+                g_tile[...] = dot_nn(
+                    held2[pack, big, :], weights[:, pl.ds(pl.multiple_of(2 * units + index * col, col), col)]
+                )
+
+                def act(part):
+                    rws = tile(part, 32)
+                    out = pl.ds(pl.multiple_of(base + part * 32, 32), 32)
+                    dhid = g_tile[rws, :]
+                    gate = gates[pack, out, cols].astype(F32)
+                    up = ups[pack, out, cols].astype(F32)
+                    cumulative = 0.5 * (1.0 + lax.erf(gate * ROOT_HALF))
+                    density = jnp.exp(-0.5 * gate * gate) * DENSITY_SCALE
+                    value = gate * cumulative
+                    hid[out, cols] = (value * up).astype(BF16)
+                    dgate[out, cols] = (dhid * up * (cumulative + gate * density)).astype(BF16)
+                    dup[out, cols] = (dhid * value).astype(BF16)
+
+                loop(2 * share // 32, act, unroll=2)
+
+            loop(n_units, bf)
+
+            def back(index):
+                rws = tile(index, col)
+                value = dot_nt(dgate[big, :], weights[rws, pl.ds(0, units)]) + dot_nt(
+                    dup[big, :], weights[rws, pl.ds(units, units)]
+                )
+                if which:
+                    scatter_two.part[:, tile(index, col)] = value
+                else:
+                    scatter_two.give[pack, :, tile(index, col)] = value.astype(BF16)
+
+            loop(n_width, back)
+            if not which:
+                scatter_two.start(pack)
+        scatter_two.middle(pack)
+
+    def weight_grads(pack):
+        def flip(index):
+            rws = tile(index, 256)
+            turned[:, rws] = held[pack, rws, :].T
+            turned2[:, rws] = held2[pack, rws, :].T
+
+        loop(rows // 256, flip)
+
+        def add(index):
+            rws = tile(index, col)
+            a = turned[rws, :]
+            b = turned2[rws, :]
+            parts = (dot_nn(a, dgate[...]), dot_nn(a, dup[...]), dot_nn(b, hid[...]))
+            for place, value in enumerate(parts):
+                cols = pl.ds(place * units, units)
+                if pack == 0:
+                    total[rws, cols] = value
+                else:
+                    value = total[rws, cols] + value
+                    if pack < packs - 1:
+                        total[rws, cols] = value
+                    else:
+                        gates[place, rws, :] = value.astype(BF16)
+
+        loop(n_width, add)
+
+    def last(pack):
+        scatter_two.finish(pack)
+
+        def third(index):
+            rws = tile(index, chunk)
+            normal, inverse = norm_parts(r1_ref[pack, rws, :])
+            grad = dr1_ref[pack, rws, :] + (
+                scatter_two.own[pack, rws, :] + scatter_two.reach[pack, rws, :].astype(F32)
+            )
+            dr1_ref[pack, rws, :] = norm_pull(grad, normal, inverse, gain1)
+            lngrad_ref[0:1, :] += jnp.sum(grad * normal, axis=0, keepdims=True)
+            lngrad_ref[1:2, :] += jnp.sum(grad, axis=0, keepdims=True)
+
+        loop(share // chunk, third)
+
+    for pack in range(packs):
+        forward(pack)
+        if pack:
+            turn(pack - 1)
+    for pack in range(packs):
+        backward(pack)
+        weight_grads(pack)
+        if pack == 0:
+            turn(packs - 1)
+        else:
+            last(pack - 1)
+    outs = [
+        pltpu.make_async_copy(
+            gates.at[place, pl.ds(0, width)],
+            grads_ref.at[:, pl.ds(place * units, units)],
+            store_sem.at[place],
+        )
+        for place in range(3)
+    ]
+    for out in outs:
+        out.start()
+    last(packs - 1)
+    for out in outs:
+        out.wait()
+    for pack in range(packs):
+        gather_one.drain(pack)
+        gather_two.drain(pack)
+        scatter_two.drain(pack)
+
+
+def ffn_call(r1, cot, weights, ln_params):
+    packs, share, width = r1.shape
+    rows = 4 * share
+    units = (weights.shape[1] - width) // 3
+    vm = pl.BlockSpec(memory_space=pltpu.VMEM)
+    hb = pl.BlockSpec(memory_space=pl.ANY)
+    dma = pltpu.SemaphoreType.DMA
+    return pl.pallas_call(
+        ffn_kernel,
+        out_shape=(
+            jax.ShapeDtypeStruct((packs, share, width), BF16),
+            jax.ShapeDtypeStruct((packs, share, width), F32),
+            jax.ShapeDtypeStruct((width, 3 * units), BF16),
+            jax.ShapeDtypeStruct((8, width), F32),
+        ),
+        in_specs=[vm, vm, hb, vm],
+        out_specs=(vm, vm, hb, vm),
+        scratch_shapes=[
+            pltpu.VMEM((width, 3 * units), BF16),
+            pltpu.VMEM((packs, rows, width), BF16),
+            pltpu.VMEM((packs, rows, width), BF16),
+            pltpu.VMEM((packs, rows, units), BF16),
+            pltpu.VMEM((packs, rows, units), BF16),
+            pltpu.VMEM((rows, units), BF16),
+            pltpu.VMEM((rows, units), BF16),
+            pltpu.VMEM((rows, units), BF16),
+            pltpu.VMEM((width, rows), BF16),
+            pltpu.VMEM((width, rows), BF16),
+            pltpu.VMEM((width, 3 * units), F32),
+            pltpu.VMEM((2 * share, 256), F32),
+            pltpu.VMEM((2 * share, 256), F32),
+            dma((packs, 3)),
+            dma((packs, 3)),
+            dma((packs, 2)),
+            dma((packs, 2)),
+            dma((packs, 3)),
+            dma((packs, 3)),
+            dma((packs, 2)),
+            dma((packs, 2)),
+            dma(()),
+            dma((3,)),
+            *scatter_scratch(packs, share, width),
+        ],
+        compiler_params=pltpu.CompilerParams(
+            collective_id=1, has_side_effects=True, vmem_limit_bytes=VMEM_LIMIT
+        ),
+        name="ffn",
+    )(r1, cot, weights, ln_params)
 
 
 def per_device(
@@ -147,55 +587,17 @@
         tiled=True,
     ).astype(jnp.float32)
     tokens = hidden_in.astype(jnp.float32)
-    normed, normal_one, inverse_one = norm_forward(tokens + attn, ln_params[0], ln_params[1])
-    normed_low = normed.astype(jnp.bfloat16)
-    piece = lax.all_gather(normed_low, "wide", axis=0, tiled=True)
-    gate = jnp.einsum("rpd,df->rpf", piece, w_gate, preferred_element_type=jnp.float32)
-    up_vals = jnp.einsum("rpd,df->rpf", piece, w_up, preferred_element_type=jnp.float32)
-    ffn_in, gate, up_vals = (piece, gate, up_vals)
-    cumulative = 0.5 * (1.0 + lax.erf(gate * ROOT_HALF))
-    hidden = (gate * cumulative * up_vals).astype(jnp.bfloat16)
-    piece = hidden
-    ffn = lax.psum_scatter(
-        jnp.einsum("rpf,df->rpd", piece, w_down, preferred_element_type=jnp.float32).astype(
-            jnp.bfloat16
-        ),
-        "wide",
-        scatter_dimension=0,
-        tiled=True,
-    ).astype(jnp.float32)
-    out, normal_two, inverse_two = norm_forward(normed + ffn, ln_params[2], ln_params[3])
-    mixed = out.astype(jnp.bfloat16)
-    grad_two, gain_two, shift_two = norm_backward(
-        cotangent.astype(jnp.float32), normal_two, inverse_two, ln_params[2]
-    )
-    piece = lax.all_gather(grad_two.astype(jnp.bfloat16), "wide", axis=0, tiled=True)
-    dffn_all = piece
-    dhidden = jnp.einsum("rpd,df->rpf", piece, w_down, preferred_element_type=jnp.float32)
-    density = jnp.exp(-0.5 * gate * gate) * DENSITY_SCALE
-    d_gate = (dhidden * up_vals * (cumulative + gate * density)).astype(jnp.bfloat16)
-    d_up = (dhidden * gate * cumulative).astype(jnp.bfloat16)
-    grad_down = jnp.einsum("rpd,rpf->df", dffn_all, hidden, preferred_element_type=jnp.float32)
-    grad_gate = jnp.einsum("rpd,rpf->df", ffn_in, d_gate, preferred_element_type=jnp.float32)
-    grad_up = jnp.einsum("rpd,rpf->df", ffn_in, d_up, preferred_element_type=jnp.float32)
-    grad_normed = grad_two + lax.psum_scatter(
-        (
-            jnp.einsum("rpf,df->rpd", d_gate, w_gate, preferred_element_type=jnp.float32)
-            + jnp.einsum("rpf,df->rpd", d_up, w_up, preferred_element_type=jnp.float32)
-        ).astype(jnp.bfloat16),
-        "wide",
-        scatter_dimension=0,
-        tiled=True,
-    ).astype(jnp.float32)
-    ffn_grads = jnp.concatenate([grad_gate, grad_up, grad_down], axis=1)
+    r1 = jnp.transpose(tokens + attn, (1, 0, 2))
+    mixed_p, dr1_p, ffn_grads, ln_rows = ffn_call(
+        r1, jnp.transpose(cotangent, (1, 0, 2)), weights, ln_params
+    )
+    mixed = jnp.transpose(mixed_p, (1, 0, 2))
+    grad_one = jnp.transpose(dr1_p, (1, 0, 2))
 
     def to_owner(grads):
         return jnp.where(valid[:, None], jnp.take(grads, source, axis=0), 0.0)
 
     ffn_owned = lax.psum_scatter(to_owner(ffn_grads), "seq", scatter_dimension=0, tiled=True)
-    grad_one, gain_one, shift_one = norm_backward(
-        grad_normed, normal_one, inverse_one, ln_params[0]
-    )
     piece = lax.all_gather(grad_one.astype(jnp.bfloat16), "wide", axis=0, tiled=True)
     dattn_all = piece
     dcontext = jnp.einsum("rpd,de->rpe", piece, w_out, preferred_element_type=jnp.float32).astype(
@@ -243,7 +645,7 @@
     attn_grads = jnp.concatenate([grad_qkv, grad_out], axis=1)
     attn_owned = lax.psum_scatter(to_owner(attn_grads), "seq", scatter_dimension=0, tiled=True)
     owned = jnp.concatenate([attn_owned, ffn_owned], axis=1)
-    ln_grads = jnp.stack([gain_one, shift_one, gain_two, shift_two], axis=0)
+    ln_grads = ln_rows[:4]
     squares, ln_total = lax.psum((jnp.sum(owned * owned), ln_grads), ("seq", "wide"))
     grad_norm = jnp.sqrt(squares + jnp.sum(ln_total * ln_total))
     clip = jnp.minimum(1.0, 1.0 / (grad_norm + 1e-06))

time: 1210 us -> 816 us (0.67)
  waiting for transfers between devices: 701 us -> 303 us
  Pallas kernels: 0 us -> 114 us
  matrix products: 282 us -> 217 us
  local copies, waits for them, and re-layouts: 75.9 us -> 41.6 us
    reduce_scatter x1, waiting for transfers between devices: 231 us -> 0.02 us  [per_device(): lax.psum_scatter(to_owner(ffn_grads), 'seq', scatter_dimension=0, tiled=T...]
    pallas_call x0 -> x1, Pallas kernels: none -> 114 us  [ffn_call(): pl.pallas_call(ffn_kernel, out_shape=(jax.ShapeDtypeStruct((packs, share,...]
    reduce_scatter x2 -> x0, waiting for transfers between devices: 95.9 us -> none  [the longest x1 48 us: per_device(): lax.psum_scatter((jnp.einsum('rpf,df->rpd', d_gate, w_gate, preferred_ele...]
    all_gather x2 -> x0, waiting for transfers between devices: 75.2 us -> none  [the longest x1 37.6 us: per_device(): lax.all_gather(grad_two.astype(jnp.bfloat16), 'wide', axis=0, tiled=True)]
    dot_general x9 -> x0, matrix products: 66 us -> none  [the longest x1 12.7 us: per_device(): jnp.einsum('rpd,df->rpf', piece, w_down, preferred_element_type=jnp.float32)]
    reduce_scatter x1, waiting for transfers between devices: 27.2 us -> 86.4 us  [per_device(): lax.psum_scatter(to_owner(attn_grads), 'seq', scatter_dimension=0, tiled=...]
    reduce_scatter x1, waiting for transfers between devices: 44 us -> 5.19 us  [per_device(): lax.psum_scatter(jnp.einsum('rpc,dc->rpd', piece, w_qkv, preferred_elemen...]
    all_gather x1, waiting for transfers between devices: 37.1 us -> 13.9 us  [per_device(): lax.all_gather(grad_one.astype(jnp.bfloat16), 'wide', axis=0, tiled=True)]
  transfers between devices with their start and end apart: 11 -> 7, of which waited for: 11 -> 6; matrix products, arithmetic and copies ran while one was open for 9% -> 30% of each run, Pallas kernels for 0% -> 0%
where the time goes in v1:
time: 816 us; the launch traced here: 809 us
  waiting for transfers between devices  303 us (37%)
  matrix products  217 us (27%)
  Pallas kernels  114 us (14%)
  other arithmetic  75.2 us (9%)
  local copies, waits for them, and re-layouts  41.6 us (5%)
  blocking collectives  40.7 us (5%)
  between operations  17.8 us (2%)
    all_gather x1, waiting for transfers between devices, per_device(): lax.all_gather(master.astype(jnp.bfloat16), 'seq', axis=0, tiled=True)  131 us
    pallas_call x1, Pallas kernels, ffn_call(): pl.pallas_call(ffn_kernel, out_shape=(jax.ShapeDtypeStruct((packs, share,...  114 us
    reduce_scatter x1, waiting for transfers between devices, per_device(): lax.psum_scatter(to_owner(attn_grads), 'seq', scatter_dimension=0, tiled=...  86.4 us
    dot_general x3, matrix products, per_device(): jnp.einsum('hqk,qhd->khd', dscaled, queries, preferred_element_type=jnp.f...  60.4 us
    dot_general x3, matrix products, per_device(): jnp.einsum('hqk,khd->qhd', dscaled, keys_all, preferred_element_type=jnp....  59.3 us
    reduce_scatter x1, waiting for transfers between devices, per_device(): lax.psum_scatter(jnp.einsum('rpe,de->rpd', piece, w_out, preferred_elemen...  47.9 us
    psum x1, blocking collectives, per_device(): lax.psum((jnp.sum(owned * owned), ln_grads), ('seq', 'wide'))  40.7 us
    dot_general x3, matrix products, scores_of(): jnp.einsum('qhd,khd->hqk', queries, keys_all, preferred_element_type=jnp....  22.5 us
  transfers between devices with their start and end apart: 7, of which 6 were waited for; matrix products, arithmetic and copies ran while one was open for 30% of the time, Pallas kernels for 0%

profile of v1, /device:TPU:0, one launch (start us, length us, event | category | flops | bytes accessed | tf_op | source)
XLA Modules:
  0.0 809.2 jit_solution(14733325395278720750)
XLA Ops:
  7.2 2.8 convert_element_type.140
  13.8 2.6 subtract_abs_fusion
  20.5 131.1 %all-gather.4.cloned.1.call-done = bf16[1536,3072]{1,0:T(8,128)(2,1)} async-done(((bf16[192,3072]{1,0:T(8,128)(2,1)}), bf16[1536,3072]{1,0:T(8,128)(2,1)}) %all-gather.4.cloned.1.call-update) | async-done | bytes 9437200 | tf_op jit(solution)/shard_map/all_gather | solution.py:540
  151.6 14.8 %gather_fusion = bf16[768,3072]{1,0:T(8,128)(2,1)} fusion(bf16[1536,3072]{1,0:T(8,128)(2,1)} %all-gather.4.cloned.1.call-done, s32[1024]{0:T(1024)S(1)} %pad_clamp_fusion.1), kind=kCustom, calls=%fused_computation | custom fusion | bytes 9440256 | tf_op jit(solution)/shard_map/jit(_take)/gather | solution.py:541
  166.4 5.0 broadcast_select_fusion.w_ref
  171.4 17.5 %all-gather.6.cloned.1.call-done = bf16[1024,3,768]{2,0,1:T(8,128)(2,1)} async-done(((bf16[256,3,768]{2,0,1:T(8,128)(2,1)}), bf16[1024,3,768]{2,0,1:T(8,128)(2,1)}) %all-gather.6.cloned.1.call-update) | async-done | bytes 4718608 | tf_op jit(solution)/shard_map/all_gather | solution.py:552
  188.8 6.0 convert_bitcast_fusion
  196.2 2.2 copy-done.10
  198.6 3.6 fusion.123
  202.8 2.9 exponential_reduce_fusion
  206.6 10.7 %fusion.124 = (f32[3,1024]{1,0:T(4,128)}, f32[3,1024,1024]{1,2,0:T(8,128)}) fusion(f32[1024,1024]{0,1:T(8,128)S(1)} %copy-done.10, f32[3]{0:T(128)} %copy-done.58, bf16[1024,3,64]{0,2,1:T(8,128)(2,1)} %bitcast.154, bf16[1024,3,64]{0,2,1:T(8,128)(2,1)} %bitcast.156, pred[1024,1024]{0,1:T(8,128)(4,1)} %broadcast_compare_fusion.1), kind=kOutput, calls=%fused_computation.167 | convolution fusion | flops 418378752 | bytes 18624524 | tf_op jit(solution)/shard_map/qhd,khd->hqk/dot_general | solution.py:79
  217.3 6.9 exponential_reduce_fusion.1
  225.5 8.2 %fusion.125 = (f32[3,1024]{1,0:T(4,128)}, f32[3,1024,1024]{1,2,0:T(8,128)}) fusion(f32[1024,1024]{0,1:T(8,128)S(1)} %copy-done.10, f32[3]{0:T(128)S(1)} %copy-done.59, bf16[1024,3,64]{0,2,1:T(8,128)(2,1)S(1)} %bitcast.150, bf16[1024,3,64]{0,2,1:T(8,128)(2,1)} %bitcast.152, pred[1024,1024]{0,1:T(8,128)(4,1)S(1)} %broadcast_compare_fusion.2), kind=kOutput, calls=%fused_computation.168 | convolution fusion | flops 418378752 | bytes 18624524 | tf_op jit(solution)/shard_map/qhd,khd->hqk/dot_general | solution.py:79
  233.8 6.2 exponential_reduce_fusion.2
  242.2 7.1 fusion.58
  249.4 2.0 fusion.52
  252.2 4.9 convolution_convert_fusion.1
  257.2 47.9 %reduce-scatter.5.cloned.1.call-done = bf16[256,3,768]{2,0,1:T(8,128)(2,1)} async-done(((bf16[1024,3,768]{2,0,1:T(8,128)(2,1)}), bf16[256,3,768]{2,0,1:T(8,128)(2,1)}) %reduce-scatter.5.cloned.1.call-update) | async-done | bytes 1179664 | tf_op jit(solution)/shard_map/reduce_scatter | solution.py:581
  305.1 2.9 add_bitcast_fusion.r1_ref
  308.1 113.8 %ffn.1 = (bf16[3,256,768]{2,1,0:T(8,128)(2,1)}, f32[3,256,768]{2,1,0:T(8,128)}, bf16[768,2304]{1,0:T(8,128)(2,1)}, f32[8,768]{1,0:T(8,128)}) custom-call(f32[3,256,768]{2,1,0:T(8,128)} %add_bitcast_fusion.r1_ref, bf16[3,256,768]{2,1,0:T(8,128)(2,1)} %bitcast.132, bf16[768,3072]{1,0:T(8,128)(2,1)} %broadcast_select_fusion.w_ref, f32[4,768]{1,0:T(4,128)} %ln_ref.1), custom_call_target="tpu_custom_call" | custom-call | tf_op jit(solution)/shard_map/ffn/pallas_call | solution.py:473
  421.9 2.9 bitcast_convert_fusion
  435.4 7.5 gather_fusion.2
  442.9 6.8 select_select_fusion
  449.8 13.9 %all-gather.8.cloned.1.call-done = bf16[1024,3,768]{2,0,1:T(8,128)(2,1)} async-done(((bf16[256,3,768]{2,0,1:T(8,128)(2,1)}), bf16[1024,3,768]{2,0,1:T(8,128)(2,1)}) %all-gather.8.cloned.1.call-update) | async-done | bytes 4718608 | tf_op jit(solution)/shard_map/all_gather | solution.py:601
  463.7 4.2 convolution_convert_fusion.2
  468.0 6.3 fusion.127
  474.4 19.9 %fusion.76 = bf16[3,64,1024]{2,1,0:T(8,128)(2,1)} fusion(bf16[1024,3,64]{0,2,1:T(8,128)(2,1)S(1)} %bitcast.157, f32[3,1024,1024]{1,2,0:T(8,128)} %fusion.127, f32[3,1024,1024]{1,2,0:T(8,128)} %get-tuple-element.47, f32[3,1024]{1,0:T(4,128)S(1)} %copy-done.31), kind=kOutput, calls=%fused_computation.77 | convolution fusion | flops 424873984 | bytes 25964544 | tf_op jit(solution)/shard_map/hqk,khd->qhd/dot_general | solution.py:619
  494.3 20.4 %fusion.79 = bf16[3,64,1024]{2,1,0:T(8,128)(2,1)} fusion(bf16[1024,3,64]{0,2,1:T(8,128)(2,1)S(1)} %bitcast.155, f32[3,1024,1024]{1,2,0:T(8,128)} %fusion.127, f32[3,1024,1024]{1,2,0:T(8,128)} %get-tuple-element.47, f32[3,1024]{1,0:T(4,128)S(1)} %copy-done.31), kind=kOutput, calls=%fused_computation.78 | convolution fusion | flops 424873984 | bytes 25964544 | tf_op jit(solution)/shard_map/hqk,qhd->khd/dot_general | solution.py:620
  514.7 6.3 fusion.126
  521.0 19.9 %fusion.82 = bf16[3,64,1024]{2,1,0:T(8,128)(2,1)} fusion(bf16[1024,3,64]{0,2,1:T(8,128)(2,1)S(1)} %bitcast.153, f32[3,1024,1024]{1,2,0:T(8,128)} %fusion.126, f32[3,1024,1024]{1,2,0:T(8,128)} %get-tuple-element.49, f32[3,1024]{1,0:T(4,128)S(1)} %copy-done.34), kind=kOutput, calls=%fused_computation.79 | convolution fusion | flops 424873984 | bytes 25964544 | tf_op jit(solution)/shard_map/hqk,khd->qhd/dot_general | solution.py:619
  540.9 20.2 %fusion.85 = bf16[3,64,1024]{2,1,0:T(8,128)(2,1)} fusion(bf16[1024,3,64]{0,2,1:T(8,128)(2,1)S(1)} %bitcast.151, f32[3,1024,1024]{1,2,0:T(8,128)} %fusion.126, f32[3,1024,1024]{1,2,0:T(8,128)} %get-tuple-element.49, f32[3,1024]{1,0:T(4,128)S(1)} %copy-done.34), kind=kOutput, calls=%fused_computation.80 | convolution fusion | flops 424873984 | bytes 25964544 | tf_op jit(solution)/shard_map/hqk,qhd->khd/dot_general | solution.py:620
  561.1 6.6 fusion.128
  567.7 19.5 %fusion.70 = bf16[3,64,1024]{2,1,0:T(8,128)(2,1)} fusion(bf16[1024,3,64]{0,2,1:T(8,128)(2,1)S(1)} %bitcast.149, f32[3,1024,1024]{1,2,0:T(8,128)} %fusion.128, f32[3,1024,1024]{1,2,0:T(8,128)} %copy-done.1, f32[3,1024]{1,0:T(4,128)S(1)} %log_add_fusion), kind=kOutput, calls=%fused_computation.75 | convolution fusion | flops 424873984 | bytes 25964544 | tf_op jit(solution)/shard_map/hqk,khd->qhd/dot_general | solution.py:619
  587.3 19.8 %fusion.73 = bf16[3,64,1024]{2,1,0:T(8,128)(2,1)} fusion(bf16[1024,3,64]{0,2,1:T(8,128)(2,1)S(1)} %bitcast.147, f32[3,1024,1024]{1,2,0:T(8,128)} %fusion.128, f32[3,1024,1024]{1,2,0:T(8,128)} %copy-done.1, f32[3,1024]{1,0:T(4,128)S(1)} %log_add_fusion), kind=kOutput, calls=%fused_computation.76 | convolution fusion | flops 424873984 | bytes 25964544 | tf_op jit(solution)/shard_map/hqk,qhd->khd/dot_general | solution.py:620
  607.2 3.4 convolution_bitcast_fusion.1
  610.6 6.8 fusion.67
  617.4 6.8 fusion.55
  624.3 2.1 fusion.61
  626.4 2.9 convolution_bitcast_fusion
  633.0 5.6 gather_fusion.1
  638.6 4.6 select_select_fusion.1
  643.4 7.2 convolution_convert_fusion
  652.7 86.4 %reduce-scatter.9.cloned.1.call-done = f32[192,768]{1,0:T(8,128)} async-done(((f32[1536,768]{1,0:T(8,128)}), f32[192,768]{1,0:T(8,128)}) %reduce-scatter.9.cloned.1.call-update) | async-done | bytes 589840 | tf_op jit(solution)/shard_map/reduce_scatter | solution.py:646
  739.1 2.3 multiply_reduce_fusion.3
  741.4 40.7 %all-reduce = (f32[]{:T(128)}, f32[4,768]{1,0:T(4,128)S(1)}) all-reduce(f32[]{:T(128)} %multiply_reduce_fusion.3, f32[4,768]{1,0:T(4,128)S(1)} %slice.80), channel_id=1, replica_groups=mesh['seq'=8,'wide'=4] {'seq','wide'}, use_global_device_ids=true, to_apply=%region_18.19 | all-reduce | flops 3073 | bytes 24584 | tf_op jit(solution)/shard_map/psum | solution.py:649
  784.8 5.2 reduce-scatter.7.cloned.1.call-done
  790.0 3.8 bitcast_add_fusion
  793.8 6.2 broadcast_select_fusion.1
  (192 shorter events, 33.8 us)
Async XLA Ops:
  7.2 9.2 %copy-start.46 = (s32[3,8]{1,0:T(4,128)S(1)}, s32[3,8]{1,0:T(4,128)}, u32[]{:S(2)}) copy-start(s32[3,8]{1,0:T(4,128)} %param.12) | copy-start | bytes 292
  7.2 144.4 %all-gather.4.cloned.1.call-start = ((), (), s32[]{:S(2)}) async-start(), calls=%async_computation.4 | async-start | bytes 10616832 | tf_op jit(solution)/shard_map/all_gather | solution.py:540
  10.1 178.7 %all-gather.6.cloned.1.call-start = ((), (), s32[]{:S(2)}) async-start(), calls=%async_computation.5 | async-start | bytes 5898240 | tf_op jit(solution)/shard_map/all_gather | solution.py:552
  10.8 294.3 %reduce-scatter.5.cloned.1.call-start = ((), (), s32[]{:S(2)}) async-start(), calls=%async_computation.6 | async-start | bytes 5898240 | tf_op jit(solution)/shard_map/reduce_scatter | solution.py:581
  13.7 182.4 %copy-start.58 = (f32[3]{0:T(128)}, f32[3]{0:T(128)S(1)}, u32[]{:S(2)}) copy-start(f32[3]{0:T(128)S(1)} %multiply_exponential_fusion) | copy-start | bytes 40
  196.1 29.4 %copy-start.25 = (bf16[1024,1,192]{0,2,1:T(8,128)(2,1)}, bf16[1024,1,192]{0,2,1:T(8,128)(2,1)S(1)}, u32[]{:S(2)}) copy-start(bf16[1024,1,192]{0,2,1:T(8,128)(2,1)S(1)} %get-tuple-element.32) | copy-start | bytes 1179652
  196.1 43.9 %copy-start.4 = (bf16[1024,1,192]{0,2,1:T(8,128)(2,1)}, bf16[1024,1,192]{0,2,1:T(8,128)(2,1)S(1)}, u32[]{:S(2)}) copy-start(bf16[1024,1,192]{0,2,1:T(8,128)(2,1)S(1)} %get-tuple-element.28) | copy-start | bytes 1179652
  196.1 46.0 %copy-start.8 = (bf16[1024,1,192]{0,2,1:T(8,128)(2,1)}, bf16[1024,1,192]{0,2,1:T(8,128)(2,1)S(1)}, u32[]{:S(2)}) copy-start(bf16[1024,1,192]{0,2,1:T(8,128)(2,1)S(1)} %get-tuple-element.31) | copy-start | bytes 1179652
  196.1 53.2 %copy-start.6 = (bf16[1024,1,192]{0,2,1:T(8,128)(2,1)}, bf16[1024,1,192]{0,2,1:T(8,128)(2,1)S(1)}, u32[]{:S(2)}) copy-start(bf16[1024,1,192]{0,2,1:T(8,128)(2,1)S(1)} %get-tuple-element.33) | copy-start | bytes 1179652
  202.2 37.8 %copy-start.1 = (f32[3,1024,1024]{1,2,0:T(8,128)}, f32[3,1024,1024]{1,2,0:T(8,128)S(1)}, u32[]{:S(2)}) copy-start(f32[3,1024,1024]{1,2,0:T(8,128)S(1)} %get-tuple-element.45) | copy-start | bytes 37748740
  217.3 8.2 %copy-start.59 = (f32[3]{0:T(128)S(1)}, f32[3]{0:T(128)}, u32[]{:S(2)}) copy-start(f32[3]{0:T(128)} %copy-done.58) | copy-start | bytes 40
  233.8 6.3 copy-start.36
  240.0 9.3 %copy-start.33 = (f32[3,1024]{1,0:T(4,128)}, f32[3,1024]{1,0:T(4,128)S(1)}, u32[]{:S(2)}) copy-start(f32[3,1024]{1,0:T(4,128)S(1)} %log_add_fusion.2) | copy-start | bytes 36868
  240.1 9.3 %slice-start.3 = ((s8[12582912]{0:T(1024)(128)(4,1)}), s8[4194304]{0:T(1024)(128)(4,1)S(1)}, s32[]{:S(2)}) async-start(s8[12582912]{0:T(1024)(128)(4,1)} %bitcast.118), calls=%async_computation.14 | async-start | bytes 8388608
  240.1 9.3 %slice-start.4 = ((s8[12582912]{0:T(1024)(128)(4,1)}), s8[4194304]{0:T(1024)(128)(4,1)S(1)}, s32[]{:S(2)}) async-start(s8[12582912]{0:T(1024)(128)(4,1)} %bitcast.118), calls=%async_computation.15 | async-start | bytes 8388608
  242.1 9.3 %copy-start.15 = (bf16[3,64,1024]{2,1,0:T(8,128)(2,1)}, bf16[3,64,1024]{2,1,0:T(8,128)(2,1)S(1)}, u32[]{:S(2)}) copy-start(bf16[3,64,1024]{2,1,0:T(8,128)(2,1)S(1)} %fusion.64) | copy-start | bytes 1179652
  242.2 7.2 slice-start.5
  252.2 52.9 %copy-start.3 = (bf16[256,3,768]{2,0,1:T(8,128)(2,1)S(1)}, bf16[256,3,768]{2,0,1:T(8,128)(2,1)}, u32[]{:S(2)}) copy-start(bf16[256,3,768]{2,0,1:T(8,128)(2,1)} %param.10) | copy-start | bytes 3538948
  257.2 206.5 %all-gather.8.cloned.1.call-start = ((), (), s32[]{:S(2)}) async-start(), calls=%async_computation.7 | async-start | bytes 5898240 | tf_op jit(solution)/shard_map/all_gather | solution.py:601
  421.8 13.6 %copy-start = (bf16[768,2304]{1,0:T(8,128)(2,1)S(1)}, bf16[768,2304]{1,0:T(8,128)(2,1)}, u32[]{:S(2)}) copy-start(bf16[768,2304]{1,0:T(8,128)(2,1)} %get-tuple-element.15) | copy-start | bytes 10616836
  424.8 226.5 %reduce-scatter.11.cloned.1.call-start = ((), (), s32[]{:S(2)}) async-start(), calls=%async_computation.10 | async-start | bytes 7962624 | tf_op jit(solution)/shard_map/reduce_scatter | solution.py:600
  449.7 18.3 %copy-start.9 = (bf16[1024,1,192]{0,2,1:T(8,128)(2,1)S(1)}, bf16[1024,1,192]{0,2,1:T(8,128)(2,1)}, u32[]{:S(2)}) copy-start(bf16[1024,1,192]{0,2,1:T(8,128)(2,1)} %copy-done.8) | copy-start | bytes 1179652
  449.7 289.4 %reduce-scatter.9.cloned.1.call-start = ((), (), s32[]{:S(2)}) async-start(), calls=%async_computation.9 | async-start | bytes 5308416 | tf_op jit(solution)/shard_map/reduce_scatter | solution.py:646
  468.0 6.4 copy-start.29
  468.0 6.3 copy-start.31
  474.4 19.9 %copy-start.28 = (bf16[1024,1,192]{0,2,1:T(8,128)(2,1)S(1)}, bf16[1024,1,192]{0,2,1:T(8,128)(2,1)}, u32[]{:S(2)}) copy-start(bf16[1024,1,192]{0,2,1:T(8,128)(2,1)} %get-tuple-element.30) | copy-start | bytes 1179652
  494.3 20.4 %copy-start.7 = (bf16[1024,1,192]{0,2,1:T(8,128)(2,1)S(1)}, bf16[1024,1,192]{0,2,1:T(8,128)(2,1)}, u32[]{:S(2)}) copy-start(bf16[1024,1,192]{0,2,1:T(8,128)(2,1)} %copy-done.6) | copy-start | bytes 1179652
  514.6 6.3 copy-start.27
  514.6 6.3 copy-start.34
  521.0 19.9 %copy-start.26 = (bf16[1024,1,192]{0,2,1:T(8,128)(2,1)S(1)}, bf16[1024,1,192]{0,2,1:T(8,128)(2,1)}, u32[]{:S(2)}) copy-start(bf16[1024,1,192]{0,2,1:T(8,128)(2,1)} %copy-done.25) | copy-start | bytes 1179652
  540.9 20.2 %copy-start.5 = (bf16[1024,1,192]{0,2,1:T(8,128)(2,1)S(1)}, bf16[1024,1,192]{0,2,1:T(8,128)(2,1)}, u32[]{:S(2)}) copy-start(bf16[1024,1,192]{0,2,1:T(8,128)(2,1)} %copy-done.4) | copy-start | bytes 1179652
  561.1 6.6 copy-start.24
  567.7 19.5 %copy-start.22 = (bf16[1024,1,192]{0,2,1:T(8,128)(2,1)S(1)}, bf16[1024,1,192]{0,2,1:T(8,128)(2,1)}, u32[]{:S(2)}) copy-start(bf16[1024,1,192]{0,2,1:T(8,128)(2,1)} %copy-done.21) | copy-start | bytes 1179652
  587.3 19.9 %copy-start.16 = (bf16[3,64,1024]{2,1,0:T(8,128)(2,1)S(1)}, bf16[3,64,1024]{2,1,0:T(8,128)(2,1)}, u32[]{:S(2)}) copy-start(bf16[3,64,1024]{2,1,0:T(8,128)(2,1)} %copy-done.15) | copy-start | bytes 1179652
  587.3 19.9 %copy-start.18 = (bf16[3,64,1024]{2,1,0:T(8,128)(2,1)S(1)}, bf16[3,64,1024]{2,1,0:T(8,128)(2,1)}, u32[]{:S(2)}) copy-start(bf16[3,64,1024]{2,1,0:T(8,128)(2,1)} %copy-done.17) | copy-start | bytes 1179652
  587.3 19.9 %copy-start.20 = (bf16[3,64,1024]{2,1,0:T(8,128)(2,1)S(1)}, bf16[3,64,1024]{2,1,0:T(8,128)(2,1)}, u32[]{:S(2)}) copy-start(bf16[3,64,1024]{2,1,0:T(8,128)(2,1)} %copy-done.19) | copy-start | bytes 1179652
  610.6 13.6 %slice-start = ((s8[12582912]{0:T(1024)(128)(4,1)}), s8[4194304]{0:T(1024)(128)(4,1)S(1)}, s32[]{:S(2)}) async-start(s8[12582912]{0:T(1024)(128)(4,1)} %bitcast.116), calls=%async_computation.11 | async-start | bytes 8388608
  610.6 13.6 %slice-start.1 = ((s8[12582912]{0:T(1024)(128)(4,1)}), s8[4194304]{0:T(1024)(128)(4,1)S(1)}, s32[]{:S(2)}) async-start(s8[12582912]{0:T(1024)(128)(4,1)} %bitcast.116), calls=%async_computation.12 | async-start | bytes 8388608
  617.4 6.8 slice-start.2
  617.4 6.8 copy-start.32
  617.4 9.0 %slice-start.6 = ((s8[4718592]{0:T(1024)(128)(4,1)}), s8[4194304]{0:T(1024)(128)(4,1)S(1)}, s32[]{:S(2)}) async-start(s8[4718592]{0:T(1024)(128)(4,1)} %bitcast.160), calls=%async_computation.17 | async-start | bytes 8388608
  643.3 8.1 copy-start.44
  643.3 146.7 %reduce-scatter.7.cloned.1.call-start = ((), (), s32[]{:S(2)}) async-start(), calls=%async_computation.8 | async-start | bytes 5898240 | tf_op jit(solution)/shard_map/reduce_scatter | solution.py:637
  650.6 133.6 %copy-start.38 = (f32[4,768]{1,0:T(4,128)S(1)}, f32[4,768]{1,0:T(4,128)}, u32[]{:S(2)}) copy-start(f32[4,768]{1,0:T(4,128)} %ln_ref.1) | copy-start | bytes 36868
  650.6 133.6 %copy-start.41 = (f32[4,768]{1,0:T(4,128)S(1)}, f32[4,768]{1,0:T(4,128)}, u32[]{:S(2)}) copy-start(f32[4,768]{1,0:T(4,128)} %param.18) | copy-start | bytes 36868
  650.6 133.6 %copy-start.42 = (f32[4,768]{1,0:T(4,128)S(1)}, f32[4,768]{1,0:T(4,128)}, u32[]{:S(2)}) copy-start(f32[4,768]{1,0:T(4,128)} %param.19) | copy-start | bytes 36868
  739.1 54.7 %copy-start.11 = (f32[192,768]{1,0:T(8,128)S(1)}, f32[192,768]{1,0:T(8,128)}, u32[]{:S(2)}) copy-start(f32[192,768]{1,0:T(8,128)} %reduce-scatter.9.cloned.1.call-done) | copy-start | bytes 1769476
  793.8 6.2 copy-start.13
  (27 other events, 87.3 us)
Sparse Core Ops, SparseCore 0:
  10.8 140.7 all-gather.3
  153.1 35.6 all-gather.5
  257.3 47.8 reduce-scatter.4
  424.9 38.6 all-gather.7
  467.7 128.9 reduce-scatter.10
  643.4 95.6 reduce-scatter.8
  741.6 48.3 reduce-scatter.6

commit v2 on v1

--- a/solution.py
+++ b/solution.py
@@ -27,6 +27,7 @@
 EPS = 1e-05
 F32 = jnp.float32
 BF16 = jnp.bfloat16
+NEG = -1e30
 VMEM_LIMIT = 60 * 2**20
 
 
@@ -48,24 +49,6 @@
     return (source, valid, target)
 
 
-def norm_forward(values, gain, shift):
-    center = values - jnp.mean(values, axis=-1, keepdims=True)
-    variance = jnp.mean(center * center, axis=-1, keepdims=True)
-    inverse = lax.rsqrt(variance + NORM_EPS)
-    normal = center * inverse
-    return (normal * gain + shift, normal, inverse)
-
-
-def norm_backward(grad, normal, inverse, gain):
-    scaled = grad * gain
-    result = inverse * (
-        scaled
-        - jnp.mean(scaled, axis=-1, keepdims=True)
-        - normal * jnp.mean(scaled * normal, axis=-1, keepdims=True)
-    )
-    return (result, jnp.sum(grad * normal, axis=(0, 1)), jnp.sum(grad, axis=(0, 1)))
-
-
 def adamw(param, grad, first, second, decay, rate):
     first_new = BETA_ONE * first + (1.0 - BETA_ONE) * grad
     second_new = BETA_TWO * second + (1.0 - BETA_TWO) * grad * grad
@@ -73,12 +56,6 @@
     second_hat = second_new / (1.0 - BETA_TWO**STEP)
     param_new = param - rate * (first_hat / (jnp.sqrt(second_hat) + EPSILON) + decay * param)
     return (param_new, first_new, second_new)
-
-
-def scores_of(queries, keys_all, same, slope, distance, scale):
-    raw = jnp.einsum("qhd,khd->hqk", queries, keys_all, preferred_element_type=jnp.float32)
-    scores = raw * scale - slope[:, None, None] * distance[None]
-    return jnp.where(same[None], scores, -1e30)
 
 
 def dot_nn(a, b):
@@ -513,6 +490,490 @@
     )(r1, cot, weights, ln_params)
 
 
+class Runs:
+    def __init__(self, offsets, pack):
+        names = [offsets[pack, place] for place in range(8)]
+        start = jnp.int32(4)
+        for place in range(3, -1, -1):
+            start = lax.select(names[place] == names[place + 3], jnp.int32(place), start)
+        self.start = start
+        self.names = [lax.select(start > place, names[place], names[place + 4]) for place in range(4)]
+
+    def masks(self, index):
+        own = self.names[0]
+        for place in range(1, 4):
+            own = lax.select(index == place, self.names[place], own)
+        return [lax.select(own == name, jnp.float32(0.0), jnp.float32(NEG)) for name in self.names]
+
+    def arrange(self, plain, order):
+        for place in range(4):
+            value = plain[held_run(place), :]
+            for start in range(1, 5):
+                value = lax.select(self.start == start, plain[held_run(place + start), :], value)
+            order(pl.ds(place * UNIT, UNIT), value)
+            value = lax.select(self.start > place, plain[held_run(place), :], plain[held_run(place + 4), :])
+            order(pl.ds((place + 4) * UNIT, UNIT), value)
+
+    def restore(self, order, plain):
+        for run in range(8):
+            first = max(0, run - 3)
+            value = order[pl.ds((run - first) * UNIT, UNIT), :]
+            for start in range(first + 1, min(run, 4) + 1):
+                value = lax.select(self.start == start, order[pl.ds((run - start) * UNIT, UNIT), :], value)
+            if run < 4:
+                value = lax.select(self.start > run, order[pl.ds((run + 4) * UNIT, UNIT), :], value)
+            else:
+                value = lax.select(self.start <= run - 4, order[pl.ds(run * UNIT, UNIT), :], value)
+            plain(held_run(run), value)
+
+
+def held_run(run):
+    half, part = divmod(run, 2)
+    return pl.ds(((half % 2) * 2 + half // 2) * 2 * UNIT + part * UNIT, UNIT)
+
+
+def writer(ref, *at):
+    def write(rows, value):
+        ref[(*at, rows, slice(None))] = value
+
+    return write
+
+
+def fill_bias(bias, slopes, wide):
+    heads, size, _ = bias.shape
+
+    def fill(index):
+        rws = tile(index, UNIT)
+        down = lax.broadcasted_iota(jnp.int32, (UNIT, size), 0) + index * UNIT
+        along = lax.broadcasted_iota(jnp.int32, (UNIT, size), 1)
+        distance = jnp.abs(down - along).astype(F32)
+        for head in range(heads):
+            bias[head, rws, :] = -slopes[wide * heads + head] * distance
+
+    loop(size // UNIT, fill)
+
+
+def split_weights(packed, w_qkv, w_out):
+    width, each = packed.shape[0], packed.shape[1] // 4
+    wide = w_out.shape[1]
+
+    def part(index):
+        rws = tile(index, 128)
+        zeros = jnp.zeros((128, wide - each), BF16)
+        for place in range(4):
+            value = jnp.concatenate([packed[rws, pl.ds(place * each, each)], zeros], axis=1)
+            if place < 3:
+                w_qkv[rws, pl.ds(place * wide, wide)] = value
+            else:
+                w_out[rws, :] = value
+
+    loop(width // 128, part)
+
+
+def head_lanes():
+    lane = lax.broadcasted_iota(jnp.int32, (1, 128), 1)
+    return lane < HD
+
+
+def attn_kernel(
+    offsets_ref,
+    slopes_ref,
+    x_ref,
+    w_ref,
+    r1_ref,
+    held_ref,
+    qkv_ref,
+    ctx_ref,
+    packed,
+    w_qkv,
+    w_out,
+    bias,
+    held,
+    plain,
+    qkv,
+    ctx_order,
+    ctx,
+    send_a,
+    recv_a,
+    send_b,
+    recv_b,
+    load_sem,
+    store_sem,
+    *buffers,
+):
+    packs, share, width = x_ref.shape
+    rows = 4 * share
+    lanes = w_out.shape[1]
+    group = rows // 2
+    load = pltpu.make_async_copy(w_ref.at[:, pl.ds(0, packed.shape[1])], packed, load_sem)
+    load.start()
+    wide, core, row, mate, across = places()
+    greet(mate, across)
+    gather = Gather(held, send_a, recv_a, share)
+    scatter = Scatter(*buffers, send_b, recv_b, share)
+    base = pl.multiple_of((core * 2 + row) * share, share)
+    for pack in range(packs):
+        held[pack, pl.ds(base, share), :] = x_ref[pack]
+        gather.start(pack)
+    fill_bias(bias, slopes_ref, wide)
+    load.wait()
+    split_weights(packed, w_qkv, w_out)
+    low = head_lanes()
+    stores = []
+
+    def attend(pack):
+        runs = Runs(offsets_ref, pack)
+        gather.finish(pack)
+
+        def project(index):
+            rws = tile(index, 256)
+            plain[rws, :] = dot_nn(held[pack, rws, :], w_qkv[...]).astype(BF16)
+
+        loop(rows // 256, project)
+        runs.arrange(plain, writer(qkv, pack))
+        for side in range(2):
+            keys = pl.ds(side * group, group)
+
+            def chunk(index, side=side, keys=keys, pack=pack):
+                rws = pl.ds(pl.multiple_of(side * group + index * UNIT, UNIT), UNIT)
+                if side:
+                    mask = jnp.concatenate(
+                        [jnp.full((1, UNIT), part, F32) for part in runs.masks(index)], axis=1
+                    )
+                outs = []
+                for head in range(3):
+                    block = pl.ds(0 if head < 2 else 128, 128)
+                    queries = qkv[pack, rws, block]
+                    if head < 2:
+                        queries = jnp.where(low if head == 0 else ~low, queries, jnp.zeros_like(queries))
+                    k_block = pl.ds(lanes + (0 if head < 2 else 128), 128)
+                    v_block = pl.ds(2 * lanes + (0 if head < 2 else 128), 128)
+                    scores = dot_nt(queries, qkv[pack, keys, k_block]) * HD ** (-0.5)
+                    scores = scores + bias[head, tile(index, UNIT), :]
+                    if side:
+                        scores = scores + mask
+                    powers = jnp.exp(scores - jnp.max(scores, axis=-1, keepdims=True))
+                    total = jnp.sum(powers, axis=-1, keepdims=True)
+                    outs.append(dot_nn(powers.astype(BF16), qkv[pack, keys, v_block]) / total)
+                ctx_order[rws, pl.ds(0, 128)] = jnp.where(low, outs[0], outs[1]).astype(BF16)
+                ctx_order[rws, pl.ds(128, 128)] = outs[2].astype(BF16)
+
+            loop(4, chunk)
+        runs.restore(ctx_order, writer(ctx, pack))
+        for which in range(2):
+            big = pl.ds(scatter.half(which), 2 * share)
+
+            def out(index, which=which, big=big):
+                cols = tile(index, 256)
+                value = dot_nt(ctx[pack, big, :], w_out[cols, :])
+                if which:
+                    scatter.part[:, cols] = value
+                else:
+                    scatter.give[pack, :, cols] = value.astype(BF16)
+
+            loop(width // 256, out)
+            if not which:
+                scatter.start(pack)
+        scatter.middle(pack)
+        for place, (source, target) in enumerate(((held, held_ref), (qkv, qkv_ref), (ctx, ctx_ref))):
+            copy = pltpu.make_async_copy(source.at[pack], target.at[pack], store_sem.at[pack, place])
+            copy.start()
+            stores.append(copy)
+
+    def settle(pack):
+        scatter.finish(pack)
+
+        def add(index):
+            rws = tile(index, 64)
+            attn = scatter.own[pack, rws, :] + scatter.reach[pack, rws, :].astype(F32)
+            r1_ref[pack, rws, :] = x_ref[pack, rws, :].astype(F32) + attn
+
+        loop(share // 64, add)
+
+    for pack in range(packs):
+        attend(pack)
+        if pack:
+            settle(pack - 1)
+    settle(packs - 1)
+    for copy in stores:
+        copy.wait()
+    for pack in range(packs):
+        gather.drain(pack)
+        scatter.drain(pack)
+
+
+def back_kernel(
+    offsets_ref,
+    slopes_ref,
+    dr1_ref,
+    w_ref,
+    x_ref,
+    qkv_ref,
+    ctx_ref,
+    grad_ref,
+    grads_ref,
+    packed,
+    w_qkv,
+    w_out,
+    bias,
+    held,
+    x_all,
+    qkv,
+    ctx,
+    plain,
+    dctx,
+    dorder,
+    dplain,
+    sum_k,
+    sum_v,
+    turned,
+    total,
+    total_out,
+    send_a,
+    recv_a,
+    send_b,
+    recv_b,
+    load_sem,
+    fetch_sem,
+    *buffers,
+):
+    packs, share, width = dr1_ref.shape
+    rows = 4 * share
+    lanes = w_out.shape[1]
+    group = rows // 2
+    load = pltpu.make_async_copy(w_ref.at[:, pl.ds(0, packed.shape[1])], packed, load_sem)
+    load.start()
+    fetches = []
+    for pack in range(packs):
+        for place, (source, target) in enumerate(((x_ref, x_all), (qkv_ref, qkv), (ctx_ref, ctx))):
+            copy = pltpu.make_async_copy(source.at[pack], target.at[pack], fetch_sem.at[pack, place])
+            copy.start()
+            fetches.append(copy)
+    wide, core, row, mate, across = places()
+    greet(mate, across)
+    gather = Gather(held, send_a, recv_a, share)
+    scatter = Scatter(*buffers, send_b, recv_b, share)
+    base = pl.multiple_of((core * 2 + row) * share, share)
+    for pack in range(packs):
+        held[pack, pl.ds(base, share), :] = dr1_ref[pack].astype(BF16)
+        gather.start(pack)
+    fill_bias(bias, slopes_ref, wide)
+    load.wait()
+    split_weights(packed, w_qkv, w_out)
+    low = head_lanes()
+    scale = HD ** (-0.5)
+
+    def pull(pack):
+        runs = Runs(offsets_ref, pack)
+        gather.finish(pack)
+
+        def project(index):
+            rws = tile(index, 256)
+            plain[rws, :] = dot_nn(held[pack, rws, :], w_out[...]).astype(BF16)
+
+        loop(rows // 256, project)
+        runs.arrange(plain, writer(dctx))
+        for copy in fetches[3 * pack : 3 * pack + 3]:
+            copy.wait()
+        for side in range(2):
+            keys = pl.ds(side * group, group)
+            sum_k[...] = jnp.zeros_like(sum_k)
+            sum_v[...] = jnp.zeros_like(sum_v)
+
+            def chunk(index, side=side, keys=keys, pack=pack):
+                rws = pl.ds(pl.multiple_of(side * group + index * UNIT, UNIT), UNIT)
+                masks = runs.masks(index)
+                for part in range(2):
+                    heads = (0, 1) if part == 0 else (2,)
+                    block = pl.ds(part * 128, 128)
+                    k_block = pl.ds(lanes + part * 128, 128)
+                    v_block = pl.ds(2 * lanes + part * 128, 128)
+                    k_all, v_all = qkv[pack, keys, k_block], qkv[pack, keys, v_block]
+                    dq = None
+                    for head in heads:
+                        queries, dout, k_own = qkv[pack, rws, block], dctx[rws, block], k_all
+                        if part == 0:
+                            keep = low if head == 0 else ~low
+                            queries = jnp.where(keep, queries, jnp.zeros_like(queries))
+                            dout = jnp.where(keep, dout, jnp.zeros_like(dout))
+                            k_own = jnp.where(keep, k_own, jnp.zeros_like(k_own))
+                        scores = dot_nt(k_all, queries) * scale + bias[head, :, tile(index, UNIT)]
+                        if side:
+                            scores = jnp.concatenate(
+                                [scores[t * UNIT : (t + 1) * UNIT] + masks[t] for t in range(4)], axis=0
+                            )
+                        powers = jnp.exp(scores - jnp.max(scores, axis=0, keepdims=True))
+                        probs = powers * (1.0 / jnp.sum(powers, axis=0, keepdims=True))
+                        dprobs = dot_nt(v_all, dout)
+                        delta = jnp.sum(probs * dprobs, axis=0, keepdims=True)
+                        dscaled = (probs * (dprobs - delta) * scale).astype(BF16)
+                        sum_v[:, block] += dot_nn(probs.astype(BF16), dout)
+                        sum_k[:, block] += dot_nn(dscaled, queries)
+                        term = dot_tn(dscaled, k_own)
+                        dq = term if dq is None else dq + term
+                    dorder[rws, block] = dq.astype(BF16)
+
+            loop(4, chunk)
+            dorder[keys, pl.ds(lanes, lanes)] = sum_k[...].astype(BF16)
+            dorder[keys, pl.ds(2 * lanes, lanes)] = sum_v[...].astype(BF16)
+        runs.restore(dorder, writer(dplain))
+        for which in range(2):
+            big = pl.ds(scatter.half(which), 2 * share)
+
+            def out(index, which=which, big=big):
+                cols = tile(index, 256)
+                value = dot_nt(dplain[big, :], w_qkv[cols, :])
+                if which:
+                    scatter.part[:, cols] = value
+                else:
+                    scatter.give[pack, :, cols] = value.astype(BF16)
+
+            loop(width // 256, out)
+            if not which:
+                scatter.start(pack)
+        scatter.middle(pack)
+
+    def weight_grads(pack):
+        for source, result, target in ((x_all, dplain, total), (held, ctx.at[pack], total_out)):
+
+            def flip(index, source=source):
+                rws = tile(index, 256)
+                turned[:, rws] = source[pack, rws, :].T
+
+            loop(rows // 256, flip)
+
+            def add(index, result=result, target=target):
+                rws = tile(index, 256)
+                value = dot_nn(turned[rws, :], result[...])
+                if pack:
+                    value = value + target[rws, :]
+                target[rws, :] = value
+
+            loop(width // 256, add)
+
+    def settle(pack):
+        scatter.finish(pack)
+
+        def add(index):
+            rws = tile(index, 64)
+            grad_ref[pack, rws, :] = dr1_ref[pack, rws, :] + (
+                scatter.own[pack, rws, :] + scatter.reach[pack, rws, :].astype(F32)
+            )
+
+        loop(share // 64, add)
+
+    for pack in range(packs):
+        pull(pack)
+        weight_grads(pack)
+        if pack:
+            settle(pack - 1)
+    each = width // 4
+
+    def pack_up(index):
+        rws = tile(index, 128)
+        pieces = [total[rws, pl.ds(place * lanes, each)] for place in range(3)]
+        pieces.append(total_out[rws, pl.ds(0, each)])
+        grads_ref[rws, :] = jnp.concatenate([piece.astype(BF16) for piece in pieces], axis=1)
+
+    loop(width // 128, pack_up)
+    settle(packs - 1)
+    for pack in range(packs):
+        gather.drain(pack)
+        scatter.drain(pack)
+
+
+def attn_call(x, weights, offsets, slopes):
+    packs, share, width = x.shape
+    rows = 4 * share
+    lanes = 256
+    vm = pl.BlockSpec(memory_space=pltpu.VMEM)
+    hb = pl.BlockSpec(memory_space=pl.ANY)
+    sm = pl.BlockSpec(memory_space=pltpu.SMEM)
+    dma = pltpu.SemaphoreType.DMA
+    return pl.pallas_call(
+        attn_kernel,
+        out_shape=(
+            jax.ShapeDtypeStruct((packs, share, width), F32),
+            jax.ShapeDtypeStruct((packs, rows, width), BF16),
+            jax.ShapeDtypeStruct((packs, rows, 3 * lanes), BF16),
+            jax.ShapeDtypeStruct((packs, rows, lanes), BF16),
+        ),
+        in_specs=[sm, sm, vm, hb],
+        out_specs=(vm, hb, hb, hb),
+        scratch_shapes=[
+            pltpu.VMEM((width, width), BF16),
+            pltpu.VMEM((width, 3 * lanes), BF16),
+            pltpu.VMEM((width, lanes), BF16),
+            pltpu.VMEM((3, rows // 2, rows // 2), F32),
+            pltpu.VMEM((packs, rows, width), BF16),
+            pltpu.VMEM((rows, 3 * lanes), BF16),
+            pltpu.VMEM((packs, rows, 3 * lanes), BF16),
+            pltpu.VMEM((rows, lanes), BF16),
+            pltpu.VMEM((packs, rows, lanes), BF16),
+            dma((packs, 3)),
+            dma((packs, 3)),
+            dma((packs, 2)),
+            dma((packs, 2)),
+            dma(()),
+            dma((packs, 3)),
+            *scatter_scratch(packs, share, width),
+        ],
+        compiler_params=pltpu.CompilerParams(
+            collective_id=2, has_side_effects=True, vmem_limit_bytes=VMEM_LIMIT
+        ),
+        name="attn",
+    )(offsets, slopes, x, weights)
+
+
+def back_call(dr1, weights, x_all, qkv, ctx, offsets, slopes):
+    packs, share, width = dr1.shape
+    rows = 4 * share
+    lanes = 256
+    vm = pl.BlockSpec(memory_space=pltpu.VMEM)
+    hb = pl.BlockSpec(memory_space=pl.ANY)
+    sm = pl.BlockSpec(memory_space=pltpu.SMEM)
+    dma = pltpu.SemaphoreType.DMA
+    return pl.pallas_call(
+        back_kernel,
+        out_shape=(
+            jax.ShapeDtypeStruct((packs, share, width), F32),
+            jax.ShapeDtypeStruct((width, width), BF16),
+        ),
+        in_specs=[sm, sm, vm, hb, hb, hb, hb],
+        out_specs=(vm, vm),
+        scratch_shapes=[
+            pltpu.VMEM((width, width), BF16),
+            pltpu.VMEM((width, 3 * lanes), BF16),
+            pltpu.VMEM((width, lanes), BF16),
+            pltpu.VMEM((3, rows // 2, rows // 2), F32),
+            pltpu.VMEM((packs, rows, width), BF16),
+            pltpu.VMEM((packs, rows, width), BF16),
+            pltpu.VMEM((packs, rows, 3 * lanes), BF16),
+            pltpu.VMEM((packs, rows, lanes), BF16),
+            pltpu.VMEM((rows, lanes), BF16),
+            pltpu.VMEM((rows, lanes), BF16),
+            pltpu.VMEM((rows, 3 * lanes), BF16),
+            pltpu.VMEM((rows, 3 * lanes), BF16),
+            pltpu.VMEM((rows // 2, lanes), F32),
+            pltpu.VMEM((rows // 2, lanes), F32),
+            pltpu.VMEM((width, rows), BF16),
+            pltpu.VMEM((width, 3 * lanes), F32),
+            pltpu.VMEM((width, lanes), F32),
+            dma((packs, 3)),
+            dma((packs, 3)),
+            dma((packs, 2)),
+            dma((packs, 2)),
+            dma(()),
+            dma((packs, 3)),
+            *scatter_scratch(packs, share, width),
+        ],
+        compiler_params=pltpu.CompilerParams(
+            collective_id=3, has_side_effects=True, vmem_limit_bytes=VMEM_LIMIT
+        ),
+        name="back",
+    )(offsets, slopes, dr1, weights, x_all, qkv, ctx)
+
+
 def per_device(
     hidden_in,
     cotangent,
@@ -525,126 +986,28 @@
     ln_first,
     ln_second,
 ):
-    wide_count = lax.axis_size("wide")
-    share = hidden_in.shape[0]
-    packs = hidden_in.shape[1]
     width = hidden_in.shape[2]
-    pack_len = share * wide_count
     slab_rows = master.shape[0]
     block = slab_rows // CAP
-    width_e = width // wide_count
-    width_f = FF // wide_count
-    heads_local = width_e // HD
-    scale = HD ** (-0.5)
     source, valid, target = owner_maps(owner_blocks, width, CAP, block)
     gathered = lax.all_gather(master.astype(jnp.bfloat16), "seq", axis=0, tiled=True)
     weights = jnp.take(gathered, target, axis=0)
-    w_qkv = weights[:, : 3 * width_e]
-    w_out = weights[:, 3 * width_e : 4 * width_e]
-    base = 4 * width_e
-    w_gate = weights[:, base : base + width_f]
-    w_up = weights[:, base + width_f : base + 2 * width_f]
-    w_down = weights[:, base + 2 * width_f : base + 3 * width_f]
-    head_ids = lax.axis_index("wide") * heads_local + jnp.arange(heads_local, dtype=jnp.int32)
-    slope = jnp.exp2(-8.0 * (head_ids.astype(jnp.float32) + 1.0) / H)
-    places = jnp.arange(pack_len, dtype=jnp.float32)
-    distance = jnp.abs(places[:, None] - places[None, :])
-    piece = lax.all_gather(hidden_in, "wide", axis=0, tiled=True)
-    tokens_all = piece
-    qkv = jnp.einsum("rpd,dc->rpc", piece, w_qkv, preferred_element_type=jnp.float32).astype(
-        jnp.bfloat16
-    )
-    masks = []
-    contexts = []
-    totals = []
-    for index in range(packs):
-        starts = jnp.repeat(seq_offsets[index], UNIT)
-        same = starts[:, None] == starts[None, :]
-        masks.append(same)
-        queries = qkv[:, index, :width_e].reshape(pack_len, heads_local, HD)
-        keys_all = qkv[:, index, width_e : 2 * width_e].reshape(pack_len, heads_local, HD)
-        values_all = qkv[:, index, 2 * width_e :].reshape(pack_len, heads_local, HD)
-        scores = scores_of(queries, keys_all, same, slope, distance, scale)
-        highest = jnp.max(scores, axis=-1, keepdims=True)
-        total = highest + jnp.log(jnp.sum(jnp.exp(scores - highest), axis=-1, keepdims=True))
-        probs = jnp.exp(scores - total)
-        context = jnp.einsum(
-            "hqk,khd->qhd",
-            probs.astype(jnp.bfloat16),
-            values_all,
-            preferred_element_type=jnp.float32,
-        )
-        contexts.append(context.reshape(pack_len, width_e).astype(jnp.bfloat16))
-        totals.append(total)
-    context_all = jnp.stack(contexts, axis=1)
-    piece = context_all
-    attn = lax.psum_scatter(
-        jnp.einsum("rpe,de->rpd", piece, w_out, preferred_element_type=jnp.float32).astype(
-            jnp.bfloat16
-        ),
-        "wide",
-        scatter_dimension=0,
-        tiled=True,
-    ).astype(jnp.float32)
-    tokens = hidden_in.astype(jnp.float32)
-    r1 = jnp.transpose(tokens + attn, (1, 0, 2))
+    slopes = jnp.exp2(-8.0 * (jnp.arange(H, dtype=jnp.float32) + 1.0) / H)
+    x = jnp.transpose(hidden_in, (1, 0, 2))
+    r1, x_all, qkv, ctx = attn_call(x, weights, seq_offsets, slopes)
     mixed_p, dr1_p, ffn_grads, ln_rows = ffn_call(
         r1, jnp.transpose(cotangent, (1, 0, 2)), weights, ln_params
     )
     mixed = jnp.transpose(mixed_p, (1, 0, 2))
-    grad_one = jnp.transpose(dr1_p, (1, 0, 2))
 
     def to_owner(grads):
         return jnp.where(valid[:, None], jnp.take(grads, source, axis=0), 0.0)
 
     ffn_owned = lax.psum_scatter(to_owner(ffn_grads), "seq", scatter_dimension=0, tiled=True)
-    piece = lax.all_gather(grad_one.astype(jnp.bfloat16), "wide", axis=0, tiled=True)
-    dattn_all = piece
-    dcontext = jnp.einsum("rpd,de->rpe", piece, w_out, preferred_element_type=jnp.float32).astype(
-        jnp.bfloat16
-    )
-    grad_out = jnp.einsum("rpd,rpe->de", dattn_all, context_all, preferred_element_type=jnp.float32)
-    pieces = []
-    for index in range(packs):
-        queries = qkv[:, index, :width_e].reshape(pack_len, heads_local, HD)
-        keys_all = qkv[:, index, width_e : 2 * width_e].reshape(pack_len, heads_local, HD)
-        values_all = qkv[:, index, 2 * width_e :].reshape(pack_len, heads_local, HD)
-        scores = scores_of(queries, keys_all, masks[index], slope, distance, scale)
-        probs = jnp.exp(scores - totals[index])
-        dctx = dcontext[:, index, :].reshape(pack_len, heads_local, HD)
-        dprobs = jnp.einsum("qhd,khd->hqk", dctx, values_all, preferred_element_type=jnp.float32)
-        dscaled = (
-            probs * (dprobs - jnp.sum(probs * dprobs, axis=-1, keepdims=True)) * scale
-        ).astype(jnp.bfloat16)
-        dqueries = jnp.einsum("hqk,khd->qhd", dscaled, keys_all, preferred_element_type=jnp.float32)
-        dkeys = jnp.einsum("hqk,qhd->khd", dscaled, queries, preferred_element_type=jnp.float32)
-        dvalues = jnp.einsum(
-            "hqk,qhd->khd", probs.astype(jnp.bfloat16), dctx, preferred_element_type=jnp.float32
-        )
-        pieces.append(
-            jnp.concatenate(
-                [
-                    dqueries.reshape(pack_len, width_e),
-                    dkeys.reshape(pack_len, width_e),
-                    dvalues.reshape(pack_len, width_e),
-                ],
-                axis=1,
-            ).astype(jnp.bfloat16)
-        )
-    d_qkv = jnp.stack(pieces, axis=1)
-    grad_qkv = jnp.einsum("rpd,rpc->dc", tokens_all, d_qkv, preferred_element_type=jnp.float32)
-    piece = d_qkv
-    input_grad = grad_one + lax.psum_scatter(
-        jnp.einsum("rpc,dc->rpd", piece, w_qkv, preferred_element_type=jnp.float32).astype(
-            jnp.bfloat16
-        ),
-        "wide",
-        scatter_dimension=0,
-        tiled=True,
-    ).astype(jnp.float32)
-    attn_grads = jnp.concatenate([grad_qkv, grad_out], axis=1)
+    grad_p, attn_grads = back_call(dr1_p, weights, x_all, qkv, ctx, seq_offsets, slopes)
+    input_grad = jnp.transpose(grad_p, (1, 0, 2))
     attn_owned = lax.psum_scatter(to_owner(attn_grads), "seq", scatter_dimension=0, tiled=True)
-    owned = jnp.concatenate([attn_owned, ffn_owned], axis=1)
+    owned = jnp.concatenate([attn_owned, ffn_owned], axis=1).astype(jnp.float32)
     ln_grads = ln_rows[:4]
     squares, ln_total = lax.psum((jnp.sum(owned * owned), ln_grads), ("seq", "wide"))
     grad_norm = jnp.sqrt(squares + jnp.sum(ln_total * ln_total))

time: 816 us -> 727 us (0.89)
  matrix products: 217 us -> 0 us
  Pallas kernels: 114 us -> 272 us
  other arithmetic: 75.2 us -> 31.2 us
  waiting for transfers between devices: 303 us -> 323 us
    dot_general x24 -> x0, matrix products: 217 us -> none  [the longest x3 60.4 us: per_device(): jnp.einsum('hqk,qhd->khd', dscaled, queries, preferred_element_type=jnp.f...]
    pallas_call x0 -> x2, Pallas kernels: none -> 159 us  [the longest x1 91.1 us: back_call(): pl.pallas_call(back_kernel, out_shape=(jax.ShapeDtypeStruct((packs, share...]
    reduce_scatter x1, waiting for transfers between devices: 0.02 us -> 132 us  [per_device(): lax.psum_scatter(to_owner(ffn_grads), 'seq', scatter_dimension=0, tiled=T...]
    reduce_scatter x2 -> x0, waiting for transfers between devices: 53.1 us -> none  [the longest x1 47.9 us: per_device(): lax.psum_scatter(jnp.einsum('rpe,de->rpd', piece, w_out, preferred_elemen...]
    reduce_scatter x1, waiting for transfers between devices: 86.4 us -> 51.2 us  [per_device(): lax.psum_scatter(to_owner(attn_grads), 'seq', scatter_dimension=0, tiled=...]
    all_gather x2 -> x0, waiting for transfers between devices: 31.4 us -> none  [the longest x1 17.5 us: per_device(): piece = lax.all_gather(hidden_in, 'wide', axis=0, tiled=True)]
    reduce_sum x3 -> x0, other arithmetic: 16 us -> none  [per_device(): jnp.sum(jnp.exp(scores - highest), axis=-1, keepdims=True)]
    all_gather x1, waiting for transfers between devices: 131 us -> 139 us  [per_device(): lax.all_gather(master.astype(jnp.bfloat16), 'seq', axis=0, tiled=True)]
  transfers between devices with their start and end apart: 7 -> 3, of which waited for: 6 -> 3; matrix products, arithmetic and copies ran while one was open for 30% -> 2% of each run, Pallas kernels for 0% -> 0%
where the time goes in v2:
time: 727 us; the launch traced here: 717 us
  waiting for transfers between devices  323 us (44%)
  Pallas kernels  272 us (37%)
  blocking collectives  39.6 us (5%)
  local copies, waits for them, and re-layouts  33.9 us (5%)
  other arithmetic  31.2 us (4%)
  between operations  16.8 us (2%)
    all_gather x1, waiting for transfers between devices, per_device(): lax.all_gather(master.astype(jnp.bfloat16), 'seq', axis=0, tiled=True)  139 us
    reduce_scatter x1, waiting for transfers between devices, per_device(): lax.psum_scatter(to_owner(ffn_grads), 'seq', scatter_dimension=0, tiled=T...  132 us
    pallas_call x1, Pallas kernels, ffn_call(): pl.pallas_call(ffn_kernel, out_shape=(jax.ShapeDtypeStruct((packs, share,...  114 us
    pallas_call x1, Pallas kernels, back_call(): pl.pallas_call(back_kernel, out_shape=(jax.ShapeDtypeStruct((packs, share...  91.1 us
    pallas_call x1, Pallas kernels, attn_call(): pl.pallas_call(attn_kernel, out_shape=(jax.ShapeDtypeStruct((packs, share...  67.6 us
    reduce_scatter x1, waiting for transfers between devices, per_device(): lax.psum_scatter(to_owner(attn_grads), 'seq', scatter_dimension=0, tiled=...  51.2 us
    psum x1, blocking collectives, per_device(): lax.psum((jnp.sum(owned * owned), ln_grads), ('seq', 'wide'))  39.6 us
    gather x2, local copies, waits for them, and re-layouts, to_owner(): return jnp.where(valid[:, None], jnp.take(grads, source, axis=0), 0.0)  15.4 us
  transfers between devices with their start and end apart: 3, of which 3 were waited for; matrix products, arithmetic and copies ran while one was open for 2% of the time, Pallas kernels for 0%

profile of v2, /device:TPU:0, one launch (start us, length us, event | category | flops | bytes accessed | tf_op | source)
XLA Modules:
  0.0 716.7 jit_solution(10970018049564388785)
XLA Ops:
  7.2 0.0 copy-start.8
  7.2 0.0 all-gather.2.cloned.1.call-start
  7.2 2.8 convert_element_type.14
  10.1 0.0 all-gather.2.cloned.1.call-update
  10.1 0.0 reduce-scatter.3.cloned.1.call-start
  10.2 0.0 copy-done.8
  10.2 0.2 reduce-window.8
  10.3 0.6 fusion.22
  11.0 0.1 multiply_add_fusion.1
  11.1 0.1 select_n.171
  11.1 0.1 add.233
  11.2 0.1 broadcast_compare_fusion
  11.3 0.1 lt.103
  11.4 0.1 convert_reduce_fusion
  11.5 0.1 select_reduce_fusion
  11.6 0.5 multiply_exponential_fusion.slopes_ref
  12.2 139.4 %all-gather.2.cloned.1.call-done = bf16[1536,3072]{1,0:T(8,128)(2,1)} async-done(((bf16[192,3072]{1,0:T(8,128)(2,1)}), bf16[1536,3072]{1,0:T(8,128)(2,1)}) %all-gather.2.cloned.1.call-update) | async-done | bytes 9437200 | tf_op jit(solution)/shard_map/all_gather | solution.py:993
  151.6 14.7 %gather_fusion = bf16[768,3072]{1,0:T(8,128)(2,1)} fusion(bf16[1536,3072]{1,0:T(8,128)(2,1)} %all-gather.2.cloned.1.call-done, s32[1024]{0:T(1024)S(1)} %pad_clamp_fusion.1), kind=kCustom, calls=%fused_computation | custom fusion | bytes 9440256 | tf_op jit(solution)/shard_map/jit(_take)/gather | solution.py:994
  166.2 5.1 broadcast_select_fusion.w_ref
  171.3 67.6 %attn.1 = (f32[3,256,768]{2,1,0:T(8,128)}, bf16[3,1024,768]{2,1,0:T(8,128)(2,1)}, bf16[3,1024,768]{2,1,0:T(8,128)(2,1)}, bf16[3,1024,256]{2,1,0:T(8,128)(2,1)}) custom-call(s32[3,8]{1,0:T(4,128)} %offsets_ref.3, f32[12]{0:T(128)} %multiply_exponential_fusion.slopes_ref, bf16[3,256,768]{2,1,0:T(8,128)(2,1)} %bitcast.10, ...), custom_call_target="tpu_custom_call" | custom-call | tf_op jit(solution)/shard_map/attn/pallas_call | solution.py:893
  238.9 113.6 %ffn.1 = (bf16[3,256,768]{2,1,0:T(8,128)(2,1)}, f32[3,256,768]{2,1,0:T(8,128)}, bf16[768,2304]{1,0:T(8,128)(2,1)}, f32[8,768]{1,0:T(8,128)}) custom-call(f32[3,256,768]{2,1,0:T(8,128)} %get-tuple-element.19.r1_ref, bf16[3,256,768]{2,1,0:T(8,128)(2,1)} %bitcast.8, bf16[768,3072]{1,0:T(8,128)(2,1)} %broadcast_select_fusion.w_ref, f32[4,768]{1,0:T(4,128)} %ln_ref.1), custom_call_target="tpu_custom_call" | custom-call | tf_op jit(solution)/shard_map/ffn/pallas_call | solution.py:450
  352.5 91.1 %back.1 = (f32[3,256,768]{2,1,0:T(8,128)}, bf16[768,768]{1,0:T(8,128)(2,1)}) custom-call(s32[3,8]{1,0:T(4,128)} %offsets_ref.3, f32[12]{0:T(128)} %multiply_exponential_fusion.slopes_ref, f32[3,256,768]{2,1,0:T(8,128)} %get-tuple-element.21.dr1_ref, bf16[768,3072]{1,0:T(8,128)(2,1)} %broadcast_select_fusion.w_ref, ...), custom_call_target="tpu_custom_call" | custom-call | tf_op jit(solution)/shard_map/back/pallas_call | solution.py:936
  443.6 8.1 %gather_fusion.1 = bf16[1536,768]{1,0:T(8,128)(2,1)} fusion(bf16[768,768]{1,0:T(8,128)(2,1)} %get-tuple-element.26, s32[2048]{0:T(1024)S(1)} %pad_clamp_fusion), kind=kCustom, calls=%fused_computation.1 | custom fusion | bytes 4724736 | tf_op jit(solution)/shard_map/jit(_take)/gather | solution.py:1004
  451.7 3.6 select_select_fusion.1
  455.3 0.0 reduce-scatter.3.cloned.1.call-update
  455.3 0.0 reduce-scatter.5.cloned.1.call-start
  455.4 0.0 copy-done
  455.4 7.3 %gather_fusion.2 = bf16[1536,2304]{1,0:T(8,128)(2,1)} fusion(bf16[768,2304]{1,0:T(8,128)(2,1)S(1)} %copy-done, s32[2048]{0:T(1024)S(1)} %pad_clamp_fusion), kind=kCustom, calls=%fused_computation.2 | custom fusion | bytes 14161920 | tf_op jit(solution)/shard_map/jit(_take)/gather | solution.py:1004
  462.7 6.9 select_select_fusion
  469.6 0.0 copy-start.1
  469.6 0.0 reduce-scatter.5.cloned.1.call-update
  469.7 0.8 broadcast_compare_fusion.1
  470.5 0.0 copy-done.7
  470.5 51.2 %reduce-scatter.3.cloned.1.call-done = bf16[192,768]{1,0:T(8,128)(2,1)} async-done(((bf16[1536,768]{1,0:T(8,128)(2,1)}), bf16[192,768]{1,0:T(8,128)(2,1)}) %reduce-scatter.3.cloned.1.call-update) | async-done | bytes 294928 | tf_op jit(solution)/shard_map/reduce_scatter | solution.py:1009
  521.7 132.2 %reduce-scatter.5.cloned.1.call-done = bf16[192,2304]{1,0:T(8,128)(2,1)} async-done(((bf16[1536,2304]{1,0:T(8,128)(2,1)}), bf16[192,2304]{1,0:T(8,128)(2,1)}) %reduce-scatter.5.cloned.1.call-update) | async-done | bytes 884752 | tf_op jit(solution)/shard_map/reduce_scatter | solution.py:1006
  653.9 2.4 fusion.2
  656.3 39.6 %all-reduce = (f32[]{:T(128)}, f32[4,768]{1,0:T(4,128)S(1)}) all-reduce(f32[]{:T(128)} %fusion.2, f32[4,768]{1,0:T(4,128)S(1)} %slice.3), channel_id=1, replica_groups=mesh['seq'=8,'wide'=4] {'seq','wide'}, use_global_device_ids=true, to_apply=%region_7.8 | all-reduce | flops 3073 | bytes 24584 | tf_op jit(solution)/shard_map/psum | solution.py:1012
  695.9 0.6 multiply_reduce_fusion
  697.9 0.0 copy-done.4
  697.9 0.0 copy-done.5
  697.9 0.0 copy-done.6
  697.9 0.6 multiply_subtract_fusion
  698.5 0.0 copy-done.1
  698.5 6.6 broadcast_select_fusion.1
  705.1 0.0 copy-done.3
  705.1 1.0 copy.21
  706.2 1.1 copy-done.2
  707.2 1.4 copy.22
  (17 shorter events, 0.1 us)
Async XLA Ops:
  7.2 3.0 copy-start.8
  7.2 144.4 %all-gather.2.cloned.1.call-start = ((), (), s32[]{:S(2)}) async-start(), calls=%async_computation.2 | async-start | bytes 10616832 | tf_op jit(solution)/shard_map/all_gather | solution.py:993
  10.1 511.6 %reduce-scatter.3.cloned.1.call-start = ((), (), s32[]{:S(2)}) async-start(), calls=%async_computation.3 | async-start | bytes 2654208 | tf_op jit(solution)/shard_map/reduce_scatter | solution.py:1009
  451.7 3.7 copy-start
  455.3 198.5 %reduce-scatter.5.cloned.1.call-start = ((), (), s32[]{:S(2)}) async-start(), calls=%async_computation.4 | async-start | bytes 7962624 | tf_op jit(solution)/shard_map/reduce_scatter | solution.py:1006
  469.6 0.9 copy-start.7
  469.6 228.2 %copy-start.4 = (f32[4,768]{1,0:T(4,128)S(1)}, f32[4,768]{1,0:T(4,128)}, u32[]{:S(2)}) copy-start(f32[4,768]{1,0:T(4,128)} %ln_ref.1) | copy-start | bytes 36868
  469.6 228.3 %copy-start.5 = (f32[4,768]{1,0:T(4,128)S(1)}, f32[4,768]{1,0:T(4,128)}, u32[]{:S(2)}) copy-start(f32[4,768]{1,0:T(4,128)} %param.18) | copy-start | bytes 36868
  469.6 228.3 %copy-start.6 = (f32[4,768]{1,0:T(4,128)S(1)}, f32[4,768]{1,0:T(4,128)}, u32[]{:S(2)}) copy-start(f32[4,768]{1,0:T(4,128)} %param.19) | copy-start | bytes 36868
  469.6 228.9 %copy-start.1 = (f32[192,3072]{1,0:T(8,128)S(1)}, f32[192,3072]{1,0:T(8,128)}, u32[]{:S(2)}) copy-start(f32[192,3072]{1,0:T(8,128)} %param.14) | copy-start | bytes 7077892
  698.5 6.6 copy-start.3
  705.1 2.1 copy-start.2
Sparse Core Ops, SparseCore 0:
  10.8 140.7 all-gather.1
  455.4 66.2 reduce-scatter.2
  525.4 128.4 reduce-scatter.4

commit v3 on v2

--- a/solution.py
+++ b/solution.py
@@ -1,3 +1,5 @@
+import functools
+
 import jax
 import jax.numpy as jnp
 from jax import lax
@@ -84,13 +86,13 @@
     pl.semaphore_wait(barrier, 2)
 
 
-def remote(source, target, send, recv, peer):
+def remote(source, target, send, recv, peer, axis="wide"):
     return pltpu.make_async_remote_copy(
         src_ref=source,
         dst_ref=target,
         send_sem=send,
         recv_sem=recv,
-        device_id={"wide": peer},
+        device_id={axis: peer},
         device_id_type=MESH,
     )
 
@@ -443,7 +445,7 @@
 def ffn_call(r1, cot, weights, ln_params):
     packs, share, width = r1.shape
     rows = 4 * share
-    units = (weights.shape[1] - width) // 3
+    units = weights.shape[1] // 3
     vm = pl.BlockSpec(memory_space=pltpu.VMEM)
     hb = pl.BlockSpec(memory_space=pl.ANY)
     dma = pltpu.SemaphoreType.DMA
@@ -486,6 +488,7 @@
         compiler_params=pltpu.CompilerParams(
             collective_id=1, has_side_effects=True, vmem_limit_bytes=VMEM_LIMIT
         ),
+        cost_estimate=pl.CostEstimate(flops=int(70e9), bytes_accessed=4 * 10**7, transcendentals=10**7),
         name="ffn",
     )(r1, cot, weights, ln_params)
 
@@ -921,6 +924,7 @@
         compiler_params=pltpu.CompilerParams(
             collective_id=2, has_side_effects=True, vmem_limit_bytes=VMEM_LIMIT
         ),
+        cost_estimate=pl.CostEstimate(flops=int(14e9), bytes_accessed=4 * 10**7, transcendentals=10**7),
         name="attn",
     )(offsets, slopes, x, weights)
 
@@ -970,8 +974,305 @@
         compiler_params=pltpu.CompilerParams(
             collective_id=3, has_side_effects=True, vmem_limit_bytes=VMEM_LIMIT
         ),
+        cost_estimate=pl.CostEstimate(flops=int(40e9), bytes_accessed=4 * 10**7, transcendentals=10**7),
         name="back",
     )(offsets, slopes, dr1, weights, x_all, qkv, ctx)
+
+
+class OwnerSum:
+    def __init__(self, source, sums, beside, along, load, send, recv, chunk):
+        self.source, self.sums, self.beside, self.along = source, sums, beside, along
+        self.load, self.send, self.recv, self.chunk = load, send, recv, chunk
+        seq = lax.axis_index("seq")
+        self.line = sums.shape[0]
+        self.x = lax.rem(seq, 2)
+        self.z = seq // 2
+
+    def chunks(self):
+        return self.sums.shape[2] // self.chunk
+
+    def cols(self, index):
+        return pl.ds(index * self.chunk, self.chunk)
+
+    def peers(self):
+        found = [2 * self.z + 1 - self.x]
+        for step in range(1, self.line):
+            found.append(2 * lax.rem(self.z + step, self.line) + self.x)
+        return found
+
+    def own_load(self):
+        return pltpu.make_async_copy(self.source.at[:, self.x], self.sums, self.load)
+
+    def cross(self, index):
+        return remote(
+            self.source.at[:, 1 - self.x, :, self.cols(index)],
+            self.beside.at[index],
+            self.send.at[index, 0],
+            self.recv.at[index, 0],
+            2 * self.z + 1 - self.x,
+            "seq",
+        )
+
+    def hop(self, index, step):
+        other = lax.rem(self.z + step, self.line)
+        return remote(
+            self.sums.at[other, :, self.cols(index)],
+            self.along.at[index, step - 1],
+            self.send.at[index, step],
+            self.recv.at[index, step],
+            2 * other + self.x,
+            "seq",
+        )
+
+    def start(self):
+        self.own_load().start()
+        for index in range(self.chunks()):
+            self.cross(index).start()
+
+    def add(self, index):
+        if index == 0:
+            self.own_load().wait()
+        self.cross(index).wait_recv()
+        cols = self.cols(index)
+        for other in range(self.line):
+
+            def part(row, other=other):
+                rws = tile(row, 32)
+                value = self.sums[other, rws, cols].astype(F32) + self.beside[index, other, rws, :].astype(F32)
+                self.sums[other, rws, cols] = value.astype(BF16)
+
+            loop(self.sums.shape[1] // 32, part)
+        for step in range(1, self.line):
+            self.hop(index, step).start()
+
+    def finish(self, index, target):
+        for step in range(1, self.line):
+            self.hop(index, step).wait_recv()
+        cols = self.cols(index)
+
+        def part(row):
+            rws = tile(row, 32)
+            value = self.sums[self.z, rws, cols].astype(F32)
+            for step in range(1, self.line):
+                value = value + self.along[index, step - 1, rws, :].astype(F32)
+            target(rws, cols, value)
+
+        loop(self.sums.shape[1] // 32, part)
+
+    def drain(self):
+        for index in range(self.chunks()):
+            self.cross(index).wait_send()
+            for step in range(1, self.line):
+                self.hop(index, step).wait_send()
+
+
+def owner_scratch(line, slab, width, chunk):
+    count = width // chunk
+    dma = pltpu.SemaphoreType.DMA
+    return [
+        pltpu.VMEM((line, slab, width), BF16),
+        pltpu.VMEM((count, line, slab, chunk), BF16),
+        pltpu.VMEM((count, line - 1, slab, chunk), BF16),
+        dma(()),
+        dma((count, line)),
+        dma((count, line)),
+    ]
+
+
+class Total:
+    def __init__(self, axis, slots, send, recv):
+        self.axis, self.slots, self.send, self.recv = axis, slots, send, recv
+        self.count = slots.shape[0]
+        self.place = lax.axis_index(axis)
+
+    def copy(self, step):
+        mine = self.slots.at[self.place]
+        return remote(
+            mine, mine, self.send.at[step - 1], self.recv.at[self.place], self.peer(step), self.axis
+        )
+
+    def peer(self, step):
+        return lax.rem(self.place + step, self.count)
+
+    def start(self, value):
+        self.slots[self.place] = value
+        for step in range(1, self.count):
+            self.copy(step).start()
+
+    def finish(self):
+        for step in range(1, self.count):
+            other = self.peer(step)
+            slot = self.slots.at[other]
+            remote(
+                slot, slot, self.send.at[step - 1], self.recv.at[other], other, self.axis
+            ).wait_recv()
+        value = self.slots[0]
+        for place in range(1, self.count):
+            value = value + self.slots[place]
+        return value
+
+    def drain(self):
+        for step in range(1, self.count):
+            self.copy(step).wait_send()
+
+
+def total_scratch(count, shape):
+    dma = pltpu.SemaphoreType.DMA
+    return [pltpu.VMEM((count, *shape), F32), dma((count - 1,)), dma((count,))]
+
+
+def greet_all(axes):
+    barrier = pltpu.get_barrier_semaphore()
+    sent = 0
+    for axis, count in axes:
+        place = lax.axis_index(axis)
+        for step in range(1, count):
+            peer = lax.rem(place + step, count)
+            pl.semaphore_signal(barrier, inc=1, device_id={axis: peer}, device_id_type=MESH)
+            sent += 1
+    pl.semaphore_wait(barrier, sent)
+
+
+def close_kernel(
+    seq_count,
+    wide_count,
+    kept_ref,
+    grads_ref,
+    ffn_ref,
+    ln_ref,
+    owned_ref,
+    ln_out_ref,
+    square_ref,
+    *scratch,
+):
+    greet_all((("seq", seq_count), ("wide", wide_count)))
+    owners = OwnerSum(grads_ref, *scratch[:6], 256)
+    norms = [Total("wide", *scratch[6:9]), Total("seq", *scratch[9:12])]
+    squares = [Total("wide", *scratch[12:15]), Total("seq", *scratch[15:18])]
+    acc = scratch[18]
+    slab = owned_ref.shape[0]
+    width = grads_ref.shape[3]
+    owners.start()
+    norms[0].start(ln_ref[...])
+    acc[...] = jnp.zeros_like(acc)
+
+    def keep(rws, value):
+        row = lax.broadcasted_iota(jnp.int32, value.shape, 0) + rws.start
+        return jnp.where(row < kept_ref[0], value, 0.0)
+
+    def note(value):
+        square = value * value
+        for place in range(value.shape[1] // 128):
+            part = square[:, place * 128 : (place + 1) * 128]
+            for row in range(0, value.shape[0], 8):
+                acc[...] += part[row : row + 8]
+
+    def put(rws, cols, value):
+        value = keep(rws, value)
+        owned_ref[rws, cols] = value
+        note(value)
+
+    def from_ffn(index):
+        rws = tile(index, 8)
+        value = keep(rws, ffn_ref[rws, :].astype(F32))
+        owned_ref[rws, pl.ds(width, ffn_ref.shape[1])] = value
+        note(value)
+
+    for index in range(owners.chunks()):
+        owners.add(index)
+    norms[1].start(norms[0].finish())
+    loop(slab // 8, from_ffn)
+    for index in range(owners.chunks()):
+        owners.finish(index, put)
+    squares[0].start(acc[...])
+    squares[1].start(squares[0].finish())
+    ln_out_ref[...] = norms[1].finish()
+    square_ref[...] = squares[1].finish()
+    owners.drain()
+    for part in (*norms, *squares):
+        part.drain()
+
+
+def close_call(kept, grads, ffn_owned, ln_rows, seq_count, wide_count):
+    slab = ffn_owned.shape[0]
+    width = grads.shape[1]
+    line = seq_count // 2
+    vm = pl.BlockSpec(memory_space=pltpu.VMEM)
+    sm = pl.BlockSpec(memory_space=pltpu.SMEM)
+    return pl.pallas_call(
+        functools.partial(close_kernel, seq_count, wide_count),
+        out_shape=(
+            jax.ShapeDtypeStruct((slab, width + ffn_owned.shape[1]), F32),
+            jax.ShapeDtypeStruct(ln_rows.shape, F32),
+            jax.ShapeDtypeStruct((8, 128), F32),
+        ),
+        in_specs=[sm, pl.BlockSpec(memory_space=pl.ANY), vm, vm],
+        out_specs=(vm, vm, vm),
+        scratch_shapes=[
+            *owner_scratch(line, slab, width, 256),
+            *total_scratch(wide_count, ln_rows.shape),
+            *total_scratch(seq_count, ln_rows.shape),
+            *total_scratch(wide_count, (8, 128)),
+            *total_scratch(seq_count, (8, 128)),
+            pltpu.VMEM((8, 128), F32),
+        ],
+        compiler_params=pltpu.CompilerParams(
+            collective_id=4, has_side_effects=True, vmem_limit_bytes=VMEM_LIMIT
+        ),
+        name="close",
+    )(kept, grads.reshape(line, 2, slab, width), ffn_owned, ln_rows)
+
+
+def pick_kernel(block, places_ref, source_ref, target_ref, held, sems, sem):
+    count = places_ref.shape[1]
+
+    def copy(index):
+        return pltpu.make_async_copy(
+            source_ref.at[pl.ds(pl.multiple_of(places_ref[0, index] * block, block), block)],
+            held.at[pl.ds(pl.multiple_of(index * block, block), block)],
+            sems.at[index],
+        )
+
+    loop(count, lambda index: copy(index).start())
+    loop(count, lambda index: copy(index).wait())
+    out = pltpu.make_async_copy(held, target_ref, sem)
+    out.start()
+    out.wait()
+
+
+def spread_kernel(block, places_ref, source_ref, target_ref, held, sems, sem):
+    count = places_ref.shape[1]
+    load = pltpu.make_async_copy(source_ref, held, sem)
+    load.start()
+    load.wait()
+
+    def copy(index):
+        return pltpu.make_async_copy(
+            held.at[pl.ds(pl.multiple_of(index * block, block), block)],
+            target_ref.at[pl.ds(pl.multiple_of(places_ref[1, index] * block, block), block)],
+            sems.at[index],
+        )
+
+    loop(count, lambda index: copy(index).start())
+    loop(count, lambda index: copy(index).wait())
+
+
+def move_blocks(kernel, source, places, rows, block):
+    hb = pl.BlockSpec(memory_space=pl.ANY)
+    count = places.shape[1]
+    return pl.pallas_call(
+        functools.partial(kernel, block),
+        out_shape=jax.ShapeDtypeStruct((rows, source.shape[1]), source.dtype),
+        in_specs=[pl.BlockSpec(memory_space=pltpu.SMEM), hb],
+        out_specs=hb,
+        scratch_shapes=[
+            pltpu.VMEM((count * block, source.shape[1]), source.dtype),
+            pltpu.SemaphoreType.DMA((count,)),
+            pltpu.SemaphoreType.DMA(()),
+        ],
+        compiler_params=pltpu.CompilerParams(vmem_limit_bytes=VMEM_LIMIT),
+        name="move",
+    )(places, source)
 
 
 def per_device(
@@ -990,32 +1291,56 @@
     slab_rows = master.shape[0]
     block = slab_rows // CAP
     source, valid, target = owner_maps(owner_blocks, width, CAP, block)
-    gathered = lax.all_gather(master.astype(jnp.bfloat16), "seq", axis=0, tiled=True)
-    weights = jnp.take(gathered, target, axis=0)
+    low = master.astype(jnp.bfloat16)
+    first = lax.all_gather(low[:, :width], "seq", axis=0, tiled=True)
+    rest = lax.all_gather(low[:, width:], "seq", axis=0, tiled=True)
+    gathered_rows = slab_rows * lax.axis_size("seq")
+    count = width // block
+    fits = block % 16 == 0
+    slots = target[::block] // block
+    both = jnp.stack([slots, slots])
+
+    def to_order(array):
+        if fits:
+            return move_blocks(pick_kernel, array, both, width, block)
+        return jnp.take(array, target, axis=0)
+
+    def to_owner(grads):
+        if fits:
+            return move_blocks(spread_kernel, grads, both, gathered_rows, block)
+        return jnp.take(grads, source, axis=0)
+
+    weights = to_order(first)
+    w_ffn = to_order(rest)
     slopes = jnp.exp2(-8.0 * (jnp.arange(H, dtype=jnp.float32) + 1.0) / H)
     x = jnp.transpose(hidden_in, (1, 0, 2))
     r1, x_all, qkv, ctx = attn_call(x, weights, seq_offsets, slopes)
     mixed_p, dr1_p, ffn_grads, ln_rows = ffn_call(
-        r1, jnp.transpose(cotangent, (1, 0, 2)), weights, ln_params
+        r1, jnp.transpose(cotangent, (1, 0, 2)), w_ffn, ln_params
     )
     mixed = jnp.transpose(mixed_p, (1, 0, 2))
 
-    def to_owner(grads):
-        return jnp.where(valid[:, None], jnp.take(grads, source, axis=0), 0.0)
-
-    ffn_owned = lax.psum_scatter(to_owner(ffn_grads), "seq", scatter_dimension=0, tiled=True)
+    ffn_padded, dr1_p = lax.optimization_barrier((to_owner(ffn_grads), dr1_p))
+    ffn_owned = lax.psum_scatter(ffn_padded, "seq", scatter_dimension=0, tiled=True)
     grad_p, attn_grads = back_call(dr1_p, weights, x_all, qkv, ctx, seq_offsets, slopes)
     input_grad = jnp.transpose(grad_p, (1, 0, 2))
-    attn_owned = lax.psum_scatter(to_owner(attn_grads), "seq", scatter_dimension=0, tiled=True)
-    owned = jnp.concatenate([attn_owned, ffn_owned], axis=1).astype(jnp.float32)
-    ln_grads = ln_rows[:4]
-    squares, ln_total = lax.psum((jnp.sum(owned * owned), ln_grads), ("seq", "wide"))
+    attn_padded = to_owner(attn_grads)
+    seq_count = lax.axis_size("seq")
+    mine = jnp.arange(seq_count, dtype=jnp.int32) == lax.axis_index("seq")
+    own_rows = jnp.sum(jnp.where(mine, owner_blocks, 0)) * block
+    kept = (jnp.arange(slab_rows, dtype=jnp.int32) < own_rows)[:, None]
+    if fits and seq_count == 8:
+        owned, ln_total, parts = close_call(
+            own_rows[None], attn_padded, ffn_owned, ln_rows, seq_count, lax.axis_size("wide")
+        )
+        squares, ln_total = jnp.sum(parts), ln_total[:4]
+    else:
+        attn_owned = lax.psum_scatter(attn_padded, "seq", scatter_dimension=0, tiled=True)
+        owned = jnp.concatenate([attn_owned, ffn_owned], axis=1).astype(jnp.float32)
+        owned = jnp.where(kept, owned, 0.0)
+        squares, ln_total = lax.psum((jnp.sum(owned * owned), ln_rows[:4]), ("seq", "wide"))
     grad_norm = jnp.sqrt(squares + jnp.sum(ln_total * ln_total))
     clip = jnp.minimum(1.0, 1.0 / (grad_norm + 1e-06))
-    seq_count = owner_blocks.shape[0]
-    mine = jnp.arange(seq_count, dtype=jnp.int32) == lax.axis_index("seq")
-    own_count = jnp.sum(jnp.where(mine, owner_blocks, 0))
-    kept = (jnp.arange(slab_rows, dtype=jnp.int32) // block < own_count)[:, None]
     param_new, first_new, second_new = adamw(
         master, owned * clip, first_moment, second_moment, DECAY, RATE
     )

time: 727 us -> 515 us (0.71)
  waiting for transfers between devices: 323 us -> 125 us
  Pallas kernels: 272 us -> 341 us
  blocking collectives: 39.6 us -> 0 us
  local copies, waits for them, and re-layouts: 33.9 us -> 5.35 us
  other arithmetic: 31.2 us -> 16.7 us
    reduce_scatter x2 -> x1, waiting for transfers between devices: 183 us -> 32.9 us  [per_device(): lax.psum_scatter(ffn_padded, 'seq', scatter_dimension=0, tiled=True)]
    pallas_call x0 -> x5, Pallas kernels: none -> 68.5 us  [the longest x1 52.7 us: close_call(): pl.pallas_call(functools.partial(close_kernel, seq_count, wide_count), ou...]
    all_gather x1 -> x2, waiting for transfers between devices: 139 us -> 91.7 us  [the longest x1 52.4 us: per_device(): first = lax.all_gather(low[:, :width], 'seq', axis=0, tiled=True)]
    psum x1 -> x0, blocking collectives: 39.6 us -> none  [per_device(): lax.psum((jnp.sum(owned * owned), ln_grads), ('seq', 'wide'))]
    gather x3 -> x0, local copies, waits for them, and re-layouts: 30.1 us -> none  [the longest x2 15.4 us: to_owner(): return jnp.where(valid[:, None], jnp.take(grads, source, axis=0), 0.0)]
    select_n x6 -> x0, other arithmetic: 15.6 us -> none  [the longest x3 10.5 us: to_owner(): return jnp.where(valid[:, None], jnp.take(grads, source, axis=0), 0.0)]
  transfers between devices with their start and end apart: 3 -> 3, of which waited for: 3 -> 3; matrix products, arithmetic and copies ran while one was open for 2% -> 1% of each run, Pallas kernels for 0% -> 32%
where the time goes in v3:
time: 515 us; the launch traced here: 505 us
  Pallas kernels  341 us (66%)
  waiting for transfers between devices  125 us (24%)
  between operations  17.3 us (3%)
  other arithmetic  16.7 us (3%)
  local copies, waits for them, and re-layouts  5.35 us (1%)
    pallas_call x1, Pallas kernels, ffn_call(): pl.pallas_call(ffn_kernel, out_shape=(jax.ShapeDtypeStruct((packs, share,...  115 us
    pallas_call x1, Pallas kernels, back_call(): pl.pallas_call(back_kernel, out_shape=(jax.ShapeDtypeStruct((packs, share...  89.6 us
    pallas_call x1, Pallas kernels, attn_call(): pl.pallas_call(attn_kernel, out_shape=(jax.ShapeDtypeStruct((packs, share...  67.6 us
    pallas_call x1, Pallas kernels, close_call(): pl.pallas_call(functools.partial(close_kernel, seq_count, wide_count), ou...  52.7 us
    all_gather x1, waiting for transfers between devices, per_device(): first = lax.all_gather(low[:, :width], 'seq', axis=0, tiled=True)  52.4 us
    all_gather x1, waiting for transfers between devices, per_device(): rest = lax.all_gather(low[:, width:], 'seq', axis=0, tiled=True)  39.3 us
    reduce_scatter x1, waiting for transfers between devices, per_device(): lax.psum_scatter(ffn_padded, 'seq', scatter_dimension=0, tiled=True)  32.9 us
    pallas_call x4, Pallas kernels, move_blocks(): pl.pallas_call(functools.partial(kernel, block), out_shape=jax.ShapeDtype...  15.8 us
  transfers between devices with their start and end apart: 3, of which 3 were waited for; matrix products, arithmetic and copies ran while one was open for 1% of the time, Pallas kernels for 32%

profile of v3, /device:TPU:0, one launch (start us, length us, event | category | flops | bytes accessed | tf_op | source)
XLA Modules:
  0.0 504.8 jit_solution(18387395076225410893)
XLA Ops:
  7.2 0.0 all-gather.3.cloned.1.call-start
  7.2 1.8 convert_element_type.7
  9.0 0.0 copy-start.6
  9.1 0.7 slice.16
  9.8 0.0 all-gather.3.cloned.1.call-update
  9.8 0.0 all-gather.5.cloned.1.call-start
  9.9 1.0 slice.17
  10.9 0.0 all-gather.5.cloned.1.call-update
  10.9 0.0 reduce-scatter.2.cloned.1.call-start
  10.9 0.0 copy-done.6
  10.9 0.2 reduce-window.8
  11.1 0.1 convert_reduce_fusion
  11.2 0.6 fusion.10
  11.8 0.1 select_reduce_fusion
  11.9 0.1 slice.12
  12.0 0.5 multiply_exponential_fusion.slopes_ref
  12.6 0.6 pad_add_fusion.places_ref
  13.2 52.4 %all-gather.3.cloned.1.call-done.source_ref = bf16[1536,768]{1,0:T(8,128)(2,1)} async-done(((bf16[192,768]{1,0:T(8,128)(2,1)}), bf16[1536,768]{1,0:T(8,128)(2,1)}) %all-gather.3.cloned.1.call-update) | async-done | bytes 2359312 | tf_op jit(solution)/shard_map/all_gather | solution.py:1295
  65.6 3.2 move.4.w_ref
  68.8 67.6 %attn.1 = (f32[3,256,768]{2,1,0:T(8,128)}, bf16[3,1024,768]{2,1,0:T(8,128)(2,1)}, bf16[3,1024,768]{2,1,0:T(8,128)(2,1)}, bf16[3,1024,256]{2,1,0:T(8,128)(2,1)}) custom-call(s32[3,8]{1,0:T(4,128)} %offsets_ref.3, f32[12]{0:T(128)} %multiply_exponential_fusion.slopes_ref, bf16[3,256,768]{2,1,0:T(8,128)(2,1)} %bitcast.16, bf16[768,768]{1,0:T(8,128)(2,1)} %move.4.w_ref), custom_call_target="tpu_custom_call" | custom-call | flops 14000000000 | bytes 40000000 | tf_op jit(solution)/shard_map/attn/pallas_call | solution.py:896
  136.4 39.3 %all-gather.5.cloned.1.call-done.source_ref = bf16[1536,2304]{1,0:T(8,128)(2,1)} async-done(((bf16[192,2304]{1,0:T(8,128)(2,1)}), bf16[1536,2304]{1,0:T(8,128)(2,1)}) %all-gather.5.cloned.1.call-update) | async-done | bytes 7077904 | tf_op jit(solution)/shard_map/all_gather | solution.py:1296
  175.7 4.8 move.5.w_ref
  180.5 114.9 %ffn.1 = (bf16[3,256,768]{2,1,0:T(8,128)(2,1)}, f32[3,256,768]{2,1,0:T(8,128)}, bf16[768,2304]{1,0:T(8,128)(2,1)}, f32[8,768]{1,0:T(8,128)}) custom-call(f32[3,256,768]{2,1,0:T(8,128)} %get-tuple-element.24.r1_ref, bf16[3,256,768]{2,1,0:T(8,128)(2,1)} %bitcast.17, bf16[768,2304]{1,0:T(8,128)(2,1)} %move.5.w_ref, f32[4,768]{1,0:T(4,128)} %ln_ref.1), custom_call_target="tpu_custom_call" | custom-call | flops 70000001024 | bytes 40000000 | tf_op jit(solution)/shard_map/ffn/pallas_call | solution.py:452
  295.4 4.7 move.6
  300.1 0.0 reduce-scatter.2.cloned.1.call-update
  300.8 89.6 %back.1 = (f32[3,256,768]{2,1,0:T(8,128)}, bf16[768,768]{1,0:T(8,128)(2,1)}) custom-call(s32[3,8]{1,0:T(4,128)} %offsets_ref.3, f32[12]{0:T(128)} %multiply_exponential_fusion.slopes_ref, f32[3,256,768]{2,1,0:T(8,128)} %get-tuple-element.28.dr1_ref, bf16[768,768]{1,0:T(8,128)(2,1)} %move.4.w_ref, bf16[3,1024,768]{2,1,0:T(8,128)(2,1)} %get-tuple-element.29.x_ref, ...), custom_call_target="tpu_custom_call" | custom-call | flops 40000000000 | bytes 40000000 | tf_op jit(solution)/shard_map/back/pallas_call | solution.py:940
  390.3 3.2 move.7
  393.5 0.0 copy-start.3
  393.5 0.0 copy-start.4
  393.5 0.0 copy-start.5
  393.6 0.0 copy-start
  393.6 32.9 %reduce-scatter.2.cloned.1.call-done.ffn_ref = bf16[192,2304]{1,0:T(8,128)(2,1)} async-done(((bf16[1536,2304]{1,0:T(8,128)(2,1)}), bf16[192,2304]{1,0:T(8,128)(2,1)}) %reduce-scatter.2.cloned.1.call-update) | async-done | bytes 884752 | tf_op jit(solution)/shard_map/reduce_scatter | solution.py:1324
  426.5 52.7 %close.1 = (f32[192,3072]{1,0:T(8,128)}, f32[8,768]{1,0:T(8,128)}, f32[8,128]{1,0:T(8,128)}) custom-call(s32[1]{0:T(128)} %bitcast.7.kept_ref, bf16[4,2,192,768]{3,2,1,0:T(8,128)(2,1)} %bitcast.11, bf16[192,2304]{1,0:T(8,128)(2,1)} %reduce-scatter.2.cloned.1.call-done.ffn_ref, f32[8,768]{1,0:T(8,128)} %get-tuple-element.35.ln_ref), custom_call_target="tpu_custom_call" | custom-call | tf_op jit(solution)/shard_map/close/pallas_call | solution.py:1202
  479.2 1.4 multiply_reduce_fusion
  480.6 1.3 reduce_sum.48
  483.2 0.0 copy-done.3
  483.3 0.0 copy-done.4
  483.3 0.0 copy-done.5
  483.3 1.4 multiply_subtract_fusion
  484.6 0.0 copy-done
  484.6 0.0 copy-start.2
  484.6 8.8 %broadcast_select_fusion = (f32[192,3072]{1,0:T(8,128)}, f32[192,3072]{1,0:T(8,128)}, f32[192,3072]{1,0:T(8,128)}) fusion(pred[192]{0:T(512)(128)(4,1)S(1)} %iota_compare_fusion.1, f32[192,3072]{1,0:T(8,128)} %get-tuple-element.36, f32[]{:T(128)S(6)} %min.3, f32[192,3072]{1,0:T(8,128)} %param.16, f32[192,3072]{1,0:T(8,128)S(1)} %copy-done, f32[192,3072]{1,0:T(8,128)} %param.15), kind=kLoop, calls=%fused_computation.4 | loop fusion | flops 11206656 | bytes 16515268 | tf_op jit(solution)/shard_map/jit(_where)/select_n | solution.py:1355
  493.5 0.0 copy-start.1
  493.5 0.0 copy-done.2
  493.5 1.0 copy.21
  494.5 1.1 copy-done.1
  495.6 1.4 copy.22
  (4 shorter events, 0.0 us)
Async XLA Ops:
  7.2 58.4 %all-gather.3.cloned.1.call-start = ((), (), s32[]{:S(2)}) async-start(), calls=%async_computation.1 | async-start | bytes 2654208 | tf_op jit(solution)/shard_map/all_gather | solution.py:1295
  9.0 1.9 copy-start.6
  9.8 165.9 %all-gather.5.cloned.1.call-start = ((), (), s32[]{:S(2)}) async-start(), calls=%async_computation.2 | async-start | bytes 7962624 | tf_op jit(solution)/shard_map/all_gather | solution.py:1296
  10.9 415.6 %reduce-scatter.2.cloned.1.call-start = ((), (), s32[]{:S(2)}) async-start(), calls=%async_computation.3 | async-start | bytes 7962624 | tf_op jit(solution)/shard_map/reduce_scatter | solution.py:1324
  393.5 89.7 %copy-start.3 = (f32[4,768]{1,0:T(4,128)S(1)}, f32[4,768]{1,0:T(4,128)}, u32[]{:S(2)}) copy-start(f32[4,768]{1,0:T(4,128)} %ln_ref.1) | copy-start | bytes 36868
  393.5 89.7 %copy-start.4 = (f32[4,768]{1,0:T(4,128)S(1)}, f32[4,768]{1,0:T(4,128)}, u32[]{:S(2)}) copy-start(f32[4,768]{1,0:T(4,128)} %param.18) | copy-start | bytes 36868
  393.5 89.7 %copy-start.5 = (f32[4,768]{1,0:T(4,128)S(1)}, f32[4,768]{1,0:T(4,128)}, u32[]{:S(2)}) copy-start(f32[4,768]{1,0:T(4,128)} %param.19) | copy-start | bytes 36868
  393.6 91.1 %copy-start = (f32[192,3072]{1,0:T(8,128)S(1)}, f32[192,3072]{1,0:T(8,128)}, u32[]{:S(2)}) copy-start(f32[192,3072]{1,0:T(8,128)} %param.14) | copy-start | bytes 7077892
  484.6 8.8 %copy-start.2 = (bf16[3,256,768]{2,1,0:T(8,128)(2,1)S(1)}, bf16[3,256,768]{2,1,0:T(8,128)(2,1)}, u32[]{:S(2)}) copy-start(bf16[3,256,768]{2,1,0:T(8,128)(2,1)} %get-tuple-element.25) | copy-start | bytes 3538948
  493.5 2.1 copy-start.1
Sparse Core Ops, SparseCore 0:
  10.8 54.7 all-gather.2
  68.3 107.3 all-gather.4
  300.2 126.2 reduce-scatter.1

commit v4 on v3

--- a/solution.py
+++ b/solution.py
@@ -30,6 +30,9 @@
 F32 = jnp.float32
 BF16 = jnp.bfloat16
 NEG = -1e30
+OWNER_CHUNKS = 6
+PAIRS = 4
+SINGLES = 2
 VMEM_LIMIT = 60 * 2**20
 
 
@@ -573,20 +576,33 @@
     loop(width // 128, part)
 
 
+def mask_row(runs, index):
+    return jnp.concatenate([jnp.full((1, UNIT), part, F32) for part in runs.masks(index)], axis=1)
+
+
+def split_heads(value, low):
+    none = jnp.zeros_like(value)
+    return jnp.concatenate([jnp.where(low, value, none), jnp.where(low, none, value)], axis=0)
+
+
 def head_lanes():
     lane = lax.broadcasted_iota(jnp.int32, (1, 128), 1)
     return lane < HD
 
 
 def attn_kernel(
+    gathering,
     offsets_ref,
     slopes_ref,
+    slots_ref,
     x_ref,
     w_ref,
     r1_ref,
     held_ref,
     qkv_ref,
     ctx_ref,
+    w_qkv_ref,
+    w_out_ref,
     packed,
     w_qkv,
     w_out,
@@ -608,10 +624,20 @@
     rows = 4 * share
     lanes = w_out.shape[1]
     group = rows // 2
-    load = pltpu.make_async_copy(w_ref.at[:, pl.ds(0, packed.shape[1])], packed, load_sem)
-    load.start()
     wide, core, row, mate, across = places()
-    greet(mate, across)
+    if gathering:
+        slabs, slab, send_w, recv_w, *buffers = buffers
+        load = pltpu.make_async_copy(w_ref.at[:, pl.ds(0, slab.shape[1])], slab, load_sem)
+        load.start()
+        owners = OwnerGather(slabs, send_w, recv_w, slab.shape[0], send_w.shape[2])
+        greet_all((("seq", 2 * owners.line), ("wide", 4)))
+        load.wait()
+        slabs[owners.mine(), :] = slab[...].astype(BF16)
+        owners.start()
+    else:
+        load = pltpu.make_async_copy(w_ref.at[:, pl.ds(0, packed.shape[1])], packed, load_sem)
+        load.start()
+        greet(mate, across)
     gather = Gather(held, send_a, recv_a, share)
     scatter = Scatter(*buffers, send_b, recv_b, share)
     base = pl.multiple_of((core * 2 + row) * share, share)
@@ -619,10 +645,21 @@
         held[pack, pl.ds(base, share), :] = x_ref[pack]
         gather.start(pack)
     fill_bias(bias, slopes_ref, wide)
-    load.wait()
+    if gathering:
+        owners.pass_on()
+        owners.finish()
+        order_slabs(slots_ref, slabs, packed, 2 * owners.line)
+    else:
+        load.wait()
     split_weights(packed, w_qkv, w_out)
     low = head_lanes()
-    stores = []
+    scale = jnp.asarray(HD ** (-0.5), BF16)
+    stores = [
+        pltpu.make_async_copy(w_qkv, w_qkv_ref, store_sem.at[packs, 0]),
+        pltpu.make_async_copy(w_out, w_out_ref, store_sem.at[packs, 1]),
+    ]
+    for copy in stores:
+        copy.start()
 
     def attend(pack):
         runs = Runs(offsets_ref, pack)
@@ -630,38 +667,45 @@
 
         def project(index):
             rws = tile(index, 256)
-            plain[rws, :] = dot_nn(held[pack, rws, :], w_qkv[...]).astype(BF16)
+            value = dot_nn(held[pack, rws, :], w_qkv[...])
+            plain[rws, pl.ds(0, lanes)] = (value[:, :lanes].astype(BF16) * scale).astype(BF16)
+            plain[rws, pl.ds(lanes, 2 * lanes)] = value[:, lanes:].astype(BF16)
 
         loop(rows // 256, project)
         runs.arrange(plain, writer(qkv, pack))
         for side in range(2):
             keys = pl.ds(side * group, group)
 
-            def chunk(index, side=side, keys=keys, pack=pack):
+            def weigh(part, queries, offset, side=side, keys=keys, pack=pack):
+                scores = dot_nt(queries, qkv[pack, keys, pl.ds(lanes + part * 128, 128)]) + offset
+                powers = jnp.exp(scores - jnp.max(scores, axis=-1, keepdims=True))
+                total = jnp.sum(powers, axis=-1, keepdims=True)
+                return dot_nn(powers.astype(BF16), qkv[pack, keys, pl.ds(2 * lanes + part * 128, 128)]) / total
+
+            def pair(index, side=side, pack=pack):
                 rws = pl.ds(pl.multiple_of(side * group + index * UNIT, UNIT), UNIT)
+                offset = jnp.concatenate([bias[head, tile(index, UNIT), :] for head in range(2)], axis=0)
                 if side:
-                    mask = jnp.concatenate(
-                        [jnp.full((1, UNIT), part, F32) for part in runs.masks(index)], axis=1
+                    offset = offset + mask_row(runs, index)
+                out = weigh(0, split_heads(qkv[pack, rws, pl.ds(0, 128)], low), offset)
+                ctx_order[rws, pl.ds(0, 128)] = jnp.where(low, out[:UNIT], out[UNIT:]).astype(BF16)
+
+            def single(index, side=side, pack=pack):
+                rws = pl.ds(pl.multiple_of(side * group + index * 2 * UNIT, 2 * UNIT), 2 * UNIT)
+                offset = bias[2, tile(index, 2 * UNIT), :]
+                if side:
+                    offset = jnp.concatenate(
+                        [
+                            offset[half * UNIT : (half + 1) * UNIT] + mask_row(runs, 2 * index + half)
+                            for half in range(2)
+                        ],
+                        axis=0,
                     )
-                outs = []
-                for head in range(3):
-                    block = pl.ds(0 if head < 2 else 128, 128)
-                    queries = qkv[pack, rws, block]
-                    if head < 2:
-                        queries = jnp.where(low if head == 0 else ~low, queries, jnp.zeros_like(queries))
-                    k_block = pl.ds(lanes + (0 if head < 2 else 128), 128)
-                    v_block = pl.ds(2 * lanes + (0 if head < 2 else 128), 128)
-                    scores = dot_nt(queries, qkv[pack, keys, k_block]) * HD ** (-0.5)
-                    scores = scores + bias[head, tile(index, UNIT), :]
-                    if side:
-                        scores = scores + mask
-                    powers = jnp.exp(scores - jnp.max(scores, axis=-1, keepdims=True))
-                    total = jnp.sum(powers, axis=-1, keepdims=True)
-                    outs.append(dot_nn(powers.astype(BF16), qkv[pack, keys, v_block]) / total)
-                ctx_order[rws, pl.ds(0, 128)] = jnp.where(low, outs[0], outs[1]).astype(BF16)
-                ctx_order[rws, pl.ds(128, 128)] = outs[2].astype(BF16)
-
-            loop(4, chunk)
+                out = weigh(1, qkv[pack, rws, pl.ds(128, 128)], offset)
+                ctx_order[rws, pl.ds(128, 128)] = out.astype(BF16)
+
+            loop(4, pair, unroll=PAIRS)
+            loop(2, single, unroll=SINGLES)
         runs.restore(ctx_order, writer(ctx, pack))
         for which in range(2):
             big = pl.ds(scatter.half(which), 2 * share)
@@ -703,49 +747,62 @@
     for pack in range(packs):
         gather.drain(pack)
         scatter.drain(pack)
+    if gathering:
+        owners.drain()
 
 
 def back_kernel(
+    summing,
     offsets_ref,
     slopes_ref,
     dr1_ref,
-    w_ref,
+    w_qkv_ref,
+    w_out_ref,
     x_ref,
     qkv_ref,
     ctx_ref,
-    grad_ref,
-    grads_ref,
-    packed,
-    w_qkv,
-    w_out,
-    bias,
-    held,
-    x_all,
-    qkv,
-    ctx,
-    plain,
-    dctx,
-    dorder,
-    dplain,
-    sum_k,
-    sum_v,
-    turned,
-    total,
-    total_out,
-    send_a,
-    recv_a,
-    send_b,
-    recv_b,
-    load_sem,
-    fetch_sem,
-    *buffers,
+    *rest,
 ):
+    padded_ref, rest = (rest[0], rest[1:]) if summing else (None, rest)
+    grad_ref, grads_ref, *rest = rest
+    owned_ref, rest = (rest[0], rest[1:]) if summing else (None, rest)
+    (
+        w_qkv,
+        w_out,
+        bias,
+        held,
+        x_all,
+        qkv,
+        ctx,
+        plain,
+        dctx,
+        dorder,
+        dplain,
+        sum_k,
+        sum_v,
+        turned,
+        total,
+        total_out,
+        send_a,
+        recv_a,
+        send_b,
+        recv_b,
+        load_sem,
+        fetch_sem,
+        *buffers,
+    ) = rest
+    if summing:
+        owners = OwnerSum(padded_ref, *buffers[6:], owned_ref.shape[1] // OWNER_CHUNKS)
     packs, share, width = dr1_ref.shape
     rows = 4 * share
     lanes = w_out.shape[1]
     group = rows // 2
-    load = pltpu.make_async_copy(w_ref.at[:, pl.ds(0, packed.shape[1])], packed, load_sem)
-    load.start()
+    loads = [
+        pltpu.make_async_copy(source, target, load_sem.at[place])
+        for place, (source, target) in enumerate(((w_qkv_ref, w_qkv), (w_out_ref, w_out)))
+    ]
+    for copy in loads:
+        copy.start()
     fetches = []
     for pack in range(packs):
         for place, (source, target) in enumerate(((x_ref, x_all), (qkv_ref, qkv), (ctx_ref, ctx))):
@@ -753,16 +810,21 @@
             copy.start()
             fetches.append(copy)
     wide, core, row, mate, across = places()
-    greet(mate, across)
+    if summing:
+        greet_all((("seq", 2 * owners.line), ("wide", 4)))
+    else:
+        greet(mate, across)
     gather = Gather(held, send_a, recv_a, share)
-    scatter = Scatter(*buffers, send_b, recv_b, share)
+    scatter = Scatter(*buffers[:6], send_b, recv_b, share)
     base = pl.multiple_of((core * 2 + row) * share, share)
     for pack in range(packs):
         held[pack, pl.ds(base, share), :] = dr1_ref[pack].astype(BF16)
         gather.start(pack)
+    if summing:
+        owners.start()
     fill_bias(bias, slopes_ref, wide)
-    load.wait()
-    split_weights(packed, w_qkv, w_out)
+    for copy in loads:
+        copy.wait()
     low = head_lanes()
     scale = HD ** (-0.5)
 
@@ -783,40 +845,58 @@
             sum_k[...] = jnp.zeros_like(sum_k)
             sum_v[...] = jnp.zeros_like(sum_v)
 
-            def chunk(index, side=side, keys=keys, pack=pack):
+            def masked(offset, index):
+                return jnp.concatenate(
+                    [offset[t * UNIT : (t + 1) * UNIT] + value for t, value in enumerate(runs.masks(index))],
+                    axis=0,
+                )
+
+            def pull_back(part, queries, dout, offset, keys=keys, pack=pack):
+                block = pl.ds(part * 128, 128)
+                k_all = qkv[pack, keys, pl.ds(lanes + part * 128, 128)]
+                v_all = qkv[pack, keys, pl.ds(2 * lanes + part * 128, 128)]
+                scores = dot_nt(k_all, queries) + offset
+                powers = jnp.exp(scores - jnp.max(scores, axis=0, keepdims=True))
+                probs = powers * (1.0 / jnp.sum(powers, axis=0, keepdims=True))
+                dprobs = dot_nt(v_all, dout)
+                delta = jnp.sum(probs * dprobs, axis=0, keepdims=True)
+                dscores = (probs * (dprobs - delta)).astype(BF16)
+                sum_v[:, block] += dot_nn(probs.astype(BF16), dout)
+                sum_k[:, block] += dot_nn(dscores, queries)
+                return dot_tn(dscores, k_all) * scale
+
+            def pair(index, side=side, pack=pack):
                 rws = pl.ds(pl.multiple_of(side * group + index * UNIT, UNIT), UNIT)
-                masks = runs.masks(index)
-                for part in range(2):
-                    heads = (0, 1) if part == 0 else (2,)
-                    block = pl.ds(part * 128, 128)
-                    k_block = pl.ds(lanes + part * 128, 128)
-                    v_block = pl.ds(2 * lanes + part * 128, 128)
-                    k_all, v_all = qkv[pack, keys, k_block], qkv[pack, keys, v_block]
-                    dq = None
-                    for head in heads:
-                        queries, dout, k_own = qkv[pack, rws, block], dctx[rws, block], k_all
-                        if part == 0:
-                            keep = low if head == 0 else ~low
-                            queries = jnp.where(keep, queries, jnp.zeros_like(queries))
-                            dout = jnp.where(keep, dout, jnp.zeros_like(dout))
-                            k_own = jnp.where(keep, k_own, jnp.zeros_like(k_own))
-                        scores = dot_nt(k_all, queries) * scale + bias[head, :, tile(index, UNIT)]
-                        if side:
-                            scores = jnp.concatenate(
-                                [scores[t * UNIT : (t + 1) * UNIT] + masks[t] for t in range(4)], axis=0
-                            )
-                        powers = jnp.exp(scores - jnp.max(scores, axis=0, keepdims=True))
-                        probs = powers * (1.0 / jnp.sum(powers, axis=0, keepdims=True))
-                        dprobs = dot_nt(v_all, dout)
-                        delta = jnp.sum(probs * dprobs, axis=0, keepdims=True)
-                        dscaled = (probs * (dprobs - delta) * scale).astype(BF16)
-                        sum_v[:, block] += dot_nn(probs.astype(BF16), dout)
-                        sum_k[:, block] += dot_nn(dscaled, queries)
-                        term = dot_tn(dscaled, k_own)
-                        dq = term if dq is None else dq + term
-                    dorder[rws, block] = dq.astype(BF16)
-
-            loop(4, chunk)
+                block = pl.ds(0, 128)
+                offsets = [bias[head, :, tile(index, UNIT)] for head in range(2)]
+                if side:
+                    offsets = [masked(offset, index) for offset in offsets]
+                dq = pull_back(
+                    0,
+                    split_heads(qkv[pack, rws, block], low),
+                    split_heads(dctx[rws, block], low),
+                    jnp.concatenate(offsets, axis=1),
+                )
+                dorder[rws, block] = jnp.where(low, dq[:UNIT], dq[UNIT:]).astype(BF16)
+
+            def single(index, side=side, pack=pack):
+                rws = pl.ds(pl.multiple_of(side * group + index * 2 * UNIT, 2 * UNIT), 2 * UNIT)
+                block = pl.ds(128, 128)
+                offset = bias[2, :, tile(index, 2 * UNIT)]
+                if side:
+                    offset = jnp.concatenate(
+                        [
+                            masked(offset[:, half * UNIT : (half + 1) * UNIT], 2 * index + half)
+                            for half in range(2)
+                        ],
+                        axis=1,
+                    )
+                dorder[rws, block] = pull_back(1, qkv[pack, rws, block], dctx[rws, block], offset).astype(BF16)
+
+            loop(4, pair, unroll=PAIRS)
+            loop(2, single, unroll=SINGLES)
+            if summing:
+                owners.add(2 * pack + side)
             dorder[keys, pl.ds(lanes, lanes)] = sum_k[...].astype(BF16)
             dorder[keys, pl.ds(2 * lanes, lanes)] = sum_v[...].astype(BF16)
         runs.restore(dorder, writer(dplain))
@@ -880,12 +960,20 @@
 
     loop(width // 128, pack_up)
     settle(packs - 1)
+
+    def put(rws, cols, value):
+        owned_ref[rws, cols] = value.astype(BF16)
+
+    if summing:
+        for index in range(OWNER_CHUNKS):
+            owners.finish(index, put)
+        owners.drain()
     for pack in range(packs):
         gather.drain(pack)
         scatter.drain(pack)
 
 
-def attn_call(x, weights, offsets, slopes):
+def attn_call(x, weights, slots, offsets, slopes, seq_count):
     packs, share, width = x.shape
     rows = 4 * share
     lanes = 256
@@ -893,16 +981,27 @@
     hb = pl.BlockSpec(memory_space=pl.ANY)
     sm = pl.BlockSpec(memory_space=pltpu.SMEM)
     dma = pltpu.SemaphoreType.DMA
+    more = []
+    if seq_count:
+        parts, slab = 2, weights.shape[0]
+        more = [
+            pltpu.VMEM((seq_count * slab, width), BF16),
+            pltpu.VMEM((slab, width), F32),
+            dma((2, seq_count // 2, parts)),
+            dma((2, seq_count // 2, parts)),
+        ]
     return pl.pallas_call(
-        attn_kernel,
+        functools.partial(attn_kernel, bool(seq_count)),
         out_shape=(
             jax.ShapeDtypeStruct((packs, share, width), F32),
             jax.ShapeDtypeStruct((packs, rows, width), BF16),
             jax.ShapeDtypeStruct((packs, rows, 3 * lanes), BF16),
             jax.ShapeDtypeStruct((packs, rows, lanes), BF16),
+            jax.ShapeDtypeStruct((width, 3 * lanes), BF16),
+            jax.ShapeDtypeStruct((width, lanes), BF16),
         ),
-        in_specs=[sm, sm, vm, hb],
-        out_specs=(vm, hb, hb, hb),
+        in_specs=[sm, sm, sm, vm, hb],
+        out_specs=(vm, hb, hb, hb, hb, hb),
         scratch_shapes=[
             pltpu.VMEM((width, width), BF16),
             pltpu.VMEM((width, 3 * lanes), BF16),
@@ -918,7 +1017,8 @@
             dma((packs, 2)),
             dma((packs, 2)),
             dma(()),
-            dma((packs, 3)),
+            dma((packs + 1, 3)),
+            *more,
             *scatter_scratch(packs, share, width),
         ],
         compiler_params=pltpu.CompilerParams(
@@ -926,27 +1026,34 @@
         ),
         cost_estimate=pl.CostEstimate(flops=int(14e9), bytes_accessed=4 * 10**7, transcendentals=10**7),
         name="attn",
-    )(offsets, slopes, x, weights)
-
-
-def back_call(dr1, weights, x_all, qkv, ctx, offsets, slopes):
+    )(offsets, slopes, slots, x, weights)
+
+
+def back_call(dr1, w_qkv, w_out, x_all, qkv, ctx, padded, offsets, slopes, seq_count):
     packs, share, width = dr1.shape
     rows = 4 * share
     lanes = 256
+    summing = padded is not None
+    more_in, more_out, more_scratch = [], [], []
+    if summing:
+        slab, cols, line = padded.shape[0] // seq_count, padded.shape[1], seq_count // 2
+        more_in = [padded.reshape(line, 2, slab, cols)]
+        more_out = [jax.ShapeDtypeStruct((slab, cols), BF16)]
+        more_scratch = owner_scratch(line, slab, cols, cols // OWNER_CHUNKS)
     vm = pl.BlockSpec(memory_space=pltpu.VMEM)
     hb = pl.BlockSpec(memory_space=pl.ANY)
     sm = pl.BlockSpec(memory_space=pltpu.SMEM)
     dma = pltpu.SemaphoreType.DMA
     return pl.pallas_call(
-        back_kernel,
+        functools.partial(back_kernel, summing),
         out_shape=(
             jax.ShapeDtypeStruct((packs, share, width), F32),
             jax.ShapeDtypeStruct((width, width), BF16),
+            *more_out,
         ),
-        in_specs=[sm, sm, vm, hb, hb, hb, hb],
-        out_specs=(vm, vm),
+        in_specs=[sm, sm, vm, hb, hb, hb, hb, hb] + [hb] * len(more_in),
+        out_specs=(vm, vm, *[vm] * len(more_out)),
         scratch_shapes=[
-            pltpu.VMEM((width, width), BF16),
             pltpu.VMEM((width, 3 * lanes), BF16),
             pltpu.VMEM((width, lanes), BF16),
             pltpu.VMEM((3, rows // 2, rows // 2), F32),
@@ -967,16 +1074,95 @@
             dma((packs, 3)),
             dma((packs, 2)),
             dma((packs, 2)),
-            dma(()),
+            dma((2,)),
             dma((packs, 3)),
             *scatter_scratch(packs, share, width),
+            *more_scratch,
         ],
         compiler_params=pltpu.CompilerParams(
             collective_id=3, has_side_effects=True, vmem_limit_bytes=VMEM_LIMIT
         ),
         cost_estimate=pl.CostEstimate(flops=int(40e9), bytes_accessed=4 * 10**7, transcendentals=10**7),
         name="back",
-    )(offsets, slopes, dr1, weights, x_all, qkv, ctx)
+    )(offsets, slopes, dr1, w_qkv, w_out, x_all, qkv, ctx, *more_in)
+
+
+class OwnerGather:
+    def __init__(self, held, send, recv, slab, parts):
+        self.held, self.send, self.recv, self.slab, self.parts = held, send, recv, slab, parts
+        seq = lax.axis_index("seq")
+        self.line = held.shape[0] // slab // 2
+        self.x = lax.rem(seq, 2)
+        self.z = seq // 2
+
+    def block(self, owner, part):
+        size = self.held.shape[1] // self.parts
+        rows = pl.ds(pl.multiple_of(owner * self.slab, self.slab), self.slab)
+        return self.held.at[rows, pl.ds(part * size, size)]
+
+    def mine(self):
+        return pl.ds(pl.multiple_of((2 * self.z + self.x) * self.slab, self.slab), self.slab)
+
+    def source(self, step):
+        return lax.rem(self.z + self.line - step, self.line)
+
+    def hop(self, step, part):
+        block = self.block(2 * self.z + self.x, part)
+        peer = 2 * lax.rem(self.z + step, self.line) + self.x
+        return remote(block, block, self.send.at[0, step, part], self.recv.at[0, step, part], peer, "seq")
+
+    def landed(self, step, part):
+        block = self.block(2 * self.source(step) + self.x, part)
+        peer = 2 * self.z + 1 - self.x
+        return remote(block, block, self.send.at[0, step, part], self.recv.at[0, step, part], peer, "seq")
+
+    def cross(self, step, part, x):
+        block = self.block(2 * self.source(step) + x, part)
+        peer = 2 * self.z + 1 - self.x
+        return remote(block, block, self.send.at[1, step, part], self.recv.at[1, step, part], peer, "seq")
+
+    def start(self):
+        for part in range(self.parts):
+            self.cross(0, part, self.x).start()
+        for step in range(1, self.line):
+            for part in range(self.parts):
+                self.hop(step, part).start()
+
+    def pass_on(self):
+        for step in range(1, self.line):
+            for part in range(self.parts):
+                self.landed(step, part).wait_recv()
+                self.cross(step, part, self.x).start()
+
+    def finish(self):
+        for step in range(self.line):
+            for part in range(self.parts):
+                self.cross(step, part, 1 - self.x).wait_recv()
+
+    def drain(self):
+        for step in range(self.line):
+            for part in range(self.parts):
+                self.cross(step, part, self.x).wait_send()
+                if step:
+                    self.hop(step, part).wait_send()
+
+
+def order_slabs(slots, slabs, packed, owners):
+    blocks, rows, slab = slots.shape[0], packed.shape[0], slabs.shape[0] // owners
+    block, step = rows // blocks, 8
+    for first in range(0, blocks, step):
+        last = first + step - 1
+        low = first // CAP
+        high = max(o for o in range(owners) if max(o, blocks - CAP * (owners - o)) <= last)
+        count = (high - low + 1) * slab
+        lines = []
+        for place in range(first, first + step):
+            down = lax.broadcasted_iota(jnp.int32, (block, count), 0)
+            along = lax.broadcasted_iota(jnp.int32, (block, count), 1)
+            hit = along - down == slots[place] * block - low * slab
+            lines.append(jnp.where(hit, 1.0, 0.0).astype(BF16))
+        value = dot_nn(jnp.concatenate(lines, axis=0), slabs[pl.ds(low * slab, count), :])
+        packed[pl.ds(first * block, step * block), :] = value.astype(BF16)
 
 
 class OwnerSum:
@@ -1292,7 +1478,6 @@
     block = slab_rows // CAP
     source, valid, target = owner_maps(owner_blocks, width, CAP, block)
     low = master.astype(jnp.bfloat16)
-    first = lax.all_gather(low[:, :width], "seq", axis=0, tiled=True)
     rest = lax.all_gather(low[:, width:], "seq", axis=0, tiled=True)
     gathered_rows = slab_rows * lax.axis_size("seq")
     count = width // block
@@ -1310,31 +1495,39 @@
             return move_blocks(spread_kernel, grads, both, gathered_rows, block)
         return jnp.take(grads, source, axis=0)
 
-    weights = to_order(first)
+    seq_count = lax.axis_size("seq")
+    own_kernels = fits and seq_count == 8
+    if own_kernels:
+        weights = master
+    else:
+        weights = to_order(lax.all_gather(low[:, :width], "seq", axis=0, tiled=True))
     w_ffn = to_order(rest)
     slopes = jnp.exp2(-8.0 * (jnp.arange(H, dtype=jnp.float32) + 1.0) / H)
     x = jnp.transpose(hidden_in, (1, 0, 2))
-    r1, x_all, qkv, ctx = attn_call(x, weights, seq_offsets, slopes)
+    r1, x_all, qkv, ctx, w_qkv, w_out = attn_call(
+        x, weights, slots, seq_offsets, slopes, seq_count if own_kernels else 0
+    )
     mixed_p, dr1_p, ffn_grads, ln_rows = ffn_call(
         r1, jnp.transpose(cotangent, (1, 0, 2)), w_ffn, ln_params
     )
     mixed = jnp.transpose(mixed_p, (1, 0, 2))
 
-    ffn_padded, dr1_p = lax.optimization_barrier((to_owner(ffn_grads), dr1_p))
-    ffn_owned = lax.psum_scatter(ffn_padded, "seq", scatter_dimension=0, tiled=True)
-    grad_p, attn_grads = back_call(dr1_p, weights, x_all, qkv, ctx, seq_offsets, slopes)
+    ffn_padded = to_owner(ffn_grads)
+    grad_p, attn_grads, *more = back_call(
+        dr1_p, w_qkv, w_out, x_all, qkv, ctx, ffn_padded if own_kernels else None, seq_offsets, slopes, seq_count
+    )
     input_grad = jnp.transpose(grad_p, (1, 0, 2))
     attn_padded = to_owner(attn_grads)
-    seq_count = lax.axis_size("seq")
     mine = jnp.arange(seq_count, dtype=jnp.int32) == lax.axis_index("seq")
     own_rows = jnp.sum(jnp.where(mine, owner_blocks, 0)) * block
     kept = (jnp.arange(slab_rows, dtype=jnp.int32) < own_rows)[:, None]
-    if fits and seq_count == 8:
+    if own_kernels:
         owned, ln_total, parts = close_call(
-            own_rows[None], attn_padded, ffn_owned, ln_rows, seq_count, lax.axis_size("wide")
+            own_rows[None], attn_padded, more[0], ln_rows, seq_count, lax.axis_size("wide")
         )
         squares, ln_total = jnp.sum(parts), ln_total[:4]
     else:
+        ffn_owned = lax.psum_scatter(ffn_padded, "seq", scatter_dimension=0, tiled=True)
         attn_owned = lax.psum_scatter(attn_padded, "seq", scatter_dimension=0, tiled=True)
         owned = jnp.concatenate([attn_owned, ffn_owned], axis=1).astype(jnp.float32)
         owned = jnp.where(kept, owned, 0.0)

time: 515 us -> 460 us (0.89)
  waiting for transfers between devices: 125 us -> 36 us
  Pallas kernels: 341 us -> 376 us
    all_gather x1 -> x0, waiting for transfers between devices: 52.4 us -> none  [per_device(): first = lax.all_gather(low[:, :width], 'seq', axis=0, tiled=True)]
    pallas_call x2, Pallas kernels: 157 us -> 195 us  [the longest x1 100 us: back_call(): pl.pallas_call(functools.partial(back_kernel, summing), out_shape=(jax.Sh...]
    reduce_scatter x1 -> x0, waiting for transfers between devices: 32.9 us -> none  [per_device(): lax.psum_scatter(ffn_padded, 'seq', scatter_dimension=0, tiled=True)]
    pallas_call x4 -> x3, Pallas kernels: 15.8 us -> 12.7 us  [move_blocks(): pl.pallas_call(functools.partial(kernel, block), out_shape=jax.ShapeDtype...]
  transfers between devices with their start and end apart: 3 -> 1, of which waited for: 3 -> 1; matrix products, arithmetic and copies ran while one was open for 1% -> 1% of each run, Pallas kernels for 32% -> 21%
where the time goes in v4:
time: 460 us; the launch traced here: 452 us
  Pallas kernels  376 us (82%)
  waiting for transfers between devices  36 us (8%)
  between operations  17.9 us (4%)
  other arithmetic  15.4 us (3%)
  local copies, waits for them, and re-layouts  6.11 us (1%)
    pallas_call x1, Pallas kernels, ffn_call(): pl.pallas_call(ffn_kernel, out_shape=(jax.ShapeDtypeStruct((packs, share,...  114 us
    pallas_call x1, Pallas kernels, back_call(): pl.pallas_call(functools.partial(back_kernel, summing), out_shape=(jax.Sh...  100 us
    pallas_call x1, Pallas kernels, attn_call(): pl.pallas_call(functools.partial(attn_kernel, bool(seq_count)), out_shape...  94.2 us
    pallas_call x1, Pallas kernels, close_call(): pl.pallas_call(functools.partial(close_kernel, seq_count, wide_count), ou...  54.7 us
    all_gather x1, waiting for transfers between devices, per_device(): rest = lax.all_gather(low[:, width:], 'seq', axis=0, tiled=True)  35.9 us
    pallas_call x3, Pallas kernels, move_blocks(): pl.pallas_call(functools.partial(kernel, block), out_shape=jax.ShapeDtype...  12.7 us
  transfers between devices with their start and end apart: 1, of which 1 were waited for; matrix products, arithmetic and copies ran while one was open for 1% of the time, Pallas kernels for 21%

profile of v4, /device:TPU:0, one launch (start us, length us, event | category | flops | bytes accessed | tf_op | source)
XLA Modules:
  0.0 451.7 jit_solution(2848032791899887809)
XLA Ops:
  7.2 0.0 copy-start.6
  7.2 0.0 all-gather.2.cloned.1.call-start
  7.2 2.5 slice.17
  9.7 0.0 all-gather.2.cloned.1.call-update
  9.7 0.0 copy-done.6
  9.8 0.2 reduce-window.8
  9.9 0.1 convert_reduce_fusion
  10.0 0.6 fusion.10
  10.7 0.1 select_reduce_fusion
  10.8 0.1 slice.9
  11.5 0.5 multiply_exponential_fusion.slopes_ref
  12.1 0.6 pad_add_fusion.places_ref
  12.6 0.5 and_select_fusion.slots_ref
  13.2 94.2 %attn.1 = (f32[3,256,768]{2,1,0:T(8,128)}, bf16[3,1024,768]{2,1,0:T(8,128)(2,1)}, bf16[3,1024,768]{2,1,0:T(8,128)(2,1)}, bf16[3,1024,256]{2,1,0:T(8,128)(2,1)}, ...) custom-call(s32[3,8]{1,0:T(4,128)} %offsets_ref.3, f32[12]{0:T(128)} %multiply_exponential_fusion.slopes_ref, ...), custom_call_target="tpu_custom_call" | custom-call | flops 14000000000 | bytes 40000000 | tf_op jit(solution)/shard_map/attn/pallas_call | solution.py:993
  107.3 35.9 %all-gather.2.cloned.1.call-done.source_ref = bf16[1536,2304]{1,0:T(8,128)(2,1)} async-done(((bf16[192,2304]{1,0:T(8,128)(2,1)}), bf16[1536,2304]{1,0:T(8,128)(2,1)}) %all-gather.2.cloned.1.call-update) | async-done | bytes 7077904 | tf_op jit(solution)/shard_map/all_gather | solution.py:1481
  143.3 4.8 %move.3.w_ref = bf16[768,2304]{1,0:T(8,128)(2,1)} custom-call(s32[2,24]{1,0:T(2,128)} %pad_add_fusion.places_ref, bf16[1536,2304]{1,0:T(8,128)(2,1)} %all-gather.2.cloned.1.call-done.source_ref), custom_call_target="tpu_custom_call" | custom-call | tf_op jit(solution)/shard_map/move/pallas_call | solution.py:1449
  148.1 114.4 %ffn.1 = (bf16[3,256,768]{2,1,0:T(8,128)(2,1)}, f32[3,256,768]{2,1,0:T(8,128)}, bf16[768,2304]{1,0:T(8,128)(2,1)}, f32[8,768]{1,0:T(8,128)}) custom-call(f32[3,256,768]{2,1,0:T(8,128)} %get-tuple-element.25.r1_ref, bf16[3,256,768]{2,1,0:T(8,128)(2,1)} %bitcast.19, bf16[768,2304]{1,0:T(8,128)(2,1)} %move.3.w_ref, f32[4,768]{1,0:T(4,128)} %ln_ref.1), custom_call_target="tpu_custom_call" | custom-call | flops 70000001024 | bytes 40000000 | tf_op jit(solution)/shard_map/ffn/pallas_call | solution.py:455
  262.5 4.7 %move.4 = bf16[1536,2304]{1,0:T(8,128)(2,1)} custom-call(s32[2,24]{1,0:T(2,128)} %pad_add_fusion.places_ref, bf16[768,2304]{1,0:T(8,128)(2,1)} %get-tuple-element.33.source_ref), custom_call_target="tpu_custom_call" | custom-call | tf_op jit(solution)/shard_map/move/pallas_call | solution.py:1449
  267.2 100.4 %back.1 = (f32[3,256,768]{2,1,0:T(8,128)}, bf16[768,768]{1,0:T(8,128)(2,1)}, bf16[192,2304]{1,0:T(8,128)(2,1)}) custom-call(s32[3,8]{1,0:T(4,128)} %offsets_ref.3, f32[12]{0:T(128)} %multiply_exponential_fusion.slopes_ref, f32[3,256,768]{2,1,0:T(8,128)} %get-tuple-element.27.dr1_ref, bf16[768,768]{1,0:T(8,128)(2,1)} %get-tuple-element.28.w_qkv_ref, ...), custom_call_target="tpu_custom_call" | custom-call | flops 40000000000 | bytes 40000000 | tf_op jit(solution)/shard_map/back/pallas_call | solution.py:1047
  367.5 3.2 move.5
  370.7 0.0 copy-start.3
  370.7 0.0 copy-start.4
  370.7 0.0 copy-start.5
  370.8 0.0 copy-start
  370.8 54.7 %close.1 = (f32[192,3072]{1,0:T(8,128)}, f32[8,768]{1,0:T(8,128)}, f32[8,128]{1,0:T(8,128)}) custom-call(s32[1]{0:T(128)} %bitcast.8.kept_ref, bf16[4,2,192,768]{3,2,1,0:T(8,128)(2,1)} %bitcast.12, bf16[192,2304]{1,0:T(8,128)(2,1)} %get-tuple-element.36.ffn_ref, f32[8,768]{1,0:T(8,128)} %get-tuple-element.37.ln_ref), custom_call_target="tpu_custom_call" | custom-call | tf_op jit(solution)/shard_map/close/pallas_call | solution.py:1388
  425.5 1.4 multiply_reduce_fusion
  426.8 1.3 reduce_sum.48
  429.5 0.0 copy-done.3
  429.5 0.0 copy-done.4
  429.5 0.0 copy-done.5
  429.5 1.4 multiply_subtract_fusion
  430.9 0.0 copy-done
  430.9 0.0 copy-start.2
  430.9 8.8 %broadcast_select_fusion = (f32[192,3072]{1,0:T(8,128)}, f32[192,3072]{1,0:T(8,128)}, f32[192,3072]{1,0:T(8,128)}) fusion(pred[192]{0:T(512)(128)(4,1)S(1)} %iota_compare_fusion.1, f32[192,3072]{1,0:T(8,128)} %get-tuple-element.38, f32[]{:T(128)S(6)} %min.3, f32[192,3072]{1,0:T(8,128)} %param.16, f32[192,3072]{1,0:T(8,128)S(1)} %copy-done, f32[192,3072]{1,0:T(8,128)} %param.15), kind=kLoop, calls=%fused_computation.5 | loop fusion | flops 11206656 | bytes 16515268 | tf_op jit(solution)/shard_map/jit(_where)/select_n | solution.py:1548
  439.7 0.0 copy-start.1
  439.7 0.0 copy-done.2
  439.7 1.0 copy.21
  440.7 1.1 copy-done.1
  441.8 1.4 copy.22
  (4 shorter events, 0.0 us)
Async XLA Ops:
  7.2 2.6 copy-start.6
  7.2 136.1 %all-gather.2.cloned.1.call-start = ((), (), s32[]{:S(2)}) async-start(), calls=%async_computation | async-start | bytes 7962624 | tf_op jit(solution)/shard_map/all_gather | solution.py:1481
  370.7 58.8 %copy-start.3 = (f32[4,768]{1,0:T(4,128)S(1)}, f32[4,768]{1,0:T(4,128)}, u32[]{:S(2)}) copy-start(f32[4,768]{1,0:T(4,128)} %ln_ref.1) | copy-start | bytes 36868
  370.7 58.8 %copy-start.4 = (f32[4,768]{1,0:T(4,128)S(1)}, f32[4,768]{1,0:T(4,128)}, u32[]{:S(2)}) copy-start(f32[4,768]{1,0:T(4,128)} %param.18) | copy-start | bytes 36868
  370.7 58.8 %copy-start.5 = (f32[4,768]{1,0:T(4,128)S(1)}, f32[4,768]{1,0:T(4,128)}, u32[]{:S(2)}) copy-start(f32[4,768]{1,0:T(4,128)} %param.19) | copy-start | bytes 36868
  370.8 60.1 %copy-start = (f32[192,3072]{1,0:T(8,128)S(1)}, f32[192,3072]{1,0:T(8,128)}, u32[]{:S(2)}) copy-start(f32[192,3072]{1,0:T(8,128)} %w_ref.1) | copy-start | bytes 7077892
  430.9 8.8 %copy-start.2 = (bf16[3,256,768]{2,1,0:T(8,128)(2,1)S(1)}, bf16[3,256,768]{2,1,0:T(8,128)(2,1)}, u32[]{:S(2)}) copy-start(bf16[3,256,768]{2,1,0:T(8,128)(2,1)} %get-tuple-element.26) | copy-start | bytes 3538948
  439.7 2.1 copy-start.1
Sparse Core Ops, SparseCore 0:
  10.8 132.4 all-gather.1
